TPU v7x, 512 devices: a whole 4x8x8 slice. The times are simulated.
512 devices in a mesh: dp: 16 (over z_hi, x), fsdp: 32 (over y, z_lo, core).
Axes of the slice: x: 4, y: 8, z: 8 (z_hi: 4, z_lo: 2; z = z_hi * 2 + z_lo), core: 2. Of those that a mesh axis runs over, the one named last changes fastest.
Arguments:
- tokens: bfloat16 [32768, 8192], P('fsdp', 'dp'), may hold values from -6 to 6
- tangent: bfloat16 [32768, 16384], P('fsdp', 'dp'), may hold values from -0.15625 to 0.15625
- projector: bfloat16 [8192, 512], P('dp'), may hold values from -0.0625 to 0.0625
- first_moment: float32 [16384, 512], P(('dp', 'fsdp')), may hold values from -6 to 6
- second_moment: float32 [16384, 512], P(('dp', 'fsdp')), may hold values from 0.3 to 3
Outputs:
- update: bfloat16 [16384, 8192], P(('dp', 'fsdp'))
- new_first: float32 [16384, 512], P(('dp', 'fsdp'))
- new_second: float32 [16384, 512], P(('dp', 'fsdp'))
All inputs are finite; a program needn't handle non-finite values.
Results may differ from a plain program's by a relative error of at most 0.0049.
Values may be sent and summed in bfloat16 or wider, within the bound.
No kernel may reach another device: no remote copies, remote signals or barrier semaphores. Data moves between devices by JAX's collectives and lax.ppermute only.
A program may use at most 64 MiB of HBM per device.

v0:
```python
import jax
import jax.numpy as jnp
from jax import lax
from jax.sharding import PartitionSpec as P

STEP = 10


def local(tokens, tangent, projector, first_moment, second_moment):
    partial_proj = jnp.dot(tokens, projector, preferred_element_type=jnp.float32)
    reduced = lax.psum(partial_proj, "dp").astype(jnp.bfloat16)
    gradient = lax.psum_scatter(
        lax.dot_general(
            tangent, reduced, (((0,), (0,)), ((), ())), preferred_element_type=jnp.float32
        ),
        "fsdp",
        scatter_dimension=0,
        tiled=True,
    )
    new_first = 0.9 * first_moment + 0.1 * gradient
    new_second = 0.999 * second_moment + 0.001 * gradient * gradient
    first_fix = 1.0 - 0.9**STEP
    second_fix = 1.0 - 0.999**STEP
    direction = (new_first / first_fix / (jnp.sqrt(new_second / second_fix) + 1e-08)).astype(
        jnp.bfloat16
    )
    update = lax.dot_general(
        direction,
        lax.all_gather(projector, "dp", axis=0, tiled=True),
        (((1,), (1,)), ((), ())),
        preferred_element_type=jnp.float32,
    ).astype(jnp.bfloat16)
    return (update, new_first, new_second)


def solution(mesh):
    in_specs = (
        P("fsdp", "dp"),
        P("fsdp", "dp"),
        P("dp", None),
        P(("dp", "fsdp"), None),
        P(("dp", "fsdp"), None),
    )
    out_specs = (P(("dp", "fsdp"), None), P(("dp", "fsdp"), None), P(("dp", "fsdp"), None))
    return jax.shard_map(local, mesh=mesh, in_specs=in_specs, out_specs=out_specs, check_vma=False)
```

profile of v0, /device:TPU:1, one launch (start us, length us, event | category | flops | bytes accessed | tf_op | source)
XLA Modules:
  0.0 327.2 jit_solution(974361438431322836)
XLA Ops:
  8.0 0.0 copy-start
  8.0 0.0 reduce-scatter.4.cloned.1.call-start
  8.1 3.6 %fusion.8 = f32[1024,512]{1,0:T(8,128)} fusion(bf16[1024,512]{1,0:T(8,128)(2,1)} %param.5, bf16[512,512]{1,0:T(8,128)(2,1)} %param.7), kind=kOutput, calls=%fused_computation.13 | convolution fusion | flops 536870912 | bytes 3670016 | tf_op jit(solution)/shard_map/dot_general | solution.py:10
  11.6 114.0 %all-reduce.1 = bf16[1024,512]{1,0:T(8,128)(2,1)S(1)} all-reduce(f32[1024,512]{1,0:T(8,128)} %fusion.8), channel_id=1, replica_groups=mesh['dp'=16,'fsdp'=32] {'dp'}, use_global_device_ids=true, to_apply=%region_0.0 | all-reduce | flops 524288 | bytes 3145728 | tf_op jit(solution)/shard_map/psum | solution.py:11
  125.6 0.0 copy-done
  125.6 2.6 convolution_bitcast_fusion
  128.2 2.9 copy.19
  131.2 0.0 copy-start.3
  131.2 0.0 copy-start.4
  131.2 0.0 reduce-scatter.4.cloned.1.call-update
  131.2 0.0 all-gather.2.cloned.1.call-start
  131.2 0.5 all-gather.2.cloned.1.call-update
  131.8 180.4 %reduce-scatter.4.cloned.1.call-done = f32[32,512]{1,0:T(8,128)} async-done(((f32[1024,512]{1,0:T(8,128)}), f32[32,512]{1,0:T(8,128)}) %reduce-scatter.4.cloned.1.call-update) | async-done | bytes 65552 | tf_op jit(solution)/shard_map/reduce_scatter | solution.py:12
  312.1 0.0 copy-done.3
  312.1 0.0 copy-done.4
  312.1 0.9 multiply_add_fusion
  313.0 0.0 copy-start.1
  313.0 0.0 copy-start.2
  313.0 0.0 all-gather.2.cloned.1.call-done
  313.1 6.7 %convolution_convert_fusion = bf16[32,8192]{1,0:T(8,128)(2,1)} fusion(bf16[8192,512]{1,0:T(8,128)(2,1)} %all-gather.2.cloned.1.call-done, f32[32,512]{1,0:T(8,128)S(1)} %get-tuple-element.10, f32[32,512]{1,0:T(8,128)S(1)} %get-tuple-element.9), kind=kOutput, calls=%fused_computation | convolution fusion | flops 268779520 | bytes 9043968 | tf_op jit(solution)/shard_map/dot_general | solution.py:27
  319.8 0.0 copy-done.1
  319.8 0.0 copy-done.2
Async XLA Ops:
  8.0 117.6 %copy-start = (bf16[1024,1024]{1,0:T(8,128)(2,1)S(1)}, bf16[1024,1024]{1,0:T(8,128)(2,1)}, u32[]{:S(2)}) copy-start(bf16[1024,1024]{1,0:T(8,128)(2,1)} %param.6) | copy-start | bytes 6291460
  8.0 304.1 %reduce-scatter.4.cloned.1.call-start = ((), (), s32[]{:S(2)}) async-start(), calls=%async_computation.2 | async-start | bytes 2162688 | tf_op jit(solution)/shard_map/reduce_scatter | solution.py:12
  131.2 181.0 %copy-start.3 = (f32[32,512]{1,0:T(8,128)S(1)}, f32[32,512]{1,0:T(8,128)}, u32[]{:S(2)}) copy-start(f32[32,512]{1,0:T(8,128)} %param.8) | copy-start | bytes 196612
  131.2 181.0 %copy-start.4 = (f32[32,512]{1,0:T(8,128)S(1)}, f32[32,512]{1,0:T(8,128)}, u32[]{:S(2)}) copy-start(f32[32,512]{1,0:T(8,128)} %param.9) | copy-start | bytes 196612
  131.2 181.9 %all-gather.2.cloned.1.call-start = ((), (), s32[]{:S(2)}) async-start(), calls=%async_computation.1 | async-start | bytes 8912896 | tf_op jit(solution)/shard_map/all_gather | solution.py:29
  313.0 6.8 %copy-start.1 = (f32[32,512]{1,0:T(8,128)}, f32[32,512]{1,0:T(8,128)S(1)}, u32[]{:S(2)}) copy-start(f32[32,512]{1,0:T(8,128)S(1)} %get-tuple-element.9) | copy-start | bytes 196612
  313.0 6.8 %copy-start.2 = (f32[32,512]{1,0:T(8,128)}, f32[32,512]{1,0:T(8,128)S(1)}, u32[]{:S(2)}) copy-start(f32[32,512]{1,0:T(8,128)S(1)} %get-tuple-element.10) | copy-start | bytes 196612
Sparse Core Ops, SparseCore 0:
  131.3 180.7 reduce-scatter.3
Sparse Core Ops, SparseCore 1:
  134.7 132.6 all-gather.1
where the time goes:
time: 333 us; the launch traced here: 327 us
  waiting for transfers between devices  181 us (54%)
  blocking collectives  114 us (34%)
  between operations  15.5 us (5%)
  matrix products  12.9 us (4%)
    reduce_scatter x1, waiting for transfers between devices, local(): lax.psum_scatter(lax.dot_general(tangent, reduced, (((0,), (0,)), ((), ()...  180 us
    psum x1, blocking collectives, local(): reduced = lax.psum(partial_proj, 'dp').astype(jnp.bfloat16)  114 us
    dot_general x1, matrix products, local(): lax.dot_general(direction, lax.all_gather(projector, 'dp', axis=0, tiled=...  6.71 us
  transfers between devices with their start and end apart: 2, of which 1 were waited for; matrix products, arithmetic and copies ran while one was open for 0% of the time, Pallas kernels for 0%

commit v1 on v0

v1 whole, which is shorter than its diff:
```python
import jax
import jax.numpy as jnp
from jax import lax
from jax.sharding import Mesh, PartitionSpec as P

STEP = 10
F32 = jnp.float32
BF16 = jnp.bfloat16


def swap(parts, axis):
    return lax.all_to_all(parts, axis, 0, 0)


def add(parts):
    return jnp.sum(parts.astype(F32), axis=0)


def spread(block, axis, n):
    return swap(jnp.broadcast_to(block[None], (n,) + block.shape), axis)


def local(tokens, tangent, projector, first_moment, second_moment):
    r = projector.shape[1]
    wide = lax.all_gather(projector, "zh", axis=0, tiled=True)
    part = jnp.dot(tokens, projector, preferred_element_type=F32).astype(BF16)
    part = add(swap(part.reshape(4, -1, r), "x")).astype(BF16)
    part = add(swap(part.reshape(4, -1, r), "zh")).astype(BF16)
    reduced = spread(part, "zh", 4).reshape(-1, r)
    reduced = spread(reduced, "x", 4).reshape(-1, r)
    grad = lax.dot_general(
        tangent, reduced, (((0,), (0,)), ((), ())), preferred_element_type=F32
    ).astype(BF16)
    grad = grad.reshape(8, 2, 2, -1, r).transpose(2, 1, 0, 3, 4)
    grad = add(swap(grad, "c")).astype(BF16)
    grad = add(swap(grad, "zl")).astype(BF16)
    gradient = add(swap(grad, "y"))

    new_first = 0.9 * first_moment + 0.1 * gradient
    new_second = 0.999 * second_moment + 0.001 * gradient * gradient
    first_fix = 1.0 - 0.9**STEP
    second_fix = 1.0 - 0.999**STEP
    direction = (new_first / first_fix / (jnp.sqrt(new_second / second_fix) + 1e-08)).astype(BF16)
    rows = direction.shape[0]
    directions = spread(direction, "x", 4).reshape(-1, r)
    out = lax.dot_general(
        directions, wide, (((1,), (1,)), ((), ())), preferred_element_type=F32
    ).astype(BF16)
    out = swap(out.reshape(4, rows, -1), "x")
    out = out.reshape(4, rows, 4, -1).transpose(1, 2, 0, 3).reshape(rows, -1)
    return (out, new_first, new_second)


def solution(mesh):
    fine = Mesh(mesh.devices.reshape(4, 4, 8, 2, 2), ("zh", "x", "y", "zl", "c"))
    dp, fsdp = ("zh", "x"), ("y", "zl", "c")
    rows = P(dp + fsdp, None)
    return jax.shard_map(
        local,
        mesh=fine,
        in_specs=(P(fsdp, dp), P(fsdp, dp), P(dp, None), rows, rows),
        out_specs=(rows, rows, rows),
        check_vma=False,
    )
```

time: 333 us -> 153 us (0.46)
  waiting for transfers between devices: 181 us -> 13.6 us
  blocking collectives: 114 us -> 89.2 us
  starting transfers between devices: 0.08 us -> 18.2 us
  matrix products: 12.9 us -> 6.9 us
    reduce_scatter x1 -> x0, waiting for transfers between devices: 180 us -> none  [local(): lax.psum_scatter(lax.dot_general(tangent, reduced, (((0,), (0,)), ((), ()...]
    psum x1 -> x0, blocking collectives: 114 us -> none  [local(): reduced = lax.psum(partial_proj, 'dp').astype(jnp.bfloat16)]
    all_to_all x0 -> x7, blocking collectives: none -> 89.2 us  [swap(): return lax.all_to_all(parts, axis, 0, 0)]
    all_to_all x0 -> x2, starting transfers between devices: none -> 18.2 us  [swap(): return lax.all_to_all(parts, axis, 0, 0)]
    all_to_all x0 -> x2, waiting for transfers between devices: none -> 12.8 us  [swap(): return lax.all_to_all(parts, axis, 0, 0)]
    dot_general x2, matrix products: 10.3 us -> 4.61 us  [the longest x1 2.4 us: local(): lax.dot_general(directions, wide, (((1,), (1,)), ((), ())), preferred_ele...]
  transfers between devices with their start and end apart: 2 -> 3, of which waited for: 1 -> 2; matrix products, arithmetic and copies ran while one was open for 0% -> 5% of each run, Pallas kernels for 0% -> 0%
where the time goes in v1:
time: 153 us; the launch traced here: 150 us
  blocking collectives  89.2 us (58%)
  starting transfers between devices  18.2 us (12%)
  between operations  14.1 us (9%)
  waiting for transfers between devices  13.6 us (9%)
  matrix products  6.9 us (5%)
  local copies, waits for them, and re-layouts  5.44 us (4%)
  other arithmetic  2.89 us (2%)
    all_to_all x7, blocking collectives, swap(): return lax.all_to_all(parts, axis, 0, 0)  89.2 us
    all_to_all x2, starting transfers between devices, swap(): return lax.all_to_all(parts, axis, 0, 0)  18.2 us
    all_to_all x2, waiting for transfers between devices, swap(): return lax.all_to_all(parts, axis, 0, 0)  12.8 us
  transfers between devices with their start and end apart: 3, of which 2 were waited for; matrix products, arithmetic and copies ran while one was open for 5% of the time, Pallas kernels for 0%

profile of v1, /device:TPU:1, one launch (start us, length us, event | category | flops | bytes accessed | tf_op | source)
XLA Modules:
  0.0 150.2 jit_solution(16791375413371946013)
XLA Ops:
  7.2 2.2 %convolution_convert_fusion.2 = bf16[1024,512]{1,0:T(8,128)(2,1)S(1)} fusion(bf16[1024,512]{1,0:T(8,128)(2,1)} %param.5, bf16[512,512]{1,0:T(8,128)(2,1)} %param.7), kind=kOutput, calls=%fused_computation.2 | convolution fusion | flops 537395200 | bytes 2621440 | tf_op jit(solution)/shard_map/dot_general | solution.py:26
  9.4 15.1 %all_to_all.45 = bf16[4,256,512]{2,1,0:T(8,128)(2,1)S(1)} all-to-all(bf16[4,256,512]{2,1,0:T(8,128)(2,1)S(1)} %bitcast.25), channel_id=1, replica_groups=mesh['zh'=4,'x'=4,'y'=8,'zl'=2,'c'=2] {'x'}, dimensions={0} | all-to-all | bytes 2097152 | tf_op jit(solution)/shard_map/all_to_all | solution.py:12
  24.5 0.9 reduce_sum.57
  25.4 13.7 %all-to-all-start.1 = ((bf16[4,64,512]{2,1,0:T(8,128)(2,1)}), bf16[4,64,512]{2,1,0:T(8,128)(2,1)S(1)}, u32[]{:S(2)}, u32[]{:S(2)}) async-start(bf16[4,64,512]{2,1,0:T(8,128)(2,1)} %bitcast.1), calls=%async_computation.1 | async-start | bytes 524288 | tf_op jit(solution)/shard_map/all_to_all | solution.py:12
  39.1 0.7 all-gather.2.cloned.1.call-update
  39.9 8.0 %all-to-all-done.1 = bf16[4,64,512]{2,1,0:T(8,128)(2,1)S(1)} async-done(((bf16[4,64,512]{2,1,0:T(8,128)(2,1)}), bf16[4,64,512]{2,1,0:T(8,128)(2,1)S(1)}, u32[]{:S(2)}, u32[]{:S(2)}) %all-to-all-start.1) | async-done | bytes 262176 | tf_op jit(solution)/shard_map/all_to_all | solution.py:12
  47.9 11.5 %all_to_all.46 = bf16[4,64,512]{2,1,0:T(8,128)(2,1)S(1)} all-to-all(bf16[4,64,512]{2,1,0:T(8,128)(2,1)S(1)} %broadcast_in_dim.8), channel_id=1, replica_groups=mesh['zh'=4,'x'=4,'y'=8,'zl'=2,'c'=2] {'zh'}, dimensions={0} | all-to-all | bytes 524288 | tf_op jit(solution)/shard_map/all_to_all | solution.py:12
  59.5 13.1 %all_to_all.47 = bf16[4,256,512]{2,1,0:T(8,128)(2,1)S(1)} all-to-all(bf16[4,256,512]{2,1,0:T(8,128)(2,1)S(1)} %broadcast_in_dim.10), channel_id=1, replica_groups=mesh['zh'=4,'x'=4,'y'=8,'zl'=2,'c'=2] {'x'}, dimensions={0} | all-to-all | bytes 2097152 | tf_op jit(solution)/shard_map/all_to_all | solution.py:12
  72.6 2.3 %fusion = bf16[1024,512]{0,1:T(8,128)(2,1)} fusion(bf16[1024,512]{1,0:T(8,128)(2,1)S(1)} %bitcast.21, bf16[1024,1024]{1,0:T(8,128)(2,1)S(1)} %copy-done), kind=kOutput, calls=%fused_computation.3 | convolution fusion | flops 1074266112 | bytes 4194304 | tf_op jit(solution)/shard_map/dot_general | solution.py:31
  74.9 1.5 copy.20
  76.5 9.6 %all_to_all.48 = bf16[2,2,8,32,512]{4,3,1,2,0:T(8,128)(2,1)S(1)} all-to-all(bf16[2,2,8,32,512]{4,3,1,2,0:T(8,128)(2,1)S(1)} %copy.21), channel_id=1, replica_groups=mesh['zh'=4,'x'=4,'y'=8,'zl'=2,'c'=2] {'c'}, dimensions={0} | all-to-all | bytes 2097152 | tf_op jit(solution)/shard_map/all_to_all | solution.py:12
  86.1 1.1 reduce_sum.59
  87.2 1.1 copy.23
  88.3 14.0 %all_to_all.49 = bf16[2,8,32,512]{3,2,1,0:T(8,128)(2,1)S(1)} all-to-all(bf16[2,8,32,512]{3,2,1,0:T(8,128)(2,1)S(1)} %copy.23), channel_id=1, replica_groups=mesh['zh'=4,'x'=4,'y'=8,'zl'=2,'c'=2] {'zl'}, dimensions={0} | all-to-all | bytes 1048576 | tf_op jit(solution)/shard_map/all_to_all | solution.py:12
  102.5 16.5 %all_to_all.50 = bf16[8,32,512]{2,1,0:T(8,128)(2,1)S(1)} all-to-all(bf16[8,32,512]{2,1,0:T(8,128)(2,1)S(1)} %reduce_sum.60), channel_id=1, replica_groups=mesh['zh'=4,'x'=4,'y'=8,'zl'=2,'c'=2] {'y'}, dimensions={0} | all-to-all | bytes 524288 | tf_op jit(solution)/shard_map/all_to_all | solution.py:12
  119.0 0.7 divide_convert_fusion
  119.7 0.7 broadcast_in_dim.22
  120.4 4.4 %all-to-all-start.7 = ((bf16[4,32,512]{2,1,0:T(8,128)(2,1)}), bf16[4,32,512]{2,1,0:T(8,128)(2,1)S(1)}, u32[]{:S(2)}, u32[]{:S(2)}) async-start(bf16[4,32,512]{2,1,0:T(8,128)(2,1)} %broadcast_in_dim.22), calls=%async_computation.7 | async-start | bytes 262144 | tf_op jit(solution)/shard_map/all_to_all | solution.py:12
  124.8 4.8 %all-to-all-done.7 = bf16[4,32,512]{2,1,0:T(8,128)(2,1)S(1)} async-done(((bf16[4,32,512]{2,1,0:T(8,128)(2,1)}), bf16[4,32,512]{2,1,0:T(8,128)(2,1)S(1)}, u32[]{:S(2)}, u32[]{:S(2)}) %all-to-all-start.7) | async-done | bytes 131104 | tf_op jit(solution)/shard_map/all_to_all | solution.py:12
  129.7 2.4 %convolution_convert_fusion = bf16[128,2048]{1,0:T(8,128)(2,1)S(1)} fusion(bf16[128,512]{1,0:T(8,128)(2,1)S(1)} %bitcast.26, bf16[2048,512]{1,0:T(8,128)(2,1)} %all-gather.2.cloned.1.call-done), kind=kOutput, calls=%fused_computation | convolution fusion | flops 268697600 | bytes 2752512 | tf_op jit(solution)/shard_map/dot_general | solution.py:46
  132.1 9.3 %all_to_all.51 = bf16[4,32,2048]{2,1,0:T(8,128)(2,1)S(1)} all-to-all(bf16[4,32,2048]{2,1,0:T(8,128)(2,1)S(1)} %bitcast.23), channel_id=1, replica_groups=mesh['zh'=4,'x'=4,'y'=8,'zl'=2,'c'=2] {'x'}, dimensions={0} | all-to-all | bytes 1048576 | tf_op jit(solution)/shard_map/all_to_all | solution.py:12
  141.4 0.4 reshape.39
  141.8 0.4 copy.27
  142.2 1.2 reshape.40
  (14 shorter events, 0.4 us)
Async XLA Ops:
  7.2 65.4 %copy-start = (bf16[1024,1024]{1,0:T(8,128)(2,1)S(1)}, bf16[1024,1024]{1,0:T(8,128)(2,1)}, u32[]{:S(2)}) copy-start(bf16[1024,1024]{1,0:T(8,128)(2,1)} %param.6) | copy-start | bytes 6291460
  25.4 22.5 %all-to-all-start.1 = ((bf16[4,64,512]{2,1,0:T(8,128)(2,1)}), bf16[4,64,512]{2,1,0:T(8,128)(2,1)S(1)}, u32[]{:S(2)}, u32[]{:S(2)}) async-start(bf16[4,64,512]{2,1,0:T(8,128)(2,1)} %bitcast.1), calls=%async_computation.1 | async-start | bytes 524288 | tf_op jit(solution)/shard_map/all_to_all | solution.py:12
  39.1 85.7 %all-gather.2.cloned.1.call-start = ((), (), s32[]{:S(2)}) async-start(), calls=%async_computation.9 | async-start | bytes 2621440 | tf_op jit(solution)/shard_map/all_gather | solution.py:25
  87.2 31.8 %copy-start.1 = (f32[32,512]{1,0:T(8,128)S(1)}, f32[32,512]{1,0:T(8,128)}, u32[]{:S(2)}) copy-start(f32[32,512]{1,0:T(8,128)} %param.8) | copy-start | bytes 196612
  87.2 31.8 %copy-start.2 = (f32[32,512]{1,0:T(8,128)S(1)}, f32[32,512]{1,0:T(8,128)}, u32[]{:S(2)}) copy-start(f32[32,512]{1,0:T(8,128)} %param.9) | copy-start | bytes 196612
  120.4 9.3 %all-to-all-start.7 = ((bf16[4,32,512]{2,1,0:T(8,128)(2,1)}), bf16[4,32,512]{2,1,0:T(8,128)(2,1)S(1)}, u32[]{:S(2)}, u32[]{:S(2)}) async-start(bf16[4,32,512]{2,1,0:T(8,128)(2,1)} %broadcast_in_dim.22), calls=%async_computation.7 | async-start | bytes 262144 | tf_op jit(solution)/shard_map/all_to_all | solution.py:12
Sparse Core Ops, SparseCore 0:
  42.1 59.7 all-gather.1

commit v2 on v1

--- a/solution.py
+++ b/solution.py
@@ -13,7 +13,10 @@
 
 
 def add(parts):
-    return jnp.sum(parts.astype(F32), axis=0)
+    total = parts[0].astype(F32)
+    for i in range(1, parts.shape[0]):
+        total = total + parts[i].astype(F32)
+    return total
 
 
 def spread(block, axis, n):
@@ -22,7 +25,11 @@
 
 def local(tokens, tangent, projector, first_moment, second_moment):
     r = projector.shape[1]
-    wide = lax.all_gather(projector, "zh", axis=0, tiled=True)
+    core = lax.axis_index("c")
+    half = r // 2
+    mine = lax.all_gather(
+        lax.dynamic_slice_in_dim(projector, core * half, half, 1), ("zh", "x"), axis=0, tiled=True
+    )
     part = jnp.dot(tokens, projector, preferred_element_type=F32).astype(BF16)
     part = add(swap(part.reshape(4, -1, r), "x")).astype(BF16)
     part = add(swap(part.reshape(4, -1, r), "zh")).astype(BF16)
@@ -31,23 +38,32 @@
     grad = lax.dot_general(
         tangent, reduced, (((0,), (0,)), ((), ())), preferred_element_type=F32
     ).astype(BF16)
+    mine, grad = lax.optimization_barrier((mine, grad))
+    other = lax.ppermute(mine, "c", [(0, 1), (1, 0)])
     grad = grad.reshape(8, 2, 2, -1, r).transpose(2, 1, 0, 3, 4)
-    grad = add(swap(grad, "c")).astype(BF16)
-    grad = add(swap(grad, "zl")).astype(BF16)
-    gradient = add(swap(grad, "y"))
+    grad = add(swap(grad.reshape(2, -1, r), "c")).astype(BF16)
+    grad = add(swap(grad.reshape(2, -1, r), "zl")).astype(BF16)
+    gradient = add(swap(grad.reshape(8, -1, r), "y"))
 
     new_first = 0.9 * first_moment + 0.1 * gradient
     new_second = 0.999 * second_moment + 0.001 * gradient * gradient
     first_fix = 1.0 - 0.9**STEP
     second_fix = 1.0 - 0.999**STEP
     direction = (new_first / first_fix / (jnp.sqrt(new_second / second_fix) + 1e-08)).astype(BF16)
-    rows = direction.shape[0]
-    directions = spread(direction, "x", 4).reshape(-1, r)
+    contract = (((1,), (1,)), ((), ()))
     out = lax.dot_general(
-        directions, wide, (((1,), (1,)), ((), ())), preferred_element_type=F32
-    ).astype(BF16)
-    out = swap(out.reshape(4, rows, -1), "x")
-    out = out.reshape(4, rows, 4, -1).transpose(1, 2, 0, 3).reshape(rows, -1)
+        lax.dynamic_slice_in_dim(direction, core * half, half, 1),
+        mine,
+        contract,
+        preferred_element_type=F32,
+    )
+    out = out + lax.dot_general(
+        lax.dynamic_slice_in_dim(direction, (1 - core) * half, half, 1),
+        other,
+        contract,
+        preferred_element_type=F32,
+    )
+    out = out.astype(BF16)
     return (out, new_first, new_second)
 
 

time: 153 us -> 160 us (1.046)
  waiting for transfers between devices: 13.6 us -> 20.7 us
  starting transfers between devices: 18.2 us -> 11.3 us
  matrix products: 6.9 us -> 12.2 us
  blocking collectives: 89.2 us -> 93.9 us
  local copies, waits for them, and re-layouts: 5.44 us -> 3.53 us
    all_to_all x2 -> x1, starting transfers between devices: 18.2 us -> 6.26 us  [swap(): return lax.all_to_all(parts, axis, 0, 0)]
    all_gather x1, waiting for transfers between devices: 0.01 us -> 10.9 us  [local(): lax.all_gather(lax.dynamic_slice_in_dim(projector, core * half, half, 1),...]
    dot_general x1 -> x2, matrix products: 2.4 us -> 7.82 us  [the longest x1 4.32 us: local(): lax.dot_general(lax.dynamic_slice_in_dim(direction, (1 - core) * half, ha...]
    ppermute x0 -> x1, starting transfers between devices: none -> 5.05 us  [local(): other = lax.ppermute(mine, 'c', [(0, 1), (1, 0)])]
    all_to_all x7 -> x6, blocking collectives: 89.2 us -> 93.9 us  [swap(): return lax.all_to_all(parts, axis, 0, 0)]
    all_to_all x2 -> x1, waiting for transfers between devices: 12.8 us -> 9.75 us  [swap(): return lax.all_to_all(parts, axis, 0, 0)]
    reduce_sum x5 -> x0, other arithmetic: 2.2 us -> none  [add(): return jnp.sum(parts.astype(F32), axis=0)]
    reshape x3 -> x0, local copies, waits for them, and re-layouts: 1.96 us -> none  [local(): out = out.reshape(4, rows, 4, -1).transpose(1, 2, 0, 3).reshape(rows, -1)]
  transfers between devices with their start and end apart: 3 -> 3, of which waited for: 2 -> 2; matrix products, arithmetic and copies ran while one was open for 5% -> 7% of each run, Pallas kernels for 0% -> 0%
where the time goes in v2:
time: 160 us; the launch traced here: 158 us
  blocking collectives  93.9 us (59%)
  waiting for transfers between devices  20.7 us (13%)
  between operations  14.1 us (9%)
  matrix products  12.2 us (8%)
  starting transfers between devices  11.3 us (7%)
  local copies, waits for them, and re-layouts  3.53 us (2%)
  other arithmetic  1.8 us (1%)
    all_to_all x6, blocking collectives, swap(): return lax.all_to_all(parts, axis, 0, 0)  93.9 us
    all_gather x1, waiting for transfers between devices, local(): lax.all_gather(lax.dynamic_slice_in_dim(projector, core * half, half, 1),...  10.9 us
    all_to_all x1, waiting for transfers between devices, swap(): return lax.all_to_all(parts, axis, 0, 0)  9.75 us
    all_to_all x1, starting transfers between devices, swap(): return lax.all_to_all(parts, axis, 0, 0)  6.26 us
    ppermute x1, starting transfers between devices, local(): other = lax.ppermute(mine, 'c', [(0, 1), (1, 0)])  5.05 us
    dot_general x1, matrix products, local(): lax.dot_general(lax.dynamic_slice_in_dim(direction, (1 - core) * half, ha...  4.32 us
    dot_general x1, matrix products, local(): lax.dot_general(lax.dynamic_slice_in_dim(direction, core * half, half, 1)...  3.5 us
  transfers between devices with their start and end apart: 3, of which 2 were waited for; matrix products, arithmetic and copies ran while one was open for 7% of the time, Pallas kernels for 0%

profile of v2, /device:TPU:1, one launch (start us, length us, event | category | flops | bytes accessed | tf_op | source)
XLA Modules:
  0.0 157.7 jit_solution(11414369787343112315)
XLA Ops:
  7.2 0.0 all-gather.2.cloned.1.call-start
  7.2 1.8 %constant_dynamic-slice_fusion = bf16[512,256]{1,0:T(8,128)(2,1)} fusion(bf16[512,512]{1,0:T(8,128)(2,1)} %param.7, s32[]{:T(128)S(6)} %select_n.7), kind=kLoop, calls=%fused_computation.21 | loop fusion | bytes 524292 | tf_op jit(solution)/shard_map/dynamic_slice | solution.py:31
  9.0 0.0 all-gather.2.cloned.1.call-update
  9.1 2.1 %convolution_convert_fusion.1 = bf16[1024,512]{1,0:T(8,128)(2,1)S(1)} fusion(bf16[1024,512]{1,0:T(8,128)(2,1)} %param.5, bf16[512,512]{1,0:T(8,128)(2,1)} %param.7), kind=kOutput, calls=%fused_computation.3 | convolution fusion | flops 537395200 | bytes 2621440 | tf_op jit(solution)/shard_map/dot_general | solution.py:33
  11.1 15.1 %all_to_all.35 = bf16[4,256,512]{2,1,0:T(8,128)(2,1)S(1)} all-to-all(bf16[4,256,512]{2,1,0:T(8,128)(2,1)S(1)} %bitcast.33), channel_id=1, replica_groups=mesh['zh'=4,'x'=4,'y'=8,'zl'=2,'c'=2] {'x'}, dimensions={0} | all-to-all | bytes 2097152 | tf_op jit(solution)/shard_map/all_to_all | solution.py:12
  26.2 0.1 add_convert_fusion.2
  26.4 27.6 %all_to_all.36 = bf16[4,64,512]{2,1,0:T(8,128)(2,1)S(1)} all-to-all(bf16[4,64,512]{2,1,0:T(8,128)(2,1)S(1)} %bitcast.31), channel_id=1, replica_groups=mesh['zh'=4,'x'=4,'y'=8,'zl'=2,'c'=2] {'zh'}, dimensions={0} | all-to-all | bytes 524288 | tf_op jit(solution)/shard_map/all_to_all | solution.py:12
  54.0 11.3 %all_to_all.37 = bf16[4,64,512]{2,1,0:T(8,128)(2,1)S(1)} all-to-all(bf16[4,64,512]{2,1,0:T(8,128)(2,1)S(1)} %broadcast_in_dim.16), channel_id=1, replica_groups=mesh['zh'=4,'x'=4,'y'=8,'zl'=2,'c'=2] {'zh'}, dimensions={0} | all-to-all | bytes 524288 | tf_op jit(solution)/shard_map/all_to_all | solution.py:12
  65.3 0.1 broadcast_in_dim.18
  65.4 24.0 %all_to_all.38 = bf16[4,256,512]{2,1,0:T(8,128)(2,1)S(1)} all-to-all(bf16[4,256,512]{2,1,0:T(8,128)(2,1)S(1)} %broadcast_in_dim.18), channel_id=1, replica_groups=mesh['zh'=4,'x'=4,'y'=8,'zl'=2,'c'=2] {'x'}, dimensions={0} | all-to-all | bytes 2097152 | tf_op jit(solution)/shard_map/all_to_all | solution.py:12
  89.3 2.4 %fusion.1 = bf16[1024,512]{0,1:T(8,128)(2,1)} fusion(bf16[1024,512]{1,0:T(8,128)(2,1)S(1)} %bitcast.29, bf16[1024,1024]{1,0:T(8,128)(2,1)S(1)} %copy-done), kind=kOutput, calls=%fused_computation.4 | convolution fusion | flops 1074266112 | bytes 4194304 | tf_op jit(solution)/shard_map/dot_general | solution.py:38
  91.7 10.9 %all-gather.2.cloned.1.call-done = bf16[8192,256]{1,0:T(8,128)(2,1)} async-done(((bf16[512,256]{1,0:T(8,128)(2,1)}), bf16[8192,256]{1,0:T(8,128)(2,1)}) %all-gather.2.cloned.1.call-update) | async-done | bytes 4194320 | tf_op jit(solution)/shard_map/all_gather | solution.py:30
  102.6 5.1 %collective-permute-start = (bf16[8192,256]{1,0:T(8,128)(2,1)}, bf16[8192,256]{1,0:T(8,128)(2,1)}, u32[]{:S(2)}, u32[]{:S(2)}) collective-permute-start(bf16[8192,256]{1,0:T(8,128)(2,1)} %all-gather.2.cloned.1.call-done), channel_id=1, source_target_pairs={{0,1},{1,0},{2,3},{3,2},{4,5},{5,4},{6,7},{7,6},{8,9},{9,8},{10,11... | collective-permute-start | bytes 12582920 | tf_op jit(solution)/shard_map/ppermute | solution.py:42
  107.7 1.5 copy.8
  109.2 0.1 copy.9
  109.3 5.9 %all_to_all.39 = bf16[2,512,512]{2,1,0:T(8,128)(2,1)S(1)} all-to-all(bf16[2,512,512]{2,1,0:T(8,128)(2,1)S(1)} %bitcast.28), channel_id=1, replica_groups=mesh['zh'=4,'x'=4,'y'=8,'zl'=2,'c'=2] {'c'}, dimensions={0} | all-to-all | bytes 2097152 | tf_op jit(solution)/shard_map/all_to_all | solution.py:12
  115.2 0.1 add_convert_fusion
  115.3 10.1 %all_to_all.40 = bf16[2,256,512]{2,1,0:T(8,128)(2,1)S(1)} all-to-all(bf16[2,256,512]{2,1,0:T(8,128)(2,1)S(1)} %bitcast.30), channel_id=1, replica_groups=mesh['zh'=4,'x'=4,'y'=8,'zl'=2,'c'=2] {'zl'}, dimensions={0} | all-to-all | bytes 1048576 | tf_op jit(solution)/shard_map/all_to_all | solution.py:12
  125.5 0.8 add_convert_fusion.1
  126.3 6.3 %all-to-all-start.6 = ((bf16[8,32,512]{2,1,0:T(8,128)(2,1)}), bf16[8,32,512]{2,1,0:T(8,128)(2,1)S(1)}, u32[]{:S(2)}, u32[]{:S(2)}) async-start(bf16[8,32,512]{2,1,0:T(8,128)(2,1)} %bitcast.10), calls=%async_computation.6 | async-start | bytes 524288 | tf_op jit(solution)/shard_map/all_to_all | solution.py:12
  132.5 9.7 %all-to-all-done.6 = bf16[8,32,512]{2,1,0:T(8,128)(2,1)S(1)} async-done(((bf16[8,32,512]{2,1,0:T(8,128)(2,1)}), bf16[8,32,512]{2,1,0:T(8,128)(2,1)S(1)}, u32[]{:S(2)}, u32[]{:S(2)}) %all-to-all-start.6) | async-done | bytes 262176 | tf_op jit(solution)/shard_map/all_to_all | solution.py:12
  142.3 0.7 divide_convert_fusion
  143.0 3.5 %fusion.6 = f32[32,8192]{1,0:T(8,128)S(1)} fusion(bf16[8192,256]{1,0:T(8,128)(2,1)} %all-gather.2.cloned.1.call-done, bf16[32,512]{1,0:T(8,128)(2,1)S(1)} %get-tuple-element.7, s32[]{:T(128)S(6)} %select_n.7), kind=kOutput, calls=%fused_computation.17 | convolution fusion | flops 134217728 | bytes 5259268 | tf_op jit(solution)/shard_map/dot_general | solution.py:54
  146.5 4.3 %fusion = bf16[32,8192]{1,0:T(8,128)(2,1)} fusion(f32[32,8192]{1,0:T(8,128)S(1)} %fusion.6, bf16[8192,256]{1,0:T(8,128)(2,1)} %collective-permute-done, bf16[32,512]{1,0:T(8,128)(2,1)S(1)} %get-tuple-element.7, s32[]{:T(128)S(6)} %select_n.8), kind=kOutput, calls=%fused_computation.1 | convolution fusion | flops 134742016 | bytes 5783556 | tf_op jit(solution)/shard_map/dot_general | solution.py:60
  (9 shorter events, 0.1 us)
Async XLA Ops:
  7.2 82.2 %copy-start = (bf16[1024,1024]{1,0:T(8,128)(2,1)S(1)}, bf16[1024,1024]{1,0:T(8,128)(2,1)}, u32[]{:S(2)}) copy-start(bf16[1024,1024]{1,0:T(8,128)(2,1)} %param.6) | copy-start | bytes 6291460
  7.2 95.5 %all-gather.2.cloned.1.call-start = ((), (), s32[]{:S(2)}) async-start(), calls=%async_computation.7 | async-start | bytes 4456448 | tf_op jit(solution)/shard_map/all_gather | solution.py:30
  102.6 43.9 %collective-permute-start = (bf16[8192,256]{1,0:T(8,128)(2,1)}, bf16[8192,256]{1,0:T(8,128)(2,1)}, u32[]{:S(2)}, u32[]{:S(2)}) collective-permute-start(bf16[8192,256]{1,0:T(8,128)(2,1)} %all-gather.2.cloned.1.call-done), channel_id=1, source_target_pairs={{0,1},{1,0},{2,3},{3,2},{4,5},{5,4},{6,7},{7,6},{8,9},{9,8},{10,11... | collective-permute-start | bytes 12582920 | tf_op jit(solution)/shard_map/ppermute | solution.py:42
  109.2 33.1 %copy-start.1 = (f32[32,512]{1,0:T(8,128)S(1)}, f32[32,512]{1,0:T(8,128)}, u32[]{:S(2)}) copy-start(f32[32,512]{1,0:T(8,128)} %param.8) | copy-start | bytes 196612
  109.2 33.1 %copy-start.2 = (f32[32,512]{1,0:T(8,128)S(1)}, f32[32,512]{1,0:T(8,128)}, u32[]{:S(2)}) copy-start(f32[32,512]{1,0:T(8,128)} %param.9) | copy-start | bytes 196612
  126.3 16.0 %all-to-all-start.6 = ((bf16[8,32,512]{2,1,0:T(8,128)(2,1)}), bf16[8,32,512]{2,1,0:T(8,128)(2,1)S(1)}, u32[]{:S(2)}, u32[]{:S(2)}) async-start(bf16[8,32,512]{2,1,0:T(8,128)(2,1)} %bitcast.10), calls=%async_computation.6 | async-start | bytes 524288 | tf_op jit(solution)/shard_map/all_to_all | solution.py:12
Sparse Core Ops, SparseCore 0:
  11.6 90.9 all-gather.1

commit v3 on v1

v3 whole, which is shorter than its diff:
```python
import jax
import jax.numpy as jnp
from jax import lax
from jax.experimental import pallas as pl
from jax.experimental.pallas import tpu as pltpu
from jax.sharding import Mesh, PartitionSpec as P

STEP = 10
F32 = jnp.float32
BF16 = jnp.bfloat16


def swap(parts, axis):
    return lax.all_to_all(parts, axis, 0, 0)


def add(parts):
    total = parts[0].astype(F32)
    for i in range(1, parts.shape[0]):
        total = total + parts[i].astype(F32)
    return total


def scattered_sum(part, axis, n):
    return add(swap(part.reshape((n, -1) + part.shape[1:]), axis))


def spread(block, axis, n):
    return swap(jnp.broadcast_to(block[None], (n,) + block.shape), axis)


def turn_kernel(in_ref, out_ref):
    turned = in_ref[...].T
    rows = out_ref.shape[2]
    for i in range(out_ref.shape[1]):
        for c in range(2):
            at = (2 * i + c) * rows
            out_ref[c, i] = turned[at : at + rows]


def turn(tangent):
    tokens, hidden = tangent.shape
    rows = hidden // 32
    step = 128 // (2 * rows)
    out = pl.pallas_call(
        turn_kernel,
        grid=(hidden // 128,),
        in_specs=[pl.BlockSpec((tokens, 128), lambda i: (0, i))],
        out_specs=pl.BlockSpec((2, step, rows, tokens), lambda i: (0, i, 0, 0)),
        out_shape=jax.ShapeDtypeStruct((2, 16, rows, tokens), tangent.dtype),
        cost_estimate=pl.CostEstimate(flops=0, bytes_accessed=4 * tokens * hidden, transcendentals=0),
        compiler_params=pltpu.CompilerParams(vmem_limit_bytes=16 * 2**20),
    )(tangent)
    return out.reshape(hidden, tokens)


def product_kernel(a_ref, b_ref, out_ref):
    step = 256

    @pl.loop(0, a_ref.shape[0] // step)
    def _(i):
        at = pl.ds(pl.multiple_of(i * step, step), step)
        out_ref[at] = jnp.dot(a_ref[at], b_ref[...], preferred_element_type=F32).astype(BF16)


def product(a, b):
    vmem = pl.BlockSpec(memory_space=pltpu.VMEM)
    m, k, n = a.shape[0], a.shape[1], b.shape[1]
    return pl.pallas_call(
        product_kernel,
        in_specs=[vmem, vmem],
        out_specs=vmem,
        out_shape=jax.ShapeDtypeStruct((m, n), BF16),
        cost_estimate=pl.CostEstimate(
            flops=2 * m * k * n, bytes_accessed=2 * (m * k + k * n + m * n), transcendentals=0
        ),
        compiler_params=pltpu.CompilerParams(vmem_limit_bytes=16 * 2**20),
    )(a, b)


def weave_kernel(core_ref, mine_ref, other_ref, out_ref):
    core = core_ref[0]
    for z in range(out_ref.shape[0]):
        for y in range(out_ref.shape[1]):
            out_ref[z, y, core] = mine_ref[y, z]
            out_ref[z, y, 1 - core] = other_ref[y, z]


def weave(core, mine, other):
    y, z, rows, r = mine.shape
    vmem = pl.BlockSpec(memory_space=pltpu.VMEM)
    out = pl.pallas_call(
        weave_kernel,
        in_specs=[pl.BlockSpec(memory_space=pltpu.SMEM), vmem, vmem],
        out_specs=vmem,
        out_shape=jax.ShapeDtypeStruct((z, y, 2, rows, r), mine.dtype),
        cost_estimate=pl.CostEstimate(flops=0, bytes_accessed=8 * mine.size, transcendentals=0),
        compiler_params=pltpu.CompilerParams(vmem_limit_bytes=16 * 2**20),
    )(core.reshape(1), mine, other)
    return out.reshape(-1, r)


def lay_kernel(in_ref, out_ref):
    n = in_ref.shape[0]
    width = in_ref.shape[2] // n
    for z in range(n):
        for x in range(n):
            at = (z * n + x) * width
            out_ref[:, at : at + width] = in_ref[x, :, z * width : (z + 1) * width]


def lay(blocks):
    n, rows, columns = blocks.shape
    vmem = pl.BlockSpec(memory_space=pltpu.VMEM)
    return pl.pallas_call(
        lay_kernel,
        in_specs=[vmem],
        out_specs=vmem,
        out_shape=jax.ShapeDtypeStruct((rows, n * columns), blocks.dtype),
        cost_estimate=pl.CostEstimate(flops=0, bytes_accessed=4 * blocks.size, transcendentals=0),
        compiler_params=pltpu.CompilerParams(vmem_limit_bytes=16 * 2**20),
    )(blocks)


def local(tokens, tangent, projector, first_moment, second_moment):
    r = projector.shape[1]
    core = lax.axis_index("c")
    share = projector.shape[0] // 16
    piece = lax.dynamic_slice_in_dim(projector, (lax.axis_index("y") * 2 + core) * share, share, 0)
    pieces = spread(piece, "zh", 4)
    mine = spread(pieces, "y", 8)
    tt = turn(tangent)
    part = jnp.dot(tokens, projector, preferred_element_type=F32).astype(BF16)
    part = scattered_sum(part, ("zh", "x"), 16).astype(BF16)
    reduced = spread(part, ("zh", "x"), 16).reshape(-1, r)
    grad = product(tt, reduced)
    mine, grad = lax.optimization_barrier((mine, grad))
    other = lax.ppermute(mine, "c", [(0, 1), (1, 0)])
    grad = scattered_sum(grad, "c", 2).astype(BF16)
    gradient = scattered_sum(grad, ("y", "zl"), 16)
    wide = weave(core, mine, other)

    new_first = 0.9 * first_moment + 0.1 * gradient
    new_second = 0.999 * second_moment + 0.001 * gradient * gradient
    first_fix = 1.0 - 0.9**STEP
    second_fix = 1.0 - 0.999**STEP
    direction = (new_first / first_fix / (jnp.sqrt(new_second / second_fix) + 1e-08)).astype(BF16)
    rows = direction.shape[0]
    directions = spread(direction, "x", 4).reshape(-1, r)
    out = lax.dot_general(
        directions, wide, (((1,), (1,)), ((), ())), preferred_element_type=F32
    ).astype(BF16)
    out = lay(swap(out.reshape(4, rows, -1), "x"))
    return (out, new_first, new_second)


def solution(mesh):
    fine = Mesh(mesh.devices.reshape(4, 4, 8, 2, 2), ("zh", "x", "y", "zl", "c"))
    dp, fsdp = ("zh", "x"), ("y", "zl", "c")
    rows = P(dp + fsdp, None)
    return jax.shard_map(
        local,
        mesh=fine,
        in_specs=(P(fsdp, dp), P(fsdp, dp), P(dp, None), rows, rows),
        out_specs=(rows, rows, rows),
        check_vma=False,
    )
```

time: 153 us -> 174 us (1.14)
  blocking collectives: 89.2 us -> 45.7 us
  waiting for transfers between devices: 13.6 us -> 55 us
  starting transfers between devices: 18.2 us -> 48.5 us
  between operations: 14.1 us -> 0.76 us
  local copies, waits for them, and re-layouts: 5.44 us -> 10.5 us
  Pallas kernels: 0 us -> 4.43 us
  matrix products: 6.9 us -> 3.55 us
    all_to_all x7 -> x3, blocking collectives: 89.2 us -> 45.7 us  [swap(): return lax.all_to_all(parts, axis, 0, 0)]
    all_to_all x2 -> x5, waiting for transfers between devices: 12.8 us -> 55 us  [swap(): return lax.all_to_all(parts, axis, 0, 0)]
    all_to_all x2 -> x5, starting transfers between devices: 18.2 us -> 45.9 us  [swap(): return lax.all_to_all(parts, axis, 0, 0)]
    unnamed x6 -> x18, local copies, waits for them, and re-layouts: 0.02 us -> 7.22 us
    pallas_call x0 -> x4, Pallas kernels: none -> 4.43 us  [the longest x1 1.75 us: product(): pl.pallas_call(product_kernel, in_specs=[vmem, vmem], out_specs=vmem, out...]
    ppermute x0 -> x1, starting transfers between devices: none -> 2.56 us  [local(): other = lax.ppermute(mine, 'c', [(0, 1), (1, 0)])]
    dot_general x1 -> x0, matrix products: 2.28 us -> none  [local(): lax.dot_general(tangent, reduced, (((0,), (0,)), ((), ())), preferred_ele...]
    reduce_sum x5 -> x0, other arithmetic: 2.2 us -> none  [add(): return jnp.sum(parts.astype(F32), axis=0)]
  transfers between devices with their start and end apart: 3 -> 6, of which waited for: 2 -> 5; matrix products, arithmetic and copies ran while one was open for 5% -> 2% of each run, Pallas kernels for 0% -> 2%
where the time goes in v3:
time: 174 us; the launch traced here: 171 us
  waiting for transfers between devices  55 us (32%)
  starting transfers between devices  48.5 us (28%)
  blocking collectives  45.7 us (26%)
  local copies, waits for them, and re-layouts  10.5 us (6%)
  Pallas kernels  4.43 us (3%)
  matrix products  3.55 us (2%)
  other arithmetic  2.83 us (2%)
    all_to_all x5, waiting for transfers between devices, swap(): return lax.all_to_all(parts, axis, 0, 0)  55 us
    all_to_all x5, starting transfers between devices, swap(): return lax.all_to_all(parts, axis, 0, 0)  45.9 us
    all_to_all x3, blocking collectives, swap(): return lax.all_to_all(parts, axis, 0, 0)  45.7 us
    unnamed x18, local copies, waits for them, and re-layouts  7.22 us
  transfers between devices with their start and end apart: 6, of which 5 were waited for; matrix products, arithmetic and copies ran while one was open for 2% of the time, Pallas kernels for 2%

profile of v3, /device:TPU:1, one launch (start us, length us, event | category | flops | bytes accessed | tf_op | source)
XLA Modules:
  0.0 171.3 jit_solution(2508322280153124104)
XLA Ops:
  0.6 1.2 copy-done
  1.9 2.7 %convolution_convert_fusion.1 = bf16[1024,512]{1,0:T(8,128)(2,1)} fusion(bf16[1024,512]{1,0:T(8,128)(2,1)S(1)} %copy-done, bf16[512,512]{1,0:T(8,128)(2,1)} %param.7), kind=kOutput, calls=%fused_computation.1 | convolution fusion | flops 537395200 | bytes 2621440 | tf_op jit(solution)/shard_map/dot_general | solution.py:133
  4.6 13.4 %all-to-all-start.2 = ((bf16[16,64,512]{2,1,0:T(8,128)(2,1)}), bf16[16,64,512]{2,1,0:T(8,128)(2,1)S(1)}, u32[]{:S(2)}, u32[]{:S(2)}) async-start(bf16[16,64,512]{2,1,0:T(8,128)(2,1)} %bitcast.1), calls=%async_computation.2 | async-start | bytes 2097152 | tf_op jit(solution)/shard_map/all_to_all | solution.py:14
  18.8 21.0 %all-to-all-done.2 = bf16[16,64,512]{2,1,0:T(8,128)(2,1)S(1)} async-done(((bf16[16,64,512]{2,1,0:T(8,128)(2,1)}), bf16[16,64,512]{2,1,0:T(8,128)(2,1)S(1)}, u32[]{:S(2)}, u32[]{:S(2)}) %all-to-all-start.2) | async-done | bytes 1048608 | tf_op jit(solution)/shard_map/all_to_all | solution.py:14
  40.5 5.8 %all-to-all-start = ((bf16[4,32,512]{2,1,0:T(8,128)(2,1)}), bf16[4,32,512]{2,1,0:T(8,128)(2,1)S(1)}, u32[]{:S(2)}, u32[]{:S(2)}) async-start(bf16[4,32,512]{2,1,0:T(8,128)(2,1)} %broadcast_in_dim.10), calls=%async_computation | async-start | bytes 262144 | tf_op jit(solution)/shard_map/all_to_all | solution.py:14
  46.4 7.1 %all-to-all-done = bf16[4,32,512]{2,1,0:T(8,128)(2,1)S(1)} async-done(((bf16[4,32,512]{2,1,0:T(8,128)(2,1)}), bf16[4,32,512]{2,1,0:T(8,128)(2,1)S(1)}, u32[]{:S(2)}, u32[]{:S(2)}) %all-to-all-start) | async-done | bytes 131104 | tf_op jit(solution)/shard_map/all_to_all | solution.py:14
  53.6 18.4 %all_to_all.40 = bf16[16,64,512]{2,1,0:T(8,128)(2,1)S(1)} all-to-all(bf16[16,64,512]{2,1,0:T(8,128)(2,1)S(1)} %broadcast_in_dim.13), channel_id=1, replica_groups=mesh['zh'=4,'x'=4,'y'=8,'zl'=2,'c'=2] {'zh','x'}, dimensions={0} | all-to-all | bytes 2097152 | tf_op jit(solution)/shard_map/all_to_all | solution.py:14
  72.0 1.1 broadcast_in_dim.11
  73.1 6.8 %all-to-all-start.1 = ((bf16[8,4,32,512]{3,2,1,0:T(8,128)(2,1)}), bf16[8,4,32,512]{3,2,1,0:T(8,128)(2,1)S(1)}, u32[]{:S(2)}, u32[]{:S(2)}) async-start(bf16[8,4,32,512]{3,2,1,0:T(8,128)(2,1)} %broadcast_in_dim.11), calls=%async_computation.1 | async-start | bytes 2097152 | tf_op jit(solution)/shard_map/all_to_all | solution.py:14
  79.9 1.6 copy-done.4
  81.5 1.7 %shard_map.76 = bf16[2,16,32,1024]{3,2,1,0:T(8,128)(2,1)S(1)} custom-call(bf16[1024,1024]{1,0:T(8,128)(2,1)S(1)} %copy-done.4), custom_call_target="tpu_custom_call" | custom-call | bytes 4194304 | tf_op jit(solution)/shard_map/pallas_call | solution.py:45
  83.2 1.7 %shard_map.77 = bf16[1024,512]{1,0:T(8,128)(2,1)S(1)} custom-call(bf16[1024,1024]{1,0:T(8,128)(2,1)S(1)} %bitcast.23, bf16[1024,512]{1,0:T(8,128)(2,1)S(1)} %bitcast.24), custom_call_target="tpu_custom_call" | custom-call | flops 1073741824 | bytes 4194304 | tf_op jit(solution)/shard_map/pallas_call | solution.py:69
  85.0 1.0 copy-done.3
  85.9 11.9 %all-to-all-done.1.mine_ref = bf16[8,4,32,512]{3,2,1,0:T(8,128)(2,1)S(1)} async-done(((bf16[8,4,32,512]{3,2,1,0:T(8,128)(2,1)}), bf16[8,4,32,512]{3,2,1,0:T(8,128)(2,1)S(1)}, u32[]{:S(2)}, u32[]{:S(2)}) %all-to-all-start.1) | async-done | bytes 1048608 | tf_op jit(solution)/shard_map/all_to_all | solution.py:14
  97.8 17.6 %all_to_all.41 = bf16[2,512,512]{2,1,0:T(8,128)(2,1)S(1)} all-to-all(bf16[2,512,512]{2,1,0:T(8,128)(2,1)} %bitcast.25), channel_id=1, replica_groups=mesh['zh'=4,'x'=4,'y'=8,'zl'=2,'c'=2] {'c'}, dimensions={0} | all-to-all | bytes 2097152 | tf_op jit(solution)/shard_map/all_to_all | solution.py:14
  116.4 16.5 %all-to-all-start.5 = ((bf16[16,32,512]{2,1,0:T(8,128)(2,1)}), bf16[16,32,512]{2,1,0:T(8,128)(2,1)}, u32[]{:S(2)}, u32[]{:S(2)}) async-start(bf16[16,32,512]{2,1,0:T(8,128)(2,1)} %bitcast.5), calls=%async_computation.5 | async-start | bytes 1048576 | tf_op jit(solution)/shard_map/all_to_all | solution.py:14
  132.9 2.6 %collective-permute-start = (bf16[8,4,32,512]{3,2,1,0:T(8,128)(2,1)S(1)}, bf16[8,4,32,512]{3,2,1,0:T(8,128)(2,1)S(1)}, u32[]{:S(2)}, u32[]{:S(2)}) collective-permute-start(bf16[8,4,32,512]{3,2,1,0:T(8,128)(2,1)S(1)} %all-to-all-done.1.mine_ref), channel_id=1, source_target_pairs={{0,1},{1,0},{2,3},{3,2},{4,5},{5,4},{6,7},{7,6},{8,9},{9,8},{10,11... | collective-permute-start | bytes 3145736 | tf_op jit(solution)/shard_map/ppermute | solution.py:138
  135.5 13.9 %all-to-all-done.5 = bf16[16,32,512]{2,1,0:T(8,128)(2,1)} async-done(((bf16[16,32,512]{2,1,0:T(8,128)(2,1)}), bf16[16,32,512]{2,1,0:T(8,128)(2,1)}, u32[]{:S(2)}, u32[]{:S(2)}) %all-to-all-start.5) | async-done | bytes 524320 | tf_op jit(solution)/shard_map/all_to_all | solution.py:14
  149.3 1.8 %divide_convert_fusion = (bf16[32,512]{1,0:T(8,128)(2,1)S(1)}, f32[32,512]{1,0:T(8,128)}, f32[32,512]{1,0:T(8,128)}) fusion(f32[32,512]{1,0:T(8,128)S(1)} %copy-done.7, f32[32,512]{1,0:T(8,128)S(1)} %copy-done.8, bf16[16,32,512]{2,1,0:T(8,128)(2,1)} %all-to-all-done.5), kind=kLoop, calls=%fused_computation.7 | loop fusion | flops 704512 | bytes 819200 | tf_op jit(solution)/shard_map/convert_element_type | solution.py:147
  151.8 3.3 %all-to-all-start.6 = ((bf16[4,32,512]{2,1,0:T(8,128)(2,1)}), bf16[4,32,512]{2,1,0:T(8,128)(2,1)S(1)}, u32[]{:S(2)}, u32[]{:S(2)}) async-start(bf16[4,32,512]{2,1,0:T(8,128)(2,1)} %broadcast_in_dim.14), calls=%async_computation.6 | async-start | bytes 262144 | tf_op jit(solution)/shard_map/all_to_all | solution.py:14
  156.1 1.2 copy-done.2
  157.3 1.2 copy-done.6
  158.7 1.2 all-to-all-done.6
  160.7 9.7 %all_to_all.42.in_ref = bf16[4,32,2048]{2,1,0:T(8,128)(2,1)S(1)} all-to-all(bf16[4,32,2048]{2,1,0:T(8,128)(2,1)S(1)} %bitcast.26), channel_id=1, replica_groups=mesh['zh'=4,'x'=4,'y'=8,'zl'=2,'c'=2] {'x'}, dimensions={0} | all-to-all | bytes 1048576 | tf_op jit(solution)/shard_map/all_to_all | solution.py:14
  (23 shorter events, 6.0 us)
Async XLA Ops:
  0.6 1.2 copy-start
  4.6 35.2 %all-to-all-start.2 = ((bf16[16,64,512]{2,1,0:T(8,128)(2,1)}), bf16[16,64,512]{2,1,0:T(8,128)(2,1)S(1)}, u32[]{:S(2)}, u32[]{:S(2)}) async-start(bf16[16,64,512]{2,1,0:T(8,128)(2,1)} %bitcast.1), calls=%async_computation.2 | async-start | bytes 2097152 | tf_op jit(solution)/shard_map/all_to_all | solution.py:14
  40.5 13.1 %all-to-all-start = ((bf16[4,32,512]{2,1,0:T(8,128)(2,1)}), bf16[4,32,512]{2,1,0:T(8,128)(2,1)S(1)}, u32[]{:S(2)}, u32[]{:S(2)}) async-start(bf16[4,32,512]{2,1,0:T(8,128)(2,1)} %broadcast_in_dim.10), calls=%async_computation | async-start | bytes 262144 | tf_op jit(solution)/shard_map/all_to_all | solution.py:14
  73.1 24.7 %all-to-all-start.1 = ((bf16[8,4,32,512]{3,2,1,0:T(8,128)(2,1)}), bf16[8,4,32,512]{3,2,1,0:T(8,128)(2,1)S(1)}, u32[]{:S(2)}, u32[]{:S(2)}) async-start(bf16[8,4,32,512]{3,2,1,0:T(8,128)(2,1)} %broadcast_in_dim.11), calls=%async_computation.1 | async-start | bytes 2097152 | tf_op jit(solution)/shard_map/all_to_all | solution.py:14
  79.9 1.6 copy-start.4
  85.0 1.0 copy-start.3
  97.8 35.1 %copy-start.1 = (bf16[8,4,32,512]{3,2,1,0:T(8,128)(2,1)}, bf16[8,4,32,512]{3,2,1,0:T(8,128)(2,1)S(1)}, u32[]{:S(2)}) copy-start(bf16[8,4,32,512]{3,2,1,0:T(8,128)(2,1)S(1)} %all-to-all-done.1.mine_ref) | copy-start | bytes 3145732
  97.8 51.5 %copy-start.7 = (f32[32,512]{1,0:T(8,128)S(1)}, f32[32,512]{1,0:T(8,128)}, u32[]{:S(2)}) copy-start(f32[32,512]{1,0:T(8,128)} %param.8) | copy-start | bytes 196612
  97.8 51.5 %copy-start.8 = (f32[32,512]{1,0:T(8,128)S(1)}, f32[32,512]{1,0:T(8,128)}, u32[]{:S(2)}) copy-start(f32[32,512]{1,0:T(8,128)} %param.9) | copy-start | bytes 196612
  116.4 33.0 %all-to-all-start.5 = ((bf16[16,32,512]{2,1,0:T(8,128)(2,1)}), bf16[16,32,512]{2,1,0:T(8,128)(2,1)}, u32[]{:S(2)}, u32[]{:S(2)}) async-start(bf16[16,32,512]{2,1,0:T(8,128)(2,1)} %bitcast.5), calls=%async_computation.5 | async-start | bytes 1048576 | tf_op jit(solution)/shard_map/all_to_all | solution.py:14
  132.9 22.2 %collective-permute-start = (bf16[8,4,32,512]{3,2,1,0:T(8,128)(2,1)S(1)}, bf16[8,4,32,512]{3,2,1,0:T(8,128)(2,1)S(1)}, u32[]{:S(2)}, u32[]{:S(2)}) collective-permute-start(bf16[8,4,32,512]{3,2,1,0:T(8,128)(2,1)S(1)} %all-to-all-done.1.mine_ref), channel_id=1, source_target_pairs={{0,1},{1,0},{2,3},{3,2},{4,5},{5,4},{6,7},{7,6},{8,9},{9,8},{10,11... | collective-permute-start | bytes 3145736 | tf_op jit(solution)/shard_map/ppermute | solution.py:138
  151.8 8.1 %all-to-all-start.6 = ((bf16[4,32,512]{2,1,0:T(8,128)(2,1)}), bf16[4,32,512]{2,1,0:T(8,128)(2,1)S(1)}, u32[]{:S(2)}, u32[]{:S(2)}) async-start(bf16[4,32,512]{2,1,0:T(8,128)(2,1)} %broadcast_in_dim.14), calls=%async_computation.6 | async-start | bytes 262144 | tf_op jit(solution)/shard_map/all_to_all | solution.py:14
  155.1 1.0 copy-start.5
  156.1 1.2 copy-start.2
  157.3 1.2 copy-start.6

commit v4 on v3

--- a/solution.py
+++ b/solution.py
@@ -27,6 +27,12 @@
 
 def spread(block, axis, n):
     return swap(jnp.broadcast_to(block[None], (n,) + block.shape), axis)
+
+
+def rotate(block, axis, n):
+    return [block] + [
+        lax.ppermute(block, axis, [(i, (i + k) % n) for i in range(n)]) for k in range(1, n)
+    ]
 
 
 def turn_kernel(in_ref, out_ref):
@@ -78,15 +84,16 @@
     )(a, b)
 
 
-def weave_kernel(core_ref, mine_ref, other_ref, out_ref):
-    core = core_ref[0]
-    for z in range(out_ref.shape[0]):
-        for y in range(out_ref.shape[1]):
-            out_ref[z, y, core] = mine_ref[y, z]
-            out_ref[z, y, 1 - core] = other_ref[y, z]
+def weave_kernel(at_ref, mine_ref, other_ref, out_ref):
+    z, y, core = at_ref[0], at_ref[1], at_ref[2]
+    for i in range(mine_ref.shape[0]):
+        for j in range(mine_ref.shape[1]):
+            to_z, to_y = lax.rem(z + 4 - j, 4), lax.rem(y + 8 - i, 8)
+            out_ref[to_z, to_y, core] = mine_ref[i, j]
+            out_ref[to_z, to_y, 1 - core] = other_ref[i, j]
 
 
-def weave(core, mine, other):
+def weave(at, mine, other):
     y, z, rows, r = mine.shape
     vmem = pl.BlockSpec(memory_space=pltpu.VMEM)
     out = pl.pallas_call(
@@ -96,7 +103,7 @@
         out_shape=jax.ShapeDtypeStruct((z, y, 2, rows, r), mine.dtype),
         cost_estimate=pl.CostEstimate(flops=0, bytes_accessed=8 * mine.size, transcendentals=0),
         compiler_params=pltpu.CompilerParams(vmem_limit_bytes=16 * 2**20),
-    )(core.reshape(1), mine, other)
+    )(at, mine, other)
     return out.reshape(-1, r)
 
 
@@ -124,21 +131,22 @@
 
 def local(tokens, tangent, projector, first_moment, second_moment):
     r = projector.shape[1]
-    core = lax.axis_index("c")
+    z, y, core = lax.axis_index("zh"), lax.axis_index("y"), lax.axis_index("c")
     share = projector.shape[0] // 16
-    piece = lax.dynamic_slice_in_dim(projector, (lax.axis_index("y") * 2 + core) * share, share, 0)
-    pieces = spread(piece, "zh", 4)
-    mine = spread(pieces, "y", 8)
+    piece = lax.dynamic_slice_in_dim(projector, (y * 2 + core) * share, share, 0)
+    pieces = jnp.stack(rotate(piece, "zh", 4))
     tt = turn(tangent)
     part = jnp.dot(tokens, projector, preferred_element_type=F32).astype(BF16)
     part = scattered_sum(part, ("zh", "x"), 16).astype(BF16)
+    pieces, tt, part = lax.optimization_barrier((pieces, tt, part))
+    mine = jnp.stack(rotate(pieces, "y", 8))
     reduced = spread(part, ("zh", "x"), 16).reshape(-1, r)
     grad = product(tt, reduced)
     mine, grad = lax.optimization_barrier((mine, grad))
+    grad = scattered_sum(grad, "c", 2).astype(BF16)
     other = lax.ppermute(mine, "c", [(0, 1), (1, 0)])
-    grad = scattered_sum(grad, "c", 2).astype(BF16)
     gradient = scattered_sum(grad, ("y", "zl"), 16)
-    wide = weave(core, mine, other)
+    wide = weave(jnp.stack([z, y, core]).astype(jnp.int32), mine, other)
 
     new_first = 0.9 * first_moment + 0.1 * gradient
     new_second = 0.999 * second_moment + 0.001 * gradient * gradient

time: 174 us -> 166 us (0.954)
  the two profiles are of different devices: /device:TPU:1 before, /device:TPU:2 now
where the time goes in v4:
time: 166 us; the launch traced here: 165 us
  starting transfers between devices  74.5 us (45%)
  waiting for transfers between devices  47.3 us (28%)
  blocking collectives  15.2 us (9%)
  local copies, waits for them, and re-layouts  13.6 us (8%)
  Pallas kernels  6.95 us (4%)
  matrix products  3.52 us (2%)
  other arithmetic  3.16 us (2%)
    ppermute x10, starting transfers between devices, rotate(): lax.ppermute(block, axis, [(i, (i + k) % n) for i in range(n)])  40.5 us
    all_to_all x4, starting transfers between devices, swap(): return lax.all_to_all(parts, axis, 0, 0)  32.2 us
    ppermute x10, waiting for transfers between devices, rotate(): lax.ppermute(block, axis, [(i, (i + k) % n) for i in range(n)])  30.6 us
    all_to_all x4, waiting for transfers between devices, swap(): return lax.all_to_all(parts, axis, 0, 0)  16.8 us
    all_to_all x2, blocking collectives, swap(): return lax.all_to_all(parts, axis, 0, 0)  15.2 us
    unnamed x19, local copies, waits for them, and re-layouts  9.69 us
  transfers between devices with their start and end apart: 15, of which 7 were waited for; matrix products, arithmetic and copies ran while one was open for 5% of the time, Pallas kernels for 2%

profile of v4, /device:TPU:2, one launch (start us, length us, event | category | flops | bytes accessed | tf_op | source)
XLA Modules:
  0.0 165.1 jit_solution(838982046796524682)
XLA Ops:
  1.9 2.7 %convolution_convert_fusion.1 = bf16[1024,512]{1,0:T(8,128)(2,1)} fusion(bf16[1024,512]{1,0:T(8,128)(2,1)S(1)} %copy-done, bf16[512,512]{1,0:T(8,128)(2,1)} %param.7), kind=kOutput, calls=%fused_computation.1 | convolution fusion | flops 537395200 | bytes 2621440 | tf_op jit(solution)/shard_map/dot_general | solution.py:139
  4.6 13.3 %all-to-all-start = ((bf16[16,64,512]{2,1,0:T(8,128)(2,1)}), bf16[16,64,512]{2,1,0:T(8,128)(2,1)}, u32[]{:S(2)}, u32[]{:S(2)}) async-start(bf16[16,64,512]{2,1,0:T(8,128)(2,1)} %bitcast.5), calls=%async_computation | async-start | bytes 2097152 | tf_op jit(solution)/shard_map/all_to_all | solution.py:14
  18.6 7.3 %collective-permute-start.1 = (bf16[32,512]{1,0:T(8,128)(2,1)S(1)}, bf16[32,512]{1,0:T(8,128)(2,1)S(1)}, u32[]{:S(2)}, u32[]{:S(2)}) collective-permute-start(bf16[32,512]{1,0:T(8,128)(2,1)S(1)} %constant_dynamic-slice_fusion), channel_id=1, source_target_pairs={{0,256},{128,384},{256,0},{384,128},{1,257},{129,385},{257,1},{385... | collective-permute-start | bytes 98312 | tf_op jit(solution)/shard_map/ppermute | solution.py:34
  25.9 2.5 %collective-permute-start = (bf16[32,512]{1,0:T(8,128)(2,1)S(1)}, bf16[32,512]{1,0:T(8,128)(2,1)S(1)}, u32[]{:S(2)}, u32[]{:S(2)}) collective-permute-start(bf16[32,512]{1,0:T(8,128)(2,1)S(1)} %constant_dynamic-slice_fusion), channel_id=1, source_target_pairs={{0,128},{128,256},{256,384},{384,0},{1,129},{129,257},{257,385},{3... | collective-permute-start | bytes 98312 | tf_op jit(solution)/shard_map/ppermute | solution.py:34
  28.4 5.5 %collective-permute-start.2 = (bf16[32,512]{1,0:T(8,128)(2,1)S(1)}, bf16[32,512]{1,0:T(8,128)(2,1)S(1)}, u32[]{:S(2)}, u32[]{:S(2)}) collective-permute-start(bf16[32,512]{1,0:T(8,128)(2,1)S(1)} %constant_dynamic-slice_fusion), channel_id=1, source_target_pairs={{0,384},{128,0},{256,128},{384,256},{1,385},{129,1},{257,129},{385... | collective-permute-start | bytes 98312 | tf_op jit(solution)/shard_map/ppermute | solution.py:34
  38.0 3.5 %collective-permute-done.1 = bf16[32,512]{1,0:T(8,128)(2,1)S(1)} collective-permute-done((bf16[32,512]{1,0:T(8,128)(2,1)S(1)}, bf16[32,512]{1,0:T(8,128)(2,1)S(1)}, u32[]{:S(2)}, u32[]{:S(2)}) %collective-permute-start.1) | collective-permute-done | bytes 32800 | tf_op jit(solution)/shard_map/ppermute | solution.py:34
  41.5 2.4 %collective-permute-done.2 = bf16[32,512]{1,0:T(8,128)(2,1)S(1)} collective-permute-done((bf16[32,512]{1,0:T(8,128)(2,1)S(1)}, bf16[32,512]{1,0:T(8,128)(2,1)S(1)}, u32[]{:S(2)}, u32[]{:S(2)}) %collective-permute-start.2) | collective-permute-done | bytes 32800 | tf_op jit(solution)/shard_map/ppermute | solution.py:34
  46.4 9.5 %all-to-all-start.1 = ((bf16[16,64,512]{2,1,0:T(8,128)(2,1)}), bf16[16,64,512]{2,1,0:T(8,128)(2,1)}, u32[]{:S(2)}, u32[]{:S(2)}) async-start(bf16[16,64,512]{2,1,0:T(8,128)(2,1)} %broadcast_in_dim.4), calls=%async_computation.1 | async-start | bytes 2097152 | tf_op jit(solution)/shard_map/all_to_all | solution.py:14
  55.9 5.4 %collective-permute-start.9 = (bf16[4,32,512]{2,1,0:T(8,128)(2,1)S(1)}, bf16[4,32,512]{2,1,0:T(8,128)(2,1)S(1)}, u32[]{:S(2)}, u32[]{:S(2)}) collective-permute-start(bf16[4,32,512]{2,1,0:T(8,128)(2,1)S(1)} %pad_maximum_fusion), channel_id=1, source_target_pairs={{0,28},{4,0},{8,4},{12,8},{16,12},{20,16},{24,20},{28,24},{1,29},{... | collective-permute-start | bytes 393224 | tf_op jit(solution)/shard_map/ppermute | solution.py:34
  61.3 4.0 %collective-permute-start.8 = (bf16[4,32,512]{2,1,0:T(8,128)(2,1)S(1)}, bf16[4,32,512]{2,1,0:T(8,128)(2,1)S(1)}, u32[]{:S(2)}, u32[]{:S(2)}) collective-permute-start(bf16[4,32,512]{2,1,0:T(8,128)(2,1)S(1)} %pad_maximum_fusion), channel_id=1, source_target_pairs={{0,24},{4,28},{8,0},{12,4},{16,8},{20,12},{24,16},{28,20},{1,25},{... | collective-permute-start | bytes 393224 | tf_op jit(solution)/shard_map/ppermute | solution.py:34
  65.3 3.0 %collective-permute-start.7 = (bf16[4,32,512]{2,1,0:T(8,128)(2,1)S(1)}, bf16[4,32,512]{2,1,0:T(8,128)(2,1)S(1)}, u32[]{:S(2)}, u32[]{:S(2)}) collective-permute-start(bf16[4,32,512]{2,1,0:T(8,128)(2,1)S(1)} %pad_maximum_fusion), channel_id=1, source_target_pairs={{0,20},{4,24},{8,28},{12,0},{16,4},{20,8},{24,12},{28,16},{1,21},{... | collective-permute-start | bytes 393224 | tf_op jit(solution)/shard_map/ppermute | solution.py:34
  68.4 5.9 %collective-permute-start.6 = (bf16[4,32,512]{2,1,0:T(8,128)(2,1)S(1)}, bf16[4,32,512]{2,1,0:T(8,128)(2,1)S(1)}, u32[]{:S(2)}, u32[]{:S(2)}) collective-permute-start(bf16[4,32,512]{2,1,0:T(8,128)(2,1)S(1)} %pad_maximum_fusion), channel_id=1, source_target_pairs={{0,16},{4,20},{8,24},{12,28},{16,0},{20,4},{24,8},{28,12},{1,17},{... | collective-permute-start | bytes 393224 | tf_op jit(solution)/shard_map/ppermute | solution.py:34
  74.3 2.6 %collective-permute-start.3 = (bf16[4,32,512]{2,1,0:T(8,128)(2,1)S(1)}, bf16[4,32,512]{2,1,0:T(8,128)(2,1)S(1)}, u32[]{:S(2)}, u32[]{:S(2)}) collective-permute-start(bf16[4,32,512]{2,1,0:T(8,128)(2,1)S(1)} %pad_maximum_fusion), channel_id=1, source_target_pairs={{0,4},{4,8},{8,12},{12,16},{16,20},{20,24},{24,28},{28,0},{1,5},{5... | collective-permute-start | bytes 393224 | tf_op jit(solution)/shard_map/ppermute | solution.py:34
  77.6 7.4 %collective-permute-done.3 = bf16[4,32,512]{2,1,0:T(8,128)(2,1)S(1)} collective-permute-done((bf16[4,32,512]{2,1,0:T(8,128)(2,1)S(1)}, bf16[4,32,512]{2,1,0:T(8,128)(2,1)S(1)}, u32[]{:S(2)}, u32[]{:S(2)}) %collective-permute-start.3) | collective-permute-done | bytes 131104 | tf_op jit(solution)/shard_map/ppermute | solution.py:34
  87.6 8.7 %collective-permute-done.4 = bf16[4,32,512]{2,1,0:T(8,128)(2,1)S(1)} collective-permute-done((bf16[4,32,512]{2,1,0:T(8,128)(2,1)S(1)}, bf16[4,32,512]{2,1,0:T(8,128)(2,1)S(1)}, u32[]{:S(2)}, u32[]{:S(2)}) %collective-permute-start.4) | collective-permute-done | bytes 131104 | tf_op jit(solution)/shard_map/ppermute | solution.py:34
  96.3 2.4 %collective-permute-start.5 = (bf16[4,32,512]{2,1,0:T(8,128)(2,1)S(1)}, bf16[4,32,512]{2,1,0:T(8,128)(2,1)S(1)}, u32[]{:S(2)}, u32[]{:S(2)}) collective-permute-start(bf16[4,32,512]{2,1,0:T(8,128)(2,1)S(1)} %pad_maximum_fusion), channel_id=1, source_target_pairs={{0,12},{4,16},{8,20},{12,24},{16,28},{20,0},{24,4},{28,8},{1,13},{... | collective-permute-start | bytes 393224 | tf_op jit(solution)/shard_map/ppermute | solution.py:34
  99.3 8.5 %collective-permute-done.5 = bf16[4,32,512]{2,1,0:T(8,128)(2,1)S(1)} collective-permute-done((bf16[4,32,512]{2,1,0:T(8,128)(2,1)S(1)}, bf16[4,32,512]{2,1,0:T(8,128)(2,1)S(1)}, u32[]{:S(2)}, u32[]{:S(2)}) %collective-permute-start.5) | collective-permute-done | bytes 131104 | tf_op jit(solution)/shard_map/ppermute | solution.py:34
  111.2 3.0 %shard_map.77 = bf16[1024,512]{1,0:T(8,128)(2,1)S(1)} custom-call(bf16[1024,1024]{1,0:T(8,128)(2,1)S(1)} %bitcast.50, bf16[1024,512]{1,0:T(8,128)(2,1)} %bitcast.16.b_ref), custom_call_target="tpu_custom_call" | custom-call | flops 1073741824 | bytes 4194304 | tf_op jit(solution)/shard_map/pallas_call | solution.py:75
  114.2 4.7 %all_to_all.30 = bf16[2,512,512]{2,1,0:T(8,128)(2,1)S(1)} all-to-all(bf16[2,512,512]{2,1,0:T(8,128)(2,1)S(1)} %bitcast.52), channel_id=1, replica_groups=mesh['zh'=4,'x'=4,'y'=8,'zl'=2,'c'=2] {'c'}, dimensions={0} | all-to-all | bytes 2097152 | tf_op jit(solution)/shard_map/all_to_all | solution.py:14
  119.8 4.1 %all-to-all-start.3 = ((bf16[16,32,512]{2,1,0:T(8,128)(2,1)}), bf16[16,32,512]{2,1,0:T(8,128)(2,1)S(1)}, u32[]{:S(2)}, u32[]{:S(2)}) async-start(bf16[16,32,512]{2,1,0:T(8,128)(2,1)} %bitcast.18), calls=%async_computation.3 | async-start | bytes 1048576 | tf_op jit(solution)/shard_map/all_to_all | solution.py:14
  123.9 1.9 %collective-permute-start.10 = (bf16[8,4,32,512]{3,2,1,0:T(8,128)(2,1)}, bf16[8,4,32,512]{3,2,1,0:T(8,128)(2,1)S(1)}, u32[]{:S(2)}, u32[]{:S(2)}) collective-permute-start(bf16[8,4,32,512]{3,2,1,0:T(8,128)(2,1)} %bitcast_dynamic-update-slice_fusion.mine_ref), channel_id=1, source_target_pairs={{0,1},{1,0},{2,3},{3,2},{4,5},{5,4},{6,7},{7,6},{8,9},{9,8},{10,11... | collective-permute-start | bytes 3145736 | tf_op jit(solution)/shard_map/ppermute | solution.py:147
  125.8 16.0 %all-to-all-done.3 = bf16[16,32,512]{2,1,0:T(8,128)(2,1)S(1)} async-done(((bf16[16,32,512]{2,1,0:T(8,128)(2,1)}), bf16[16,32,512]{2,1,0:T(8,128)(2,1)S(1)}, u32[]{:S(2)}, u32[]{:S(2)}) %all-to-all-start.3) | async-done | bytes 524320 | tf_op jit(solution)/shard_map/all_to_all | solution.py:14
  143.2 5.3 %all-to-all-start.4 = ((bf16[4,32,512]{2,1,0:T(8,128)(2,1)}), bf16[4,32,512]{2,1,0:T(8,128)(2,1)S(1)}, u32[]{:S(2)}, u32[]{:S(2)}) async-start(bf16[4,32,512]{2,1,0:T(8,128)(2,1)} %broadcast_in_dim.5), calls=%async_computation.4 | async-start | bytes 262144 | tf_op jit(solution)/shard_map/all_to_all | solution.py:14
  153.8 10.5 %all_to_all.31.in_ref = bf16[4,32,2048]{2,1,0:T(8,128)(2,1)S(1)} all-to-all(bf16[4,32,2048]{2,1,0:T(8,128)(2,1)S(1)} %bitcast.53), channel_id=1, replica_groups=mesh['zh'=4,'x'=4,'y'=8,'zl'=2,'c'=2] {'x'}, dimensions={0} | all-to-all | bytes 1048576 | tf_op jit(solution)/shard_map/all_to_all | solution.py:14
  (43 shorter events, 24.3 us)
Async XLA Ops:
  0.6 1.2 copy-start
  4.6 39.4 %all-to-all-start = ((bf16[16,64,512]{2,1,0:T(8,128)(2,1)}), bf16[16,64,512]{2,1,0:T(8,128)(2,1)}, u32[]{:S(2)}, u32[]{:S(2)}) async-start(bf16[16,64,512]{2,1,0:T(8,128)(2,1)} %bitcast.5), calls=%async_computation | async-start | bytes 2097152 | tf_op jit(solution)/shard_map/all_to_all | solution.py:14
  18.6 22.9 %collective-permute-start.1 = (bf16[32,512]{1,0:T(8,128)(2,1)S(1)}, bf16[32,512]{1,0:T(8,128)(2,1)S(1)}, u32[]{:S(2)}, u32[]{:S(2)}) collective-permute-start(bf16[32,512]{1,0:T(8,128)(2,1)S(1)} %constant_dynamic-slice_fusion), channel_id=1, source_target_pairs={{0,256},{128,384},{256,0},{384,128},{1,257},{129,385},{257,1},{385... | collective-permute-start | bytes 98312 | tf_op jit(solution)/shard_map/ppermute | solution.py:34
  25.9 15.6 %collective-permute-start = (bf16[32,512]{1,0:T(8,128)(2,1)S(1)}, bf16[32,512]{1,0:T(8,128)(2,1)S(1)}, u32[]{:S(2)}, u32[]{:S(2)}) collective-permute-start(bf16[32,512]{1,0:T(8,128)(2,1)S(1)} %constant_dynamic-slice_fusion), channel_id=1, source_target_pairs={{0,128},{128,256},{256,384},{384,0},{1,129},{129,257},{257,385},{3... | collective-permute-start | bytes 98312 | tf_op jit(solution)/shard_map/ppermute | solution.py:34
  28.4 15.5 %collective-permute-start.2 = (bf16[32,512]{1,0:T(8,128)(2,1)S(1)}, bf16[32,512]{1,0:T(8,128)(2,1)S(1)}, u32[]{:S(2)}, u32[]{:S(2)}) collective-permute-start(bf16[32,512]{1,0:T(8,128)(2,1)S(1)} %constant_dynamic-slice_fusion), channel_id=1, source_target_pairs={{0,384},{128,0},{256,128},{384,256},{1,385},{129,1},{257,129},{385... | collective-permute-start | bytes 98312 | tf_op jit(solution)/shard_map/ppermute | solution.py:34
  34.7 1.6 copy-start.1
  46.4 64.8 %all-to-all-start.1 = ((bf16[16,64,512]{2,1,0:T(8,128)(2,1)}), bf16[16,64,512]{2,1,0:T(8,128)(2,1)}, u32[]{:S(2)}, u32[]{:S(2)}) async-start(bf16[16,64,512]{2,1,0:T(8,128)(2,1)} %broadcast_in_dim.4), calls=%async_computation.1 | async-start | bytes 2097152 | tf_op jit(solution)/shard_map/all_to_all | solution.py:14
  55.9 54.6 %collective-permute-start.9 = (bf16[4,32,512]{2,1,0:T(8,128)(2,1)S(1)}, bf16[4,32,512]{2,1,0:T(8,128)(2,1)S(1)}, u32[]{:S(2)}, u32[]{:S(2)}) collective-permute-start(bf16[4,32,512]{2,1,0:T(8,128)(2,1)S(1)} %pad_maximum_fusion), channel_id=1, source_target_pairs={{0,28},{4,0},{8,4},{12,8},{16,12},{20,16},{24,20},{28,24},{1,29},{... | collective-permute-start | bytes 393224 | tf_op jit(solution)/shard_map/ppermute | solution.py:34
  61.3 48.6 %collective-permute-start.8 = (bf16[4,32,512]{2,1,0:T(8,128)(2,1)S(1)}, bf16[4,32,512]{2,1,0:T(8,128)(2,1)S(1)}, u32[]{:S(2)}, u32[]{:S(2)}) collective-permute-start(bf16[4,32,512]{2,1,0:T(8,128)(2,1)S(1)} %pad_maximum_fusion), channel_id=1, source_target_pairs={{0,24},{4,28},{8,0},{12,4},{16,8},{20,12},{24,16},{28,20},{1,25},{... | collective-permute-start | bytes 393224 | tf_op jit(solution)/shard_map/ppermute | solution.py:34
  65.3 43.8 %collective-permute-start.7 = (bf16[4,32,512]{2,1,0:T(8,128)(2,1)S(1)}, bf16[4,32,512]{2,1,0:T(8,128)(2,1)S(1)}, u32[]{:S(2)}, u32[]{:S(2)}) collective-permute-start(bf16[4,32,512]{2,1,0:T(8,128)(2,1)S(1)} %pad_maximum_fusion), channel_id=1, source_target_pairs={{0,20},{4,24},{8,28},{12,0},{16,4},{20,8},{24,12},{28,16},{1,21},{... | collective-permute-start | bytes 393224 | tf_op jit(solution)/shard_map/ppermute | solution.py:34
  68.4 40.1 %collective-permute-start.6 = (bf16[4,32,512]{2,1,0:T(8,128)(2,1)S(1)}, bf16[4,32,512]{2,1,0:T(8,128)(2,1)S(1)}, u32[]{:S(2)}, u32[]{:S(2)}) collective-permute-start(bf16[4,32,512]{2,1,0:T(8,128)(2,1)S(1)} %pad_maximum_fusion), channel_id=1, source_target_pairs={{0,16},{4,20},{8,24},{12,28},{16,0},{20,4},{24,8},{28,12},{1,17},{... | collective-permute-start | bytes 393224 | tf_op jit(solution)/shard_map/ppermute | solution.py:34
  74.3 10.7 %collective-permute-start.3 = (bf16[4,32,512]{2,1,0:T(8,128)(2,1)S(1)}, bf16[4,32,512]{2,1,0:T(8,128)(2,1)S(1)}, u32[]{:S(2)}, u32[]{:S(2)}) collective-permute-start(bf16[4,32,512]{2,1,0:T(8,128)(2,1)S(1)} %pad_maximum_fusion), channel_id=1, source_target_pairs={{0,4},{4,8},{8,12},{12,16},{16,20},{20,24},{24,28},{28,0},{1,5},{5... | collective-permute-start | bytes 393224 | tf_op jit(solution)/shard_map/ppermute | solution.py:34
  85.0 11.3 %collective-permute-start.4 = (bf16[4,32,512]{2,1,0:T(8,128)(2,1)S(1)}, bf16[4,32,512]{2,1,0:T(8,128)(2,1)S(1)}, u32[]{:S(2)}, u32[]{:S(2)}) collective-permute-start(bf16[4,32,512]{2,1,0:T(8,128)(2,1)S(1)} %pad_maximum_fusion), channel_id=1, source_target_pairs={{0,8},{4,12},{8,16},{12,20},{16,24},{20,28},{24,0},{28,4},{1,9},{5... | collective-permute-start | bytes 393224 | tf_op jit(solution)/shard_map/ppermute | solution.py:34
  96.3 11.6 %collective-permute-start.5 = (bf16[4,32,512]{2,1,0:T(8,128)(2,1)S(1)}, bf16[4,32,512]{2,1,0:T(8,128)(2,1)S(1)}, u32[]{:S(2)}, u32[]{:S(2)}) collective-permute-start(bf16[4,32,512]{2,1,0:T(8,128)(2,1)S(1)} %pad_maximum_fusion), channel_id=1, source_target_pairs={{0,12},{4,16},{8,20},{12,24},{16,28},{20,0},{24,4},{28,8},{1,13},{... | collective-permute-start | bytes 393224 | tf_op jit(solution)/shard_map/ppermute | solution.py:34
  114.2 27.6 %copy-start.4 = (f32[32,512]{1,0:T(8,128)S(1)}, f32[32,512]{1,0:T(8,128)}, u32[]{:S(2)}) copy-start(f32[32,512]{1,0:T(8,128)} %param.8) | copy-start | bytes 196612
  114.2 27.6 %copy-start.5 = (f32[32,512]{1,0:T(8,128)S(1)}, f32[32,512]{1,0:T(8,128)}, u32[]{:S(2)}) copy-start(f32[32,512]{1,0:T(8,128)} %param.9) | copy-start | bytes 196612
  119.8 22.0 %all-to-all-start.3 = ((bf16[16,32,512]{2,1,0:T(8,128)(2,1)}), bf16[16,32,512]{2,1,0:T(8,128)(2,1)S(1)}, u32[]{:S(2)}, u32[]{:S(2)}) async-start(bf16[16,32,512]{2,1,0:T(8,128)(2,1)} %bitcast.18), calls=%async_computation.3 | async-start | bytes 1048576 | tf_op jit(solution)/shard_map/all_to_all | solution.py:14
  123.9 24.7 %collective-permute-start.10 = (bf16[8,4,32,512]{3,2,1,0:T(8,128)(2,1)}, bf16[8,4,32,512]{3,2,1,0:T(8,128)(2,1)S(1)}, u32[]{:S(2)}, u32[]{:S(2)}) collective-permute-start(bf16[8,4,32,512]{3,2,1,0:T(8,128)(2,1)} %bitcast_dynamic-update-slice_fusion.mine_ref), channel_id=1, source_target_pairs={{0,1},{1,0},{2,3},{3,2},{4,5},{5,4},{6,7},{7,6},{8,9},{9,8},{10,11... | collective-permute-start | bytes 3145736 | tf_op jit(solution)/shard_map/ppermute | solution.py:147
  143.2 9.8 %all-to-all-start.4 = ((bf16[4,32,512]{2,1,0:T(8,128)(2,1)}), bf16[4,32,512]{2,1,0:T(8,128)(2,1)S(1)}, u32[]{:S(2)}, u32[]{:S(2)}) async-start(bf16[4,32,512]{2,1,0:T(8,128)(2,1)} %broadcast_in_dim.5), calls=%async_computation.4 | async-start | bytes 262144 | tf_op jit(solution)/shard_map/all_to_all | solution.py:14
  148.6 1.0 copy-start.2
  149.6 1.2 copy-start.3

commit v5 on v3

--- a/solution.py
+++ b/solution.py
@@ -27,6 +27,10 @@
 
 def spread(block, axis, n):
     return swap(jnp.broadcast_to(block[None], (n,) + block.shape), axis)
+
+
+def back(block, axis, n, k):
+    return lax.ppermute(block, axis, [(i, (i + k) % n) for i in range(n)])
 
 
 def turn_kernel(in_ref, out_ref):
@@ -78,25 +82,28 @@
     )(a, b)
 
 
-def weave_kernel(core_ref, mine_ref, other_ref, out_ref):
-    core = core_ref[0]
-    for z in range(out_ref.shape[0]):
-        for y in range(out_ref.shape[1]):
-            out_ref[z, y, core] = mine_ref[y, z]
-            out_ref[z, y, 1 - core] = other_ref[y, z]
+def weave_kernel(at_ref, own_ref, mine_ref, other_ref, out_ref):
+    z, core = at_ref[0], at_ref[1]
+    half = own_ref.shape[0] // 2
+    out_ref[z, 0] = own_ref[:half]
+    out_ref[z, 1] = own_ref[half:]
+    for k in range(mine_ref.shape[0]):
+        to = lax.rem(z + 3 - k, 4)
+        out_ref[to, core] = mine_ref[k]
+        out_ref[to, 1 - core] = other_ref[k]
 
 
-def weave(core, mine, other):
-    y, z, rows, r = mine.shape
+def weave(at, own, mine, other):
+    back_z, rows, r = mine.shape
     vmem = pl.BlockSpec(memory_space=pltpu.VMEM)
     out = pl.pallas_call(
         weave_kernel,
-        in_specs=[pl.BlockSpec(memory_space=pltpu.SMEM), vmem, vmem],
+        in_specs=[pl.BlockSpec(memory_space=pltpu.SMEM), vmem, vmem, vmem],
         out_specs=vmem,
-        out_shape=jax.ShapeDtypeStruct((z, y, 2, rows, r), mine.dtype),
+        out_shape=jax.ShapeDtypeStruct((back_z + 1, 2, rows, r), mine.dtype),
         cost_estimate=pl.CostEstimate(flops=0, bytes_accessed=8 * mine.size, transcendentals=0),
         compiler_params=pltpu.CompilerParams(vmem_limit_bytes=16 * 2**20),
-    )(core.reshape(1), mine, other)
+    )(at, own, mine, other)
     return out.reshape(-1, r)
 
 
@@ -124,21 +131,27 @@
 
 def local(tokens, tangent, projector, first_moment, second_moment):
     r = projector.shape[1]
-    core = lax.axis_index("c")
-    share = projector.shape[0] // 16
-    piece = lax.dynamic_slice_in_dim(projector, (lax.axis_index("y") * 2 + core) * share, share, 0)
-    pieces = spread(piece, "zh", 4)
-    mine = spread(pieces, "y", 8)
+    z, core = lax.axis_index("zh"), lax.axis_index("c")
     tt = turn(tangent)
+    half = projector.shape[0] // 2
+    share = lax.dynamic_slice_in_dim(projector, core * half, half, 0)
+    one, three = back(share, "zh", 4, 1), back(share, "zh", 4, 3)
     part = jnp.dot(tokens, projector, preferred_element_type=F32).astype(BF16)
-    part = scattered_sum(part, ("zh", "x"), 16).astype(BF16)
-    reduced = spread(part, ("zh", "x"), 16).reshape(-1, r)
+    part = scattered_sum(part, "x", 4).astype(BF16)
+    one, three, tt, part = lax.optimization_barrier((one, three, tt, part))
+    part = scattered_sum(part, "zh", 4).astype(BF16)
+    part = spread(part, "zh", 4).reshape(-1, r)
+    share, part = lax.optimization_barrier((share, part))
+    two = back(share, "zh", 4, 2)
+    reduced = spread(part, "x", 4).reshape(-1, r)
+    two, reduced = lax.optimization_barrier((two, reduced))
     grad = product(tt, reduced)
-    mine, grad = lax.optimization_barrier((mine, grad))
+    grad = scattered_sum(grad, "c", 2).astype(BF16)
+    one, two, three, grad = lax.optimization_barrier((one, two, three, grad))
+    mine = jnp.stack([one, two, three])
     other = lax.ppermute(mine, "c", [(0, 1), (1, 0)])
-    grad = scattered_sum(grad, "c", 2).astype(BF16)
     gradient = scattered_sum(grad, ("y", "zl"), 16)
-    wide = weave(core, mine, other)
+    wide = weave(jnp.stack([z, core]).astype(jnp.int32), projector, mine, other)
 
     new_first = 0.9 * first_moment + 0.1 * gradient
     new_second = 0.999 * second_moment + 0.001 * gradient * gradient

time: 174 us -> 144 us (0.83)
  the two profiles are of different devices: /device:TPU:1 before, /device:TPU:2 now
where the time goes in v5:
time: 144 us; the launch traced here: 143 us
  starting transfers between devices  43.3 us (30%)
  blocking collectives  40.9 us (28%)
  waiting for transfers between devices  35 us (24%)
  local copies, waits for them, and re-layouts  8.78 us (6%)
  Pallas kernels  6.2 us (4%)
  other arithmetic  4.32 us (3%)
  matrix products  3.52 us (2%)
    all_to_all x4, blocking collectives, swap(): return lax.all_to_all(parts, axis, 0, 0)  40.9 us
    all_to_all x4, starting transfers between devices, swap(): return lax.all_to_all(parts, axis, 0, 0)  29.8 us
    ppermute x3, waiting for transfers between devices, back(): return lax.ppermute(block, axis, [(i, (i + k) % n) for i in range(n)])  20.2 us
    all_to_all x4, waiting for transfers between devices, swap(): return lax.all_to_all(parts, axis, 0, 0)  14.8 us
    ppermute x3, starting transfers between devices, back(): return lax.ppermute(block, axis, [(i, (i + k) % n) for i in range(n)])  11.6 us
    unnamed x20, local copies, waits for them, and re-layouts  7.03 us
    pallas_call x1, Pallas kernels, product(): pl.pallas_call(product_kernel, in_specs=[vmem, vmem], out_specs=vmem, out...  2.97 us
  transfers between devices with their start and end apart: 8, of which 4 were waited for; matrix products, arithmetic and copies ran while one was open for 3% of the time, Pallas kernels for 2%

profile of v5, /device:TPU:2, one launch (start us, length us, event | category | flops | bytes accessed | tf_op | source)
XLA Modules:
  0.0 142.8 jit_solution(4673293857098743304)
XLA Ops:
  0.7 1.2 copy-done
  1.9 2.7 %convolution_convert_fusion.1 = bf16[1024,512]{1,0:T(8,128)(2,1)} fusion(bf16[1024,512]{1,0:T(8,128)(2,1)S(1)} %copy-done, bf16[512,512]{1,0:T(8,128)(2,1)} %own_ref.1), kind=kOutput, calls=%fused_computation.1 | convolution fusion | flops 537395200 | bytes 2621440 | tf_op jit(solution)/shard_map/dot_general | solution.py:139
  4.6 10.1 %all-to-all-start = ((bf16[4,256,512]{2,1,0:T(8,128)(2,1)}), bf16[4,256,512]{2,1,0:T(8,128)(2,1)}, u32[]{:S(2)}, u32[]{:S(2)}) async-start(bf16[4,256,512]{2,1,0:T(8,128)(2,1)} %bitcast.1), calls=%async_computation | async-start | bytes 2097152 | tf_op jit(solution)/shard_map/all_to_all | solution.py:14
  14.7 5.7 %collective-permute-start.1 = (bf16[256,512]{1,0:T(8,128)(2,1)S(1)}, bf16[256,512]{1,0:T(8,128)(2,1)}, u32[]{:S(2)}, u32[]{:S(2)}) collective-permute-start(bf16[256,512]{1,0:T(8,128)(2,1)S(1)} %constant_dynamic-slice_fusion), channel_id=1, source_target_pairs={{0,384},{128,0},{256,128},{384,256},{1,385},{129,1},{257,129},{385... | collective-permute-start | bytes 786440 | tf_op jit(solution)/shard_map/ppermute | solution.py:33
  20.4 1.9 %collective-permute-start = (bf16[256,512]{1,0:T(8,128)(2,1)S(1)}, bf16[256,512]{1,0:T(8,128)(2,1)}, u32[]{:S(2)}, u32[]{:S(2)}) collective-permute-start(bf16[256,512]{1,0:T(8,128)(2,1)S(1)} %constant_dynamic-slice_fusion), channel_id=1, source_target_pairs={{0,128},{128,256},{256,384},{384,0},{1,129},{129,257},{257,385},{3... | collective-permute-start | bytes 786440 | tf_op jit(solution)/shard_map/ppermute | solution.py:33
  22.3 1.6 %copy-done.3 = bf16[1024,1024]{1,0:T(8,128)(2,1)S(1)} copy-done((bf16[1024,1024]{1,0:T(8,128)(2,1)S(1)}, bf16[1024,1024]{1,0:T(8,128)(2,1)}, u32[]{:S(2)}) %copy-start.3) | copy-done | bytes 2097176
  23.9 1.7 %shard_map.76 = bf16[2,16,32,1024]{3,2,1,0:T(8,128)(2,1)S(1)} custom-call(bf16[1024,1024]{1,0:T(8,128)(2,1)S(1)} %copy-done.3), custom_call_target="tpu_custom_call" | custom-call | bytes 4194304 | tf_op jit(solution)/shard_map/pallas_call | solution.py:49
  25.6 1.3 fusion.1
  27.0 4.2 %collective-permute-done.1 = bf16[256,512]{1,0:T(8,128)(2,1)} collective-permute-done((bf16[256,512]{1,0:T(8,128)(2,1)S(1)}, bf16[256,512]{1,0:T(8,128)(2,1)}, u32[]{:S(2)}, u32[]{:S(2)}) %collective-permute-start.1) | collective-permute-done | bytes 262176 | tf_op jit(solution)/shard_map/ppermute | solution.py:33
  31.2 6.3 %collective-permute-done = bf16[256,512]{1,0:T(8,128)(2,1)} collective-permute-done((bf16[256,512]{1,0:T(8,128)(2,1)S(1)}, bf16[256,512]{1,0:T(8,128)(2,1)}, u32[]{:S(2)}, u32[]{:S(2)}) %collective-permute-start) | collective-permute-done | bytes 262176 | tf_op jit(solution)/shard_map/ppermute | solution.py:33
  37.5 11.8 %all_to_all.40 = bf16[4,64,512]{2,1,0:T(8,128)(2,1)S(1)} all-to-all(bf16[4,64,512]{2,1,0:T(8,128)(2,1)S(1)} %bitcast.36), channel_id=1, replica_groups=mesh['zh'=4,'x'=4,'y'=8,'zl'=2,'c'=2] {'zh'}, dimensions={0} | all-to-all | bytes 524288 | tf_op jit(solution)/shard_map/all_to_all | solution.py:14
  49.4 13.3 %all_to_all.41 = bf16[4,64,512]{2,1,0:T(8,128)(2,1)S(1)} all-to-all(bf16[4,64,512]{2,1,0:T(8,128)(2,1)S(1)} %broadcast_in_dim.9), channel_id=1, replica_groups=mesh['zh'=4,'x'=4,'y'=8,'zl'=2,'c'=2] {'zh'}, dimensions={0} | all-to-all | bytes 524288 | tf_op jit(solution)/shard_map/all_to_all | solution.py:14
  63.7 4.8 %all-to-all-start.3 = ((bf16[4,256,512]{2,1,0:T(8,128)(2,1)}), bf16[4,256,512]{2,1,0:T(8,128)(2,1)}, u32[]{:S(2)}, u32[]{:S(2)}) async-start(bf16[4,256,512]{2,1,0:T(8,128)(2,1)} %broadcast_in_dim.10), calls=%async_computation.3 | async-start | bytes 2097152 | tf_op jit(solution)/shard_map/all_to_all | solution.py:14
  68.5 4.0 %collective-permute-start.2 = (bf16[256,512]{1,0:T(8,128)(2,1)S(1)}, bf16[256,512]{1,0:T(8,128)(2,1)}, u32[]{:S(2)}, u32[]{:S(2)}) collective-permute-start(bf16[256,512]{1,0:T(8,128)(2,1)S(1)} %constant_dynamic-slice_fusion), channel_id=1, source_target_pairs={{0,256},{128,384},{256,0},{384,128},{1,257},{129,385},{257,1},{385... | collective-permute-start | bytes 786440 | tf_op jit(solution)/shard_map/ppermute | solution.py:33
  72.5 9.7 %collective-permute-done.2 = bf16[256,512]{1,0:T(8,128)(2,1)} collective-permute-done((bf16[256,512]{1,0:T(8,128)(2,1)S(1)}, bf16[256,512]{1,0:T(8,128)(2,1)}, u32[]{:S(2)}, u32[]{:S(2)}) %collective-permute-start.2) | collective-permute-done | bytes 262176 | tf_op jit(solution)/shard_map/ppermute | solution.py:33
  82.1 3.0 %shard_map.77 = bf16[1024,512]{1,0:T(8,128)(2,1)S(1)} custom-call(bf16[1024,1024]{1,0:T(8,128)(2,1)S(1)} %bitcast.32, bf16[1024,512]{1,0:T(8,128)(2,1)} %bitcast.6.b_ref), custom_call_target="tpu_custom_call" | custom-call | flops 1073741824 | bytes 4194304 | tf_op jit(solution)/shard_map/pallas_call | solution.py:73
  85.1 4.6 %all_to_all.42 = bf16[2,512,512]{2,1,0:T(8,128)(2,1)S(1)} all-to-all(bf16[2,512,512]{2,1,0:T(8,128)(2,1)S(1)} %bitcast.34), channel_id=1, replica_groups=mesh['zh'=4,'x'=4,'y'=8,'zl'=2,'c'=2] {'c'}, dimensions={0} | all-to-all | bytes 2097152 | tf_op jit(solution)/shard_map/all_to_all | solution.py:14
  90.6 10.1 %all-to-all-start.5 = ((bf16[16,32,512]{2,1,0:T(8,128)(2,1)}), bf16[16,32,512]{2,1,0:T(8,128)(2,1)S(1)}, u32[]{:S(2)}, u32[]{:S(2)}) async-start(bf16[16,32,512]{2,1,0:T(8,128)(2,1)} %bitcast.9), calls=%async_computation.5 | async-start | bytes 1048576 | tf_op jit(solution)/shard_map/all_to_all | solution.py:14
  100.7 1.2 pad_maximum_fusion.mine_ref
  102.0 1.9 %collective-permute-start.3 = (bf16[3,256,512]{2,1,0:T(8,128)(2,1)S(1)}, bf16[3,256,512]{2,1,0:T(8,128)(2,1)S(1)}, u32[]{:S(2)}, u32[]{:S(2)}) collective-permute-start(bf16[3,256,512]{2,1,0:T(8,128)(2,1)S(1)} %pad_maximum_fusion.mine_ref), channel_id=1, source_target_pairs={{0,1},{1,0},{2,3},{3,2},{4,5},{5,4},{6,7},{7,6},{8,9},{9,8},{10,11... | collective-permute-start | bytes 2359304 | tf_op jit(solution)/shard_map/ppermute | solution.py:152
  103.9 14.8 %all-to-all-done.5 = bf16[16,32,512]{2,1,0:T(8,128)(2,1)S(1)} async-done(((bf16[16,32,512]{2,1,0:T(8,128)(2,1)}), bf16[16,32,512]{2,1,0:T(8,128)(2,1)S(1)}, u32[]{:S(2)}, u32[]{:S(2)}) %all-to-all-start.5) | async-done | bytes 524320 | tf_op jit(solution)/shard_map/all_to_all | solution.py:14
  120.1 4.8 %all-to-all-start.6 = ((bf16[4,32,512]{2,1,0:T(8,128)(2,1)}), bf16[4,32,512]{2,1,0:T(8,128)(2,1)S(1)}, u32[]{:S(2)}, u32[]{:S(2)}) async-start(bf16[4,32,512]{2,1,0:T(8,128)(2,1)} %broadcast_in_dim.11), calls=%async_computation.6 | async-start | bytes 262144 | tf_op jit(solution)/shard_map/all_to_all | solution.py:14
  125.9 1.1 copy-done.2
  130.7 11.2 %all_to_all.43.in_ref = bf16[4,32,2048]{2,1,0:T(8,128)(2,1)S(1)} all-to-all(bf16[4,32,2048]{2,1,0:T(8,128)(2,1)S(1)} %bitcast.35), channel_id=1, replica_groups=mesh['zh'=4,'x'=4,'y'=8,'zl'=2,'c'=2] {'x'}, dimensions={0} | all-to-all | bytes 1048576 | tf_op jit(solution)/shard_map/all_to_all | solution.py:14
  (32 shorter events, 9.0 us)
Async XLA Ops:
  0.6 1.2 copy-start
  0.6 14.0 %copy-start.4 = (bf16[512,512]{1,0:T(8,128)(2,1)S(1)}, bf16[512,512]{1,0:T(8,128)(2,1)}, u32[]{:S(2)}) copy-start(bf16[512,512]{1,0:T(8,128)(2,1)} %own_ref.1) | copy-start | bytes 1572868
  4.6 21.1 %all-to-all-start = ((bf16[4,256,512]{2,1,0:T(8,128)(2,1)}), bf16[4,256,512]{2,1,0:T(8,128)(2,1)}, u32[]{:S(2)}, u32[]{:S(2)}) async-start(bf16[4,256,512]{2,1,0:T(8,128)(2,1)} %bitcast.1), calls=%async_computation | async-start | bytes 2097152 | tf_op jit(solution)/shard_map/all_to_all | solution.py:14
  14.7 16.4 %collective-permute-start.1 = (bf16[256,512]{1,0:T(8,128)(2,1)S(1)}, bf16[256,512]{1,0:T(8,128)(2,1)}, u32[]{:S(2)}, u32[]{:S(2)}) collective-permute-start(bf16[256,512]{1,0:T(8,128)(2,1)S(1)} %constant_dynamic-slice_fusion), channel_id=1, source_target_pairs={{0,384},{128,0},{256,128},{384,256},{1,385},{129,1},{257,129},{385... | collective-permute-start | bytes 786440 | tf_op jit(solution)/shard_map/ppermute | solution.py:33
  20.4 17.1 %collective-permute-start = (bf16[256,512]{1,0:T(8,128)(2,1)S(1)}, bf16[256,512]{1,0:T(8,128)(2,1)}, u32[]{:S(2)}, u32[]{:S(2)}) collective-permute-start(bf16[256,512]{1,0:T(8,128)(2,1)S(1)} %constant_dynamic-slice_fusion), channel_id=1, source_target_pairs={{0,128},{128,256},{256,384},{384,0},{1,129},{129,257},{257,385},{3... | collective-permute-start | bytes 786440 | tf_op jit(solution)/shard_map/ppermute | solution.py:33
  22.3 1.6 %copy-start.3 = (bf16[1024,1024]{1,0:T(8,128)(2,1)S(1)}, bf16[1024,1024]{1,0:T(8,128)(2,1)}, u32[]{:S(2)}) copy-start(bf16[1024,1024]{1,0:T(8,128)(2,1)} %in_ref.1) | copy-start | bytes 6291460
  63.7 18.4 %all-to-all-start.3 = ((bf16[4,256,512]{2,1,0:T(8,128)(2,1)}), bf16[4,256,512]{2,1,0:T(8,128)(2,1)}, u32[]{:S(2)}, u32[]{:S(2)}) async-start(bf16[4,256,512]{2,1,0:T(8,128)(2,1)} %broadcast_in_dim.10), calls=%async_computation.3 | async-start | bytes 2097152 | tf_op jit(solution)/shard_map/all_to_all | solution.py:14
  68.5 13.6 %collective-permute-start.2 = (bf16[256,512]{1,0:T(8,128)(2,1)S(1)}, bf16[256,512]{1,0:T(8,128)(2,1)}, u32[]{:S(2)}, u32[]{:S(2)}) collective-permute-start(bf16[256,512]{1,0:T(8,128)(2,1)S(1)} %constant_dynamic-slice_fusion), channel_id=1, source_target_pairs={{0,256},{128,384},{256,0},{384,128},{1,257},{129,385},{257,1},{385... | collective-permute-start | bytes 786440 | tf_op jit(solution)/shard_map/ppermute | solution.py:33
  89.7 29.0 %copy-start.8 = (f32[32,512]{1,0:T(8,128)S(1)}, f32[32,512]{1,0:T(8,128)}, u32[]{:S(2)}) copy-start(f32[32,512]{1,0:T(8,128)} %param.8) | copy-start | bytes 196612
  89.7 29.0 %copy-start.9 = (f32[32,512]{1,0:T(8,128)S(1)}, f32[32,512]{1,0:T(8,128)}, u32[]{:S(2)}) copy-start(f32[32,512]{1,0:T(8,128)} %param.9) | copy-start | bytes 196612
  90.6 28.0 %all-to-all-start.5 = ((bf16[16,32,512]{2,1,0:T(8,128)(2,1)}), bf16[16,32,512]{2,1,0:T(8,128)(2,1)S(1)}, u32[]{:S(2)}, u32[]{:S(2)}) async-start(bf16[16,32,512]{2,1,0:T(8,128)(2,1)} %bitcast.9), calls=%async_computation.5 | async-start | bytes 1048576 | tf_op jit(solution)/shard_map/all_to_all | solution.py:14
  101.9 23.0 %copy-start.1 = (bf16[3,256,512]{2,1,0:T(8,128)(2,1)}, bf16[3,256,512]{2,1,0:T(8,128)(2,1)S(1)}, u32[]{:S(2)}) copy-start(bf16[3,256,512]{2,1,0:T(8,128)(2,1)S(1)} %pad_maximum_fusion.mine_ref) | copy-start | bytes 2359300
  102.0 23.0 %collective-permute-start.3 = (bf16[3,256,512]{2,1,0:T(8,128)(2,1)S(1)}, bf16[3,256,512]{2,1,0:T(8,128)(2,1)S(1)}, u32[]{:S(2)}, u32[]{:S(2)}) collective-permute-start(bf16[3,256,512]{2,1,0:T(8,128)(2,1)S(1)} %pad_maximum_fusion.mine_ref), channel_id=1, source_target_pairs={{0,1},{1,0},{2,3},{3,2},{4,5},{5,4},{6,7},{7,6},{8,9},{9,8},{10,11... | collective-permute-start | bytes 2359304 | tf_op jit(solution)/shard_map/ppermute | solution.py:152
  120.1 9.8 %all-to-all-start.6 = ((bf16[4,32,512]{2,1,0:T(8,128)(2,1)}), bf16[4,32,512]{2,1,0:T(8,128)(2,1)S(1)}, u32[]{:S(2)}, u32[]{:S(2)}) async-start(bf16[4,32,512]{2,1,0:T(8,128)(2,1)} %broadcast_in_dim.11), calls=%async_computation.6 | async-start | bytes 262144 | tf_op jit(solution)/shard_map/all_to_all | solution.py:14
  125.0 0.9 copy-start.6
  125.9 1.1 copy-start.2
  127.0 1.0 copy-start.5
  128.1 1.1 copy-start.7

commit v6 on v5

--- a/solution.py
+++ b/solution.py
@@ -83,24 +83,26 @@
 
 
 def weave_kernel(at_ref, own_ref, mine_ref, other_ref, out_ref):
-    z, core = at_ref[0], at_ref[1]
-    half = own_ref.shape[0] // 2
-    out_ref[z, 0] = own_ref[:half]
-    out_ref[z, 1] = own_ref[half:]
-    for k in range(mine_ref.shape[0]):
+    z, core, odd = at_ref[0], at_ref[1], at_ref[2]
+    rows = own_ref.shape[0] // 4
+    for i in range(4):
+        out_ref[z, i // 2, i % 2] = own_ref[i * rows : (i + 1) * rows]
+    for k in range(mine_ref.shape[1]):
         to = lax.rem(z + 3 - k, 4)
-        out_ref[to, core] = mine_ref[k]
-        out_ref[to, 1 - core] = other_ref[k]
+        out_ref[to, core, odd] = mine_ref[0, k]
+        out_ref[to, core, 1 - odd] = mine_ref[1, k]
+        out_ref[to, 1 - core, odd] = other_ref[0, k]
+        out_ref[to, 1 - core, 1 - odd] = other_ref[1, k]
 
 
 def weave(at, own, mine, other):
-    back_z, rows, r = mine.shape
+    _, back_z, rows, r = mine.shape
     vmem = pl.BlockSpec(memory_space=pltpu.VMEM)
     out = pl.pallas_call(
         weave_kernel,
         in_specs=[pl.BlockSpec(memory_space=pltpu.SMEM), vmem, vmem, vmem],
         out_specs=vmem,
-        out_shape=jax.ShapeDtypeStruct((back_z + 1, 2, rows, r), mine.dtype),
+        out_shape=jax.ShapeDtypeStruct((back_z + 1, 2, 2, rows, r), mine.dtype),
         cost_estimate=pl.CostEstimate(flops=0, bytes_accessed=8 * mine.size, transcendentals=0),
         compiler_params=pltpu.CompilerParams(vmem_limit_bytes=16 * 2**20),
     )(at, own, mine, other)
@@ -131,27 +133,26 @@
 
 def local(tokens, tangent, projector, first_moment, second_moment):
     r = projector.shape[1]
-    z, core = lax.axis_index("zh"), lax.axis_index("c")
+    z, core, odd = lax.axis_index("zh"), lax.axis_index("c"), lax.axis_index("y") % 2
     tt = turn(tangent)
-    half = projector.shape[0] // 2
-    share = lax.dynamic_slice_in_dim(projector, core * half, half, 0)
-    one, three = back(share, "zh", 4, 1), back(share, "zh", 4, 3)
+    rows = projector.shape[0] // 4
+    share = lax.dynamic_slice_in_dim(projector, (core * 2 + odd) * rows, rows, 0)
+    shares = [back(share, "zh", 4, k) for k in (1, 2, 3)]
     part = jnp.dot(tokens, projector, preferred_element_type=F32).astype(BF16)
     part = scattered_sum(part, "x", 4).astype(BF16)
-    one, three, tt, part = lax.optimization_barrier((one, three, tt, part))
+    *shares, tt, part = lax.optimization_barrier((*shares, tt, part))
     part = scattered_sum(part, "zh", 4).astype(BF16)
-    part = spread(part, "zh", 4).reshape(-1, r)
-    share, part = lax.optimization_barrier((share, part))
-    two = back(share, "zh", 4, 2)
-    reduced = spread(part, "x", 4).reshape(-1, r)
-    two, reduced = lax.optimization_barrier((two, reduced))
+    shares = jnp.stack(shares)
+    neighbour = lax.ppermute(shares, "y", [(i, i ^ 1) for i in range(8)])
+    reduced = spread(part, ("x", "zh"), 16).reshape(-1, r)
+    neighbour, reduced = lax.optimization_barrier((neighbour, reduced))
     grad = product(tt, reduced)
     grad = scattered_sum(grad, "c", 2).astype(BF16)
-    one, two, three, grad = lax.optimization_barrier((one, two, three, grad))
-    mine = jnp.stack([one, two, three])
+    shares, neighbour, grad = lax.optimization_barrier((shares, neighbour, grad))
+    mine = jnp.stack([shares, neighbour])
     other = lax.ppermute(mine, "c", [(0, 1), (1, 0)])
     gradient = scattered_sum(grad, ("y", "zl"), 16)
-    wide = weave(jnp.stack([z, core]).astype(jnp.int32), projector, mine, other)
+    wide = weave(jnp.stack([z, core, odd]).astype(jnp.int32), projector, mine, other)
 
     new_first = 0.9 * first_moment + 0.1 * gradient
     new_second = 0.999 * second_moment + 0.001 * gradient * gradient

time: 144 us -> 148 us (1.028)
  blocking collectives: 40.9 us -> 31.4 us
  waiting for transfers between devices: 35 us -> 41.2 us
  starting transfers between devices: 43.3 us -> 47.4 us
  other arithmetic: 4.32 us -> 6.14 us
    ppermute x3, waiting for transfers between devices: 20.2 us -> 4.06 us  [back(): return lax.ppermute(block, axis, [(i, (i + k) % n) for i in range(n)])]
    all_to_all x4, waiting for transfers between devices: 14.8 us -> 28.3 us  [swap(): return lax.all_to_all(parts, axis, 0, 0)]
    all_to_all x4 -> x3, blocking collectives: 40.9 us -> 31.4 us  [swap(): return lax.all_to_all(parts, axis, 0, 0)]
    ppermute x0 -> x1, waiting for transfers between devices: none -> 8.85 us  [local(): neighbour = lax.ppermute(shares, 'y', [(i, i ^ 1) for i in range(8)])]
    ppermute x0 -> x1, starting transfers between devices: none -> 3.49 us  [local(): neighbour = lax.ppermute(shares, 'y', [(i, i ^ 1) for i in range(8)])]
    ppermute x3, starting transfers between devices: 11.6 us -> 13.6 us  [back(): return lax.ppermute(block, axis, [(i, (i + k) % n) for i in range(n)])]
    unnamed x20 -> x18, local copies, waits for them, and re-layouts: 7.03 us -> 7.04 us
  transfers between devices with their start and end apart: 8 -> 9, of which waited for: 4 -> 5; matrix products, arithmetic and copies ran while one was open for 3% -> 5% of each run, Pallas kernels for 2% -> 2%
where the time goes in v6:
time: 148 us; the launch traced here: 146 us
  starting transfers between devices  47.4 us (32%)
  waiting for transfers between devices  41.2 us (28%)
  blocking collectives  31.4 us (21%)
  local copies, waits for them, and re-layouts  9.69 us (7%)
  Pallas kernels  6.19 us (4%)
  other arithmetic  6.14 us (4%)
  matrix products  3.53 us (2%)
    all_to_all x3, blocking collectives, swap(): return lax.all_to_all(parts, axis, 0, 0)  31.4 us
    all_to_all x4, starting transfers between devices, swap(): return lax.all_to_all(parts, axis, 0, 0)  28.4 us
    all_to_all x4, waiting for transfers between devices, swap(): return lax.all_to_all(parts, axis, 0, 0)  28.3 us
    ppermute x3, starting transfers between devices, back(): return lax.ppermute(block, axis, [(i, (i + k) % n) for i in range(n)])  13.6 us
    ppermute x1, waiting for transfers between devices, local(): neighbour = lax.ppermute(shares, 'y', [(i, i ^ 1) for i in range(8)])  8.85 us
    unnamed x18, local copies, waits for them, and re-layouts  7.04 us
    ppermute x3, waiting for transfers between devices, back(): return lax.ppermute(block, axis, [(i, (i + k) % n) for i in range(n)])  4.06 us
    ppermute x1, starting transfers between devices, local(): neighbour = lax.ppermute(shares, 'y', [(i, i ^ 1) for i in range(8)])  3.49 us
  transfers between devices with their start and end apart: 9, of which 5 were waited for; matrix products, arithmetic and copies ran while one was open for 5% of the time, Pallas kernels for 2%

profile of v6, /device:TPU:2, one launch (start us, length us, event | category | flops | bytes accessed | tf_op | source)
XLA Modules:
  0.0 146.4 jit_solution(11647674815037946363)
XLA Ops:
  0.6 1.2 copy-done
  1.9 2.7 %convolution_convert_fusion.1 = bf16[1024,512]{1,0:T(8,128)(2,1)} fusion(bf16[1024,512]{1,0:T(8,128)(2,1)S(1)} %copy-done, bf16[512,512]{1,0:T(8,128)(2,1)} %own_ref.1), kind=kOutput, calls=%fused_computation.1 | convolution fusion | flops 537395200 | bytes 2621440 | tf_op jit(solution)/shard_map/dot_general | solution.py:141
  4.6 10.1 %all-to-all-start = ((bf16[4,256,512]{2,1,0:T(8,128)(2,1)}), bf16[4,256,512]{2,1,0:T(8,128)(2,1)}, u32[]{:S(2)}, u32[]{:S(2)}) async-start(bf16[4,256,512]{2,1,0:T(8,128)(2,1)} %bitcast.1), calls=%async_computation | async-start | bytes 2097152 | tf_op jit(solution)/shard_map/all_to_all | solution.py:14
  15.6 1.9 %collective-permute-start = (bf16[128,512]{1,0:T(8,128)(2,1)S(1)}, bf16[128,512]{1,0:T(8,128)(2,1)S(1)}, u32[]{:S(2)}, u32[]{:S(2)}) collective-permute-start(bf16[128,512]{1,0:T(8,128)(2,1)S(1)} %constant_dynamic-slice_fusion), channel_id=1, source_target_pairs={{0,128},{128,256},{256,384},{384,0},{1,129},{129,257},{257,385},{3... | collective-permute-start | bytes 393224 | tf_op jit(solution)/shard_map/ppermute | solution.py:33
  17.5 8.0 %collective-permute-start.1 = (bf16[128,512]{1,0:T(8,128)(2,1)S(1)}, bf16[128,512]{1,0:T(8,128)(2,1)S(1)}, u32[]{:S(2)}, u32[]{:S(2)}) collective-permute-start(bf16[128,512]{1,0:T(8,128)(2,1)S(1)} %constant_dynamic-slice_fusion), channel_id=1, source_target_pairs={{0,256},{128,384},{256,0},{384,128},{1,257},{129,385},{257,1},{385... | collective-permute-start | bytes 393224 | tf_op jit(solution)/shard_map/ppermute | solution.py:33
  25.5 3.7 %collective-permute-start.2 = (bf16[128,512]{1,0:T(8,128)(2,1)S(1)}, bf16[128,512]{1,0:T(8,128)(2,1)}, u32[]{:S(2)}, u32[]{:S(2)}) collective-permute-start(bf16[128,512]{1,0:T(8,128)(2,1)S(1)} %constant_dynamic-slice_fusion), channel_id=1, source_target_pairs={{0,384},{128,0},{256,128},{384,256},{1,385},{129,1},{257,129},{385... | collective-permute-start | bytes 393224 | tf_op jit(solution)/shard_map/ppermute | solution.py:33
  29.2 1.6 %copy-done.3 = bf16[1024,1024]{1,0:T(8,128)(2,1)S(1)} copy-done((bf16[1024,1024]{1,0:T(8,128)(2,1)S(1)}, bf16[1024,1024]{1,0:T(8,128)(2,1)}, u32[]{:S(2)}) %copy-start.3) | copy-done | bytes 2097176
  30.8 1.7 %shard_map.76 = bf16[2,16,32,1024]{3,2,1,0:T(8,128)(2,1)S(1)} custom-call(bf16[1024,1024]{1,0:T(8,128)(2,1)S(1)} %copy-done.3), custom_call_target="tpu_custom_call" | custom-call | bytes 4194304 | tf_op jit(solution)/shard_map/pallas_call | solution.py:49
  32.5 1.3 fusion.1
  35.0 3.0 %collective-permute-done.2 = bf16[128,512]{1,0:T(8,128)(2,1)} collective-permute-done((bf16[128,512]{1,0:T(8,128)(2,1)S(1)}, bf16[128,512]{1,0:T(8,128)(2,1)}, u32[]{:S(2)}, u32[]{:S(2)}) %collective-permute-start.2) | collective-permute-done | bytes 131104 | tf_op jit(solution)/shard_map/ppermute | solution.py:33
  38.0 15.6 %all_to_all.35 = bf16[4,64,512]{2,1,0:T(8,128)(2,1)S(1)} all-to-all(bf16[4,64,512]{2,1,0:T(8,128)(2,1)S(1)} %bitcast.39), channel_id=1, replica_groups=mesh['zh'=4,'x'=4,'y'=8,'zl'=2,'c'=2] {'zh'}, dimensions={0} | all-to-all | bytes 524288 | tf_op jit(solution)/shard_map/all_to_all | solution.py:14
  54.7 5.7 %all-to-all-start.2 = ((bf16[16,64,512]{2,1,0:T(8,128)(2,1)}), bf16[16,64,512]{2,1,0:T(8,128)(2,1)}, u32[]{:S(2)}, u32[]{:S(2)}) async-start(bf16[16,64,512]{2,1,0:T(8,128)(2,1)} %broadcast_in_dim.7), calls=%async_computation.2 | async-start | bytes 2097152 | tf_op jit(solution)/shard_map/all_to_all | solution.py:14
  61.5 3.5 %collective-permute-start.3 = (bf16[3,128,512]{2,1,0:T(8,128)(2,1)S(1)}, bf16[3,128,512]{2,1,0:T(8,128)(2,1)}, u32[]{:S(2)}, u32[]{:S(2)}) collective-permute-start(bf16[3,128,512]{2,1,0:T(8,128)(2,1)S(1)} %pad_maximum_fusion.1), channel_id=1, source_target_pairs={{0,4},{4,0},{8,12},{12,8},{16,20},{20,16},{24,28},{28,24},{1,5},{5... | collective-permute-start | bytes 1179656 | tf_op jit(solution)/shard_map/ppermute | solution.py:146
  65.0 8.8 %collective-permute-done.3 = bf16[3,128,512]{2,1,0:T(8,128)(2,1)} collective-permute-done((bf16[3,128,512]{2,1,0:T(8,128)(2,1)S(1)}, bf16[3,128,512]{2,1,0:T(8,128)(2,1)}, u32[]{:S(2)}, u32[]{:S(2)}) %collective-permute-start.3) | collective-permute-done | bytes 393248 | tf_op jit(solution)/shard_map/ppermute | solution.py:146
  73.8 13.4 %all-to-all-done.2 = bf16[16,64,512]{2,1,0:T(8,128)(2,1)} async-done(((bf16[16,64,512]{2,1,0:T(8,128)(2,1)}), bf16[16,64,512]{2,1,0:T(8,128)(2,1)}, u32[]{:S(2)}, u32[]{:S(2)}) %all-to-all-start.2) | async-done | bytes 1048608 | tf_op jit(solution)/shard_map/all_to_all | solution.py:14
  87.2 3.0 %shard_map.77 = bf16[1024,512]{1,0:T(8,128)(2,1)S(1)} custom-call(bf16[1024,1024]{1,0:T(8,128)(2,1)S(1)} %bitcast.34, bf16[1024,512]{1,0:T(8,128)(2,1)} %bitcast.8.b_ref), custom_call_target="tpu_custom_call" | custom-call | flops 1073741824 | bytes 4194304 | tf_op jit(solution)/shard_map/pallas_call | solution.py:73
  90.2 4.6 %all_to_all.36 = bf16[2,512,512]{2,1,0:T(8,128)(2,1)S(1)} all-to-all(bf16[2,512,512]{2,1,0:T(8,128)(2,1)S(1)} %bitcast.36), channel_id=1, replica_groups=mesh['zh'=4,'x'=4,'y'=8,'zl'=2,'c'=2] {'c'}, dimensions={0} | all-to-all | bytes 2097152 | tf_op jit(solution)/shard_map/all_to_all | solution.py:14
  95.7 7.2 %all-to-all-start.4 = ((bf16[16,32,512]{2,1,0:T(8,128)(2,1)}), bf16[16,32,512]{2,1,0:T(8,128)(2,1)S(1)}, u32[]{:S(2)}, u32[]{:S(2)}) async-start(bf16[16,32,512]{2,1,0:T(8,128)(2,1)} %bitcast.11), calls=%async_computation.4 | async-start | bytes 1048576 | tf_op jit(solution)/shard_map/all_to_all | solution.py:14
  104.0 1.9 %collective-permute-start.4 = (bf16[2,3,128,512]{3,2,1,0:T(8,128)(2,1)S(1)}, bf16[2,3,128,512]{3,2,1,0:T(8,128)(2,1)S(1)}, u32[]{:S(2)}, u32[]{:S(2)}) collective-permute-start(bf16[2,3,128,512]{3,2,1,0:T(8,128)(2,1)S(1)} %pad_maximum_fusion.mine_ref), channel_id=1, source_target_pairs={{0,1},{1,0},{2,3},{3,2},{4,5},{5,4},{6,7},{7,6},{8,9},{9,8},{10,11... | collective-permute-start | bytes 2359304 | tf_op jit(solution)/shard_map/ppermute | solution.py:153
  105.9 14.9 %all-to-all-done.4 = bf16[16,32,512]{2,1,0:T(8,128)(2,1)S(1)} async-done(((bf16[16,32,512]{2,1,0:T(8,128)(2,1)}), bf16[16,32,512]{2,1,0:T(8,128)(2,1)S(1)}, u32[]{:S(2)}, u32[]{:S(2)}) %all-to-all-start.4) | async-done | bytes 524320 | tf_op jit(solution)/shard_map/all_to_all | solution.py:14
  120.8 1.6 %divide_convert_fusion = (bf16[32,512]{1,0:T(8,128)(2,1)S(1)}, f32[32,512]{1,0:T(8,128)}, f32[32,512]{1,0:T(8,128)}) fusion(f32[32,512]{1,0:T(8,128)} %param.8, f32[32,512]{1,0:T(8,128)} %param.9, bf16[16,32,512]{2,1,0:T(8,128)(2,1)S(1)} %all-to-all-done.4), kind=kLoop, calls=%fused_computation.13 | loop fusion | flops 704512 | bytes 819200 | tf_op jit(solution)/shard_map/convert_element_type | solution.py:161
  123.1 5.4 %all-to-all-start.5 = ((bf16[4,32,512]{2,1,0:T(8,128)(2,1)}), bf16[4,32,512]{2,1,0:T(8,128)(2,1)S(1)}, u32[]{:S(2)}, u32[]{:S(2)}) async-start(bf16[4,32,512]{2,1,0:T(8,128)(2,1)} %broadcast_in_dim.16), calls=%async_computation.5 | async-start | bytes 262144 | tf_op jit(solution)/shard_map/all_to_all | solution.py:14
  129.5 1.1 copy-done.2
  134.4 11.2 %all_to_all.37.in_ref = bf16[4,32,2048]{2,1,0:T(8,128)(2,1)S(1)} all-to-all(bf16[4,32,2048]{2,1,0:T(8,128)(2,1)S(1)} %bitcast.37), channel_id=1, replica_groups=mesh['zh'=4,'x'=4,'y'=8,'zl'=2,'c'=2] {'x'}, dimensions={0} | all-to-all | bytes 1048576 | tf_op jit(solution)/shard_map/all_to_all | solution.py:14
  (31 shorter events, 12.4 us)
Async XLA Ops:
  0.6 1.2 copy-start
  4.6 28.0 %all-to-all-start = ((bf16[4,256,512]{2,1,0:T(8,128)(2,1)}), bf16[4,256,512]{2,1,0:T(8,128)(2,1)}, u32[]{:S(2)}, u32[]{:S(2)}) async-start(bf16[4,256,512]{2,1,0:T(8,128)(2,1)} %bitcast.1), calls=%async_computation | async-start | bytes 2097152 | tf_op jit(solution)/shard_map/all_to_all | solution.py:14
  15.6 18.3 %collective-permute-start = (bf16[128,512]{1,0:T(8,128)(2,1)S(1)}, bf16[128,512]{1,0:T(8,128)(2,1)S(1)}, u32[]{:S(2)}, u32[]{:S(2)}) collective-permute-start(bf16[128,512]{1,0:T(8,128)(2,1)S(1)} %constant_dynamic-slice_fusion), channel_id=1, source_target_pairs={{0,128},{128,256},{256,384},{384,0},{1,129},{129,257},{257,385},{3... | collective-permute-start | bytes 393224 | tf_op jit(solution)/shard_map/ppermute | solution.py:33
  17.5 17.4 %collective-permute-start.1 = (bf16[128,512]{1,0:T(8,128)(2,1)S(1)}, bf16[128,512]{1,0:T(8,128)(2,1)S(1)}, u32[]{:S(2)}, u32[]{:S(2)}) collective-permute-start(bf16[128,512]{1,0:T(8,128)(2,1)S(1)} %constant_dynamic-slice_fusion), channel_id=1, source_target_pairs={{0,256},{128,384},{256,0},{384,128},{1,257},{129,385},{257,1},{385... | collective-permute-start | bytes 393224 | tf_op jit(solution)/shard_map/ppermute | solution.py:33
  25.5 12.4 %collective-permute-start.2 = (bf16[128,512]{1,0:T(8,128)(2,1)S(1)}, bf16[128,512]{1,0:T(8,128)(2,1)}, u32[]{:S(2)}, u32[]{:S(2)}) collective-permute-start(bf16[128,512]{1,0:T(8,128)(2,1)S(1)} %constant_dynamic-slice_fusion), channel_id=1, source_target_pairs={{0,384},{128,0},{256,128},{384,256},{1,385},{129,1},{257,129},{385... | collective-permute-start | bytes 393224 | tf_op jit(solution)/shard_map/ppermute | solution.py:33
  29.2 1.6 %copy-start.3 = (bf16[1024,1024]{1,0:T(8,128)(2,1)S(1)}, bf16[1024,1024]{1,0:T(8,128)(2,1)}, u32[]{:S(2)}) copy-start(bf16[1024,1024]{1,0:T(8,128)(2,1)} %in_ref.1) | copy-start | bytes 6291460
  33.9 26.5 %copy-start.7 = (bf16[128,512]{1,0:T(8,128)(2,1)}, bf16[128,512]{1,0:T(8,128)(2,1)S(1)}, u32[]{:S(2)}) copy-start(bf16[128,512]{1,0:T(8,128)(2,1)S(1)} %collective-permute-done) | copy-start | bytes 393220
  35.0 25.4 %copy-start.8 = (bf16[128,512]{1,0:T(8,128)(2,1)}, bf16[128,512]{1,0:T(8,128)(2,1)S(1)}, u32[]{:S(2)}) copy-start(bf16[128,512]{1,0:T(8,128)(2,1)S(1)} %collective-permute-done.1) | copy-start | bytes 393220
  54.7 32.5 %all-to-all-start.2 = ((bf16[16,64,512]{2,1,0:T(8,128)(2,1)}), bf16[16,64,512]{2,1,0:T(8,128)(2,1)}, u32[]{:S(2)}, u32[]{:S(2)}) async-start(bf16[16,64,512]{2,1,0:T(8,128)(2,1)} %broadcast_in_dim.7), calls=%async_computation.2 | async-start | bytes 2097152 | tf_op jit(solution)/shard_map/all_to_all | solution.py:14
  61.5 12.3 %collective-permute-start.3 = (bf16[3,128,512]{2,1,0:T(8,128)(2,1)S(1)}, bf16[3,128,512]{2,1,0:T(8,128)(2,1)}, u32[]{:S(2)}, u32[]{:S(2)}) collective-permute-start(bf16[3,128,512]{2,1,0:T(8,128)(2,1)S(1)} %pad_maximum_fusion.1), channel_id=1, source_target_pairs={{0,4},{4,0},{8,12},{12,8},{16,20},{20,16},{24,28},{28,24},{1,5},{5... | collective-permute-start | bytes 1179656 | tf_op jit(solution)/shard_map/ppermute | solution.py:146
  95.7 25.1 %all-to-all-start.4 = ((bf16[16,32,512]{2,1,0:T(8,128)(2,1)}), bf16[16,32,512]{2,1,0:T(8,128)(2,1)S(1)}, u32[]{:S(2)}, u32[]{:S(2)}) async-start(bf16[16,32,512]{2,1,0:T(8,128)(2,1)} %bitcast.11), calls=%async_computation.4 | async-start | bytes 1048576 | tf_op jit(solution)/shard_map/all_to_all | solution.py:14
  104.0 24.6 %copy-start.1 = (bf16[2,3,128,512]{3,2,1,0:T(8,128)(2,1)}, bf16[2,3,128,512]{3,2,1,0:T(8,128)(2,1)S(1)}, u32[]{:S(2)}) copy-start(bf16[2,3,128,512]{3,2,1,0:T(8,128)(2,1)S(1)} %pad_maximum_fusion.mine_ref) | copy-start | bytes 2359300
  104.0 24.6 %collective-permute-start.4 = (bf16[2,3,128,512]{3,2,1,0:T(8,128)(2,1)S(1)}, bf16[2,3,128,512]{3,2,1,0:T(8,128)(2,1)S(1)}, u32[]{:S(2)}, u32[]{:S(2)}) collective-permute-start(bf16[2,3,128,512]{3,2,1,0:T(8,128)(2,1)S(1)} %pad_maximum_fusion.mine_ref), channel_id=1, source_target_pairs={{0,1},{1,0},{2,3},{3,2},{4,5},{5,4},{6,7},{7,6},{8,9},{9,8},{10,11... | collective-permute-start | bytes 2359304 | tf_op jit(solution)/shard_map/ppermute | solution.py:153
  123.1 10.4 %all-to-all-start.5 = ((bf16[4,32,512]{2,1,0:T(8,128)(2,1)}), bf16[4,32,512]{2,1,0:T(8,128)(2,1)S(1)}, u32[]{:S(2)}, u32[]{:S(2)}) async-start(bf16[4,32,512]{2,1,0:T(8,128)(2,1)} %broadcast_in_dim.16), calls=%async_computation.5 | async-start | bytes 262144 | tf_op jit(solution)/shard_map/all_to_all | solution.py:14
  128.6 0.9 copy-start.5
  129.5 1.1 copy-start.2
  130.7 1.0 copy-start.4
  131.7 1.1 copy-start.6

commit v7 on v3

--- a/solution.py
+++ b/solution.py
@@ -78,28 +78,6 @@
     )(a, b)
 
 
-def weave_kernel(core_ref, mine_ref, other_ref, out_ref):
-    core = core_ref[0]
-    for z in range(out_ref.shape[0]):
-        for y in range(out_ref.shape[1]):
-            out_ref[z, y, core] = mine_ref[y, z]
-            out_ref[z, y, 1 - core] = other_ref[y, z]
-
-
-def weave(core, mine, other):
-    y, z, rows, r = mine.shape
-    vmem = pl.BlockSpec(memory_space=pltpu.VMEM)
-    out = pl.pallas_call(
-        weave_kernel,
-        in_specs=[pl.BlockSpec(memory_space=pltpu.SMEM), vmem, vmem],
-        out_specs=vmem,
-        out_shape=jax.ShapeDtypeStruct((z, y, 2, rows, r), mine.dtype),
-        cost_estimate=pl.CostEstimate(flops=0, bytes_accessed=8 * mine.size, transcendentals=0),
-        compiler_params=pltpu.CompilerParams(vmem_limit_bytes=16 * 2**20),
-    )(core.reshape(1), mine, other)
-    return out.reshape(-1, r)
-
-
 def lay_kernel(in_ref, out_ref):
     n = in_ref.shape[0]
     width = in_ref.shape[2] // n
@@ -124,21 +102,18 @@
 
 def local(tokens, tangent, projector, first_moment, second_moment):
     r = projector.shape[1]
-    core = lax.axis_index("c")
     share = projector.shape[0] // 16
-    piece = lax.dynamic_slice_in_dim(projector, (lax.axis_index("y") * 2 + core) * share, share, 0)
-    pieces = spread(piece, "zh", 4)
-    mine = spread(pieces, "y", 8)
+    at = (lax.axis_index("y") * 2 + lax.axis_index("c")) * share
+    piece = lax.dynamic_slice_in_dim(projector, at, share, 0)
+    wide = lax.all_gather(piece, ("zh", "y", "c"), axis=0, tiled=True)
     tt = turn(tangent)
     part = jnp.dot(tokens, projector, preferred_element_type=F32).astype(BF16)
     part = scattered_sum(part, ("zh", "x"), 16).astype(BF16)
+    tt, part = lax.optimization_barrier((tt, part))
     reduced = spread(part, ("zh", "x"), 16).reshape(-1, r)
     grad = product(tt, reduced)
-    mine, grad = lax.optimization_barrier((mine, grad))
-    other = lax.ppermute(mine, "c", [(0, 1), (1, 0)])
     grad = scattered_sum(grad, "c", 2).astype(BF16)
     gradient = scattered_sum(grad, ("y", "zl"), 16)
-    wide = weave(core, mine, other)
 
     new_first = 0.9 * first_moment + 0.1 * gradient
     new_second = 0.999 * second_moment + 0.001 * gradient * gradient

time: 174 us -> 151 us (0.87)
  the two profiles are of different devices: /device:TPU:1 before, /device:TPU:2 now
where the time goes in v7:
time: 151 us; the launch traced here: 150 us
  blocking collectives  79.4 us (53%)
  waiting for transfers between devices  21.7 us (14%)
  starting transfers between devices  18.4 us (12%)
  between operations  14.1 us (9%)
  matrix products  5.15 us (3%)
  local copies, waits for them, and re-layouts  4.94 us (3%)
  Pallas kernels  4.29 us (3%)
  other arithmetic  2.28 us (2%)
    all_to_all x4, blocking collectives, swap(): return lax.all_to_all(parts, axis, 0, 0)  79.4 us
    all_to_all x2, waiting for transfers between devices, swap(): return lax.all_to_all(parts, axis, 0, 0)  21.3 us
    all_to_all x2, starting transfers between devices, swap(): return lax.all_to_all(parts, axis, 0, 0)  18.4 us
  transfers between devices with their start and end apart: 3, of which 3 were waited for; matrix products, arithmetic and copies ran while one was open for 3% of the time, Pallas kernels for 2%

profile of v7, /device:TPU:2, one launch (start us, length us, event | category | flops | bytes accessed | tf_op | source)
XLA Modules:
  0.0 150.3 jit_solution(6555096370225149204)
XLA Ops:
  7.2 1.2 copy-done
  8.4 2.8 %convolution_convert_fusion.1 = bf16[1024,512]{1,0:T(8,128)(2,1)} fusion(bf16[1024,512]{1,0:T(8,128)(2,1)S(1)} %copy-done, bf16[512,512]{1,0:T(8,128)(2,1)} %param.7), kind=kOutput, calls=%fused_computation.1 | convolution fusion | flops 537395200 | bytes 2621440 | tf_op jit(solution)/shard_map/dot_general | solution.py:110
  11.1 13.3 %all-to-all-start = ((bf16[16,64,512]{2,1,0:T(8,128)(2,1)}), bf16[16,64,512]{2,1,0:T(8,128)(2,1)}, u32[]{:S(2)}, u32[]{:S(2)}) async-start(bf16[16,64,512]{2,1,0:T(8,128)(2,1)} %bitcast.1), calls=%async_computation | async-start | bytes 2097152 | tf_op jit(solution)/shard_map/all_to_all | solution.py:14
  24.5 0.0 all-gather.2.cloned.1.call-start
  24.5 1.4 constant_dynamic-slice_fusion
  25.9 0.0 all-gather.2.cloned.1.call-update
  25.9 1.6 %copy-done.1 = bf16[1024,1024]{1,0:T(8,128)(2,1)S(1)} copy-done((bf16[1024,1024]{1,0:T(8,128)(2,1)S(1)}, bf16[1024,1024]{1,0:T(8,128)(2,1)}, u32[]{:S(2)}) %copy-start.1) | copy-done | bytes 2097176
  27.5 1.7 %shard_map.76 = bf16[2,16,32,1024]{3,2,1,0:T(8,128)(2,1)S(1)} custom-call(bf16[1024,1024]{1,0:T(8,128)(2,1)S(1)} %copy-done.1), custom_call_target="tpu_custom_call" | custom-call | bytes 4194304 | tf_op jit(solution)/shard_map/pallas_call | solution.py:45
  29.2 17.2 %all-to-all-done = bf16[16,64,512]{2,1,0:T(8,128)(2,1)} async-done(((bf16[16,64,512]{2,1,0:T(8,128)(2,1)}), bf16[16,64,512]{2,1,0:T(8,128)(2,1)}, u32[]{:S(2)}, u32[]{:S(2)}) %all-to-all-start) | async-done | bytes 1048608 | tf_op jit(solution)/shard_map/all_to_all | solution.py:14
  46.4 1.4 fusion
  47.8 0.1 broadcast_in_dim.4
  47.9 28.5 %all_to_all.30 = bf16[16,64,512]{2,1,0:T(8,128)(2,1)S(1)} all-to-all(bf16[16,64,512]{2,1,0:T(8,128)(2,1)S(1)} %broadcast_in_dim.4), channel_id=1, replica_groups=mesh['zh'=4,'x'=4,'y'=8,'zl'=2,'c'=2] {'zh','x'}, dimensions={0} | all-to-all | bytes 2097152 | tf_op jit(solution)/shard_map/all_to_all | solution.py:14
  76.4 1.7 %shard_map.77 = bf16[1024,512]{1,0:T(8,128)(2,1)S(1)} custom-call(bf16[1024,1024]{1,0:T(8,128)(2,1)S(1)} %bitcast.25, bf16[1024,512]{1,0:T(8,128)(2,1)S(1)} %bitcast.26), custom_call_target="tpu_custom_call" | custom-call | flops 1073741824 | bytes 4194304 | tf_op jit(solution)/shard_map/pallas_call | solution.py:69
  78.2 4.7 %all_to_all.31 = bf16[2,512,512]{2,1,0:T(8,128)(2,1)S(1)} all-to-all(bf16[2,512,512]{2,1,0:T(8,128)(2,1)S(1)} %bitcast.27), channel_id=1, replica_groups=mesh['zh'=4,'x'=4,'y'=8,'zl'=2,'c'=2] {'c'}, dimensions={0} | all-to-all | bytes 2097152 | tf_op jit(solution)/shard_map/all_to_all | solution.py:14
  82.9 0.1 add_convert_fusion
  83.0 35.7 %all_to_all.32 = bf16[16,32,512]{2,1,0:T(8,128)(2,1)S(1)} all-to-all(bf16[16,32,512]{2,1,0:T(8,128)(2,1)S(1)} %bitcast.28), channel_id=1, replica_groups=mesh['zh'=4,'x'=4,'y'=8,'zl'=2,'c'=2] {'y','zl'}, dimensions={0} | all-to-all | bytes 1048576 | tf_op jit(solution)/shard_map/all_to_all | solution.py:14
  118.7 0.8 divide_convert_fusion
  119.5 0.7 broadcast_in_dim.5
  120.1 5.1 %all-to-all-start.4 = ((bf16[4,32,512]{2,1,0:T(8,128)(2,1)}), bf16[4,32,512]{2,1,0:T(8,128)(2,1)S(1)}, u32[]{:S(2)}, u32[]{:S(2)}) async-start(bf16[4,32,512]{2,1,0:T(8,128)(2,1)} %broadcast_in_dim.5), calls=%async_computation.4 | async-start | bytes 262144 | tf_op jit(solution)/shard_map/all_to_all | solution.py:14
  125.2 0.4 all-gather.2.cloned.1.call-done
  125.6 4.1 %all-to-all-done.4 = bf16[4,32,512]{2,1,0:T(8,128)(2,1)S(1)} async-done(((bf16[4,32,512]{2,1,0:T(8,128)(2,1)}), bf16[4,32,512]{2,1,0:T(8,128)(2,1)S(1)}, u32[]{:S(2)}, u32[]{:S(2)}) %all-to-all-start.4) | async-done | bytes 131104 | tf_op jit(solution)/shard_map/all_to_all | solution.py:14
  129.7 2.4 %convolution_convert_fusion = bf16[128,2048]{1,0:T(8,128)(2,1)S(1)} fusion(bf16[128,512]{1,0:T(8,128)(2,1)S(1)} %bitcast.30, bf16[2048,512]{1,0:T(8,128)(2,1)} %all-gather.2.cloned.1.call-done), kind=kOutput, calls=%fused_computation | convolution fusion | flops 268697600 | bytes 2752512 | tf_op jit(solution)/shard_map/dot_general | solution.py:125
  132.1 10.5 %all_to_all.33.in_ref = bf16[4,32,2048]{2,1,0:T(8,128)(2,1)S(1)} all-to-all(bf16[4,32,2048]{2,1,0:T(8,128)(2,1)S(1)} %bitcast.29), channel_id=1, replica_groups=mesh['zh'=4,'x'=4,'y'=8,'zl'=2,'c'=2] {'x'}, dimensions={0} | all-to-all | bytes 1048576 | tf_op jit(solution)/shard_map/all_to_all | solution.py:14
  142.6 0.8 shard_map.78
  (6 shorter events, 0.0 us)
Async XLA Ops:
  7.2 1.2 copy-start
  11.1 35.2 %all-to-all-start = ((bf16[16,64,512]{2,1,0:T(8,128)(2,1)}), bf16[16,64,512]{2,1,0:T(8,128)(2,1)}, u32[]{:S(2)}, u32[]{:S(2)}) async-start(bf16[16,64,512]{2,1,0:T(8,128)(2,1)} %bitcast.1), calls=%async_computation | async-start | bytes 2097152 | tf_op jit(solution)/shard_map/all_to_all | solution.py:14
  24.5 101.1 %all-gather.2.cloned.1.call-start = ((), (), s32[]{:S(2)}) async-start(), calls=%async_computation.6 | async-start | bytes 2129920 | tf_op jit(solution)/shard_map/all_gather | solution.py:108
  25.9 1.6 %copy-start.1 = (bf16[1024,1024]{1,0:T(8,128)(2,1)S(1)}, bf16[1024,1024]{1,0:T(8,128)(2,1)}, u32[]{:S(2)}) copy-start(bf16[1024,1024]{1,0:T(8,128)(2,1)} %in_ref.1) | copy-start | bytes 6291460
  78.2 40.5 %copy-start.2 = (f32[32,512]{1,0:T(8,128)S(1)}, f32[32,512]{1,0:T(8,128)}, u32[]{:S(2)}) copy-start(f32[32,512]{1,0:T(8,128)} %param.8) | copy-start | bytes 196612
  78.2 40.5 %copy-start.3 = (f32[32,512]{1,0:T(8,128)S(1)}, f32[32,512]{1,0:T(8,128)}, u32[]{:S(2)}) copy-start(f32[32,512]{1,0:T(8,128)} %param.9) | copy-start | bytes 196612
  120.1 9.6 %all-to-all-start.4 = ((bf16[4,32,512]{2,1,0:T(8,128)(2,1)}), bf16[4,32,512]{2,1,0:T(8,128)(2,1)S(1)}, u32[]{:S(2)}, u32[]{:S(2)}) async-start(bf16[4,32,512]{2,1,0:T(8,128)(2,1)} %broadcast_in_dim.5), calls=%async_computation.4 | async-start | bytes 262144 | tf_op jit(solution)/shard_map/all_to_all | solution.py:14
Sparse Core Ops, SparseCore 0:
  28.6 96.8 all-gather.1

commit v8 on v5

--- a/solution.py
+++ b/solution.py
@@ -133,24 +133,19 @@
     r = projector.shape[1]
     z, core = lax.axis_index("zh"), lax.axis_index("c")
     tt = turn(tangent)
+    part = jnp.dot(tokens, projector, preferred_element_type=F32).astype(BF16)
+    part = scattered_sum(part, ("zh", "x"), 16).astype(BF16)
+    tt, part = lax.optimization_barrier((tt, part))
+    reduced = spread(part, ("zh", "x"), 16).reshape(-1, r)
+    grad = product(tt, reduced)
+    grad = scattered_sum(grad, "c", 2).astype(BF16)
     half = projector.shape[0] // 2
     share = lax.dynamic_slice_in_dim(projector, core * half, half, 0)
-    one, three = back(share, "zh", 4, 1), back(share, "zh", 4, 3)
-    part = jnp.dot(tokens, projector, preferred_element_type=F32).astype(BF16)
-    part = scattered_sum(part, "x", 4).astype(BF16)
-    one, three, tt, part = lax.optimization_barrier((one, three, tt, part))
-    part = scattered_sum(part, "zh", 4).astype(BF16)
-    part = spread(part, "zh", 4).reshape(-1, r)
-    share, part = lax.optimization_barrier((share, part))
-    two = back(share, "zh", 4, 2)
-    reduced = spread(part, "x", 4).reshape(-1, r)
-    two, reduced = lax.optimization_barrier((two, reduced))
-    grad = product(tt, reduced)
-    grad = scattered_sum(grad, "c", 2).astype(BF16)
-    one, two, three, grad = lax.optimization_barrier((one, two, three, grad))
-    mine = jnp.stack([one, two, three])
+    share, grad = lax.optimization_barrier((share, grad))
+    mine = jnp.stack([back(share, "zh", 4, k) for k in (1, 2, 3)])
+    gradient = scattered_sum(grad, ("y", "zl"), 16)
+    mine, gradient = lax.optimization_barrier((mine, gradient))
     other = lax.ppermute(mine, "c", [(0, 1), (1, 0)])
-    gradient = scattered_sum(grad, ("y", "zl"), 16)
     wide = weave(jnp.stack([z, core]).astype(jnp.int32), projector, mine, other)
 
     new_first = 0.9 * first_moment + 0.1 * gradient

time: 144 us -> 161 us (1.12)
  the two profiles are of different devices: /device:TPU:2 before, /device:TPU:1 now
where the time goes in v8:
time: 161 us; the launch traced here: 160 us
  waiting for transfers between devices  60.9 us (38%)
  starting transfers between devices  50.8 us (32%)
  blocking collectives  25 us (16%)
  local copies, waits for them, and re-layouts  9.76 us (6%)
  Pallas kernels  6.19 us (4%)
  matrix products  3.53 us (2%)
  other arithmetic  3.23 us (2%)
    all_to_all x4, starting transfers between devices, swap(): return lax.all_to_all(parts, axis, 0, 0)  38.3 us
    all_to_all x4, waiting for transfers between devices, swap(): return lax.all_to_all(parts, axis, 0, 0)  34.2 us
    ppermute x3, waiting for transfers between devices, back(): return lax.ppermute(block, axis, [(i, (i + k) % n) for i in range(n)])  26.7 us
    all_to_all x2, blocking collectives, swap(): return lax.all_to_all(parts, axis, 0, 0)  25 us
    ppermute x3, starting transfers between devices, back(): return lax.ppermute(block, axis, [(i, (i + k) % n) for i in range(n)])  9.69 us
    unnamed x18, local copies, waits for them, and re-layouts  7.04 us
  transfers between devices with their start and end apart: 8, of which 5 were waited for; matrix products, arithmetic and copies ran while one was open for 2% of the time, Pallas kernels for 1%

profile of v8, /device:TPU:1, one launch (start us, length us, event | category | flops | bytes accessed | tf_op | source)
XLA Modules:
  0.0 160.2 jit_solution(16576340841369247268)
XLA Ops:
  0.6 1.2 copy-done
  1.9 2.7 %convolution_convert_fusion.1 = bf16[1024,512]{1,0:T(8,128)(2,1)} fusion(bf16[1024,512]{1,0:T(8,128)(2,1)S(1)} %copy-done, bf16[512,512]{1,0:T(8,128)(2,1)} %own_ref.1), kind=kOutput, calls=%fused_computation.1 | convolution fusion | flops 537395200 | bytes 2621440 | tf_op jit(solution)/shard_map/dot_general | solution.py:136
  4.6 13.5 %all-to-all-start = ((bf16[16,64,512]{2,1,0:T(8,128)(2,1)}), bf16[16,64,512]{2,1,0:T(8,128)(2,1)}, u32[]{:S(2)}, u32[]{:S(2)}) async-start(bf16[16,64,512]{2,1,0:T(8,128)(2,1)} %bitcast.1), calls=%async_computation | async-start | bytes 2097152 | tf_op jit(solution)/shard_map/all_to_all | solution.py:14
  18.1 1.6 copy-done.3
  19.7 1.7 %shard_map.76 = bf16[2,16,32,1024]{3,2,1,0:T(8,128)(2,1)S(1)} custom-call(bf16[1024,1024]{1,0:T(8,128)(2,1)S(1)} %copy-done.3), custom_call_target="tpu_custom_call" | custom-call | bytes 4194304 | tf_op jit(solution)/shard_map/pallas_call | solution.py:49
  21.4 18.5 %all-to-all-done = bf16[16,64,512]{2,1,0:T(8,128)(2,1)} async-done(((bf16[16,64,512]{2,1,0:T(8,128)(2,1)}), bf16[16,64,512]{2,1,0:T(8,128)(2,1)}, u32[]{:S(2)}, u32[]{:S(2)}) %all-to-all-start) | async-done | bytes 1048608 | tf_op jit(solution)/shard_map/all_to_all | solution.py:14
  39.9 1.4 fusion.1
  41.3 1.1 broadcast_in_dim.4
  42.3 6.0 %all-to-all-start.1 = ((bf16[16,64,512]{2,1,0:T(8,128)(2,1)}), bf16[16,64,512]{2,1,0:T(8,128)(2,1)}, u32[]{:S(2)}, u32[]{:S(2)}) async-start(bf16[16,64,512]{2,1,0:T(8,128)(2,1)} %broadcast_in_dim.4), calls=%async_computation.1 | async-start | bytes 2097152 | tf_op jit(solution)/shard_map/all_to_all | solution.py:14
  49.3 15.6 %all-to-all-done.1 = bf16[16,64,512]{2,1,0:T(8,128)(2,1)} async-done(((bf16[16,64,512]{2,1,0:T(8,128)(2,1)}), bf16[16,64,512]{2,1,0:T(8,128)(2,1)}, u32[]{:S(2)}, u32[]{:S(2)}) %all-to-all-start.1) | async-done | bytes 1048608 | tf_op jit(solution)/shard_map/all_to_all | solution.py:14
  65.0 3.0 %shard_map.77 = bf16[1024,512]{1,0:T(8,128)(2,1)S(1)} custom-call(bf16[1024,1024]{1,0:T(8,128)(2,1)S(1)} %bitcast.33, bf16[1024,512]{1,0:T(8,128)(2,1)} %bitcast.4.b_ref), custom_call_target="tpu_custom_call" | custom-call | flops 1073741824 | bytes 4194304 | tf_op jit(solution)/shard_map/pallas_call | solution.py:73
  67.9 12.5 %all_to_all.30 = bf16[2,512,512]{2,1,0:T(8,128)(2,1)S(1)} all-to-all(bf16[2,512,512]{2,1,0:T(8,128)(2,1)S(1)} %bitcast.35), channel_id=1, replica_groups=mesh['zh'=4,'x'=4,'y'=8,'zl'=2,'c'=2] {'c'}, dimensions={0} | all-to-all | bytes 2097152 | tf_op jit(solution)/shard_map/all_to_all | solution.py:14
  81.4 15.5 %all-to-all-start.3 = ((bf16[16,32,512]{2,1,0:T(8,128)(2,1)}), bf16[16,32,512]{2,1,0:T(8,128)(2,1)S(1)}, u32[]{:S(2)}, u32[]{:S(2)}) async-start(bf16[16,32,512]{2,1,0:T(8,128)(2,1)} %bitcast.10), calls=%async_computation.3 | async-start | bytes 1048576 | tf_op jit(solution)/shard_map/all_to_all | solution.py:14
  96.9 3.3 %collective-permute-start.2 = (bf16[256,512]{1,0:T(8,128)(2,1)S(1)}, bf16[256,512]{1,0:T(8,128)(2,1)S(1)}, u32[]{:S(2)}, u32[]{:S(2)}) collective-permute-start(bf16[256,512]{1,0:T(8,128)(2,1)S(1)} %constant_dynamic-slice_fusion), channel_id=1, source_target_pairs={{0,384},{128,0},{256,128},{384,256},{1,385},{129,1},{257,129},{385... | collective-permute-start | bytes 786440 | tf_op jit(solution)/shard_map/ppermute | solution.py:33
  100.1 4.5 %collective-permute-start.1 = (bf16[256,512]{1,0:T(8,128)(2,1)S(1)}, bf16[256,512]{1,0:T(8,128)(2,1)S(1)}, u32[]{:S(2)}, u32[]{:S(2)}) collective-permute-start(bf16[256,512]{1,0:T(8,128)(2,1)S(1)} %constant_dynamic-slice_fusion), channel_id=1, source_target_pairs={{0,256},{128,384},{256,0},{384,128},{1,257},{129,385},{257,1},{385... | collective-permute-start | bytes 786440 | tf_op jit(solution)/shard_map/ppermute | solution.py:33
  104.7 1.9 %collective-permute-start = (bf16[256,512]{1,0:T(8,128)(2,1)S(1)}, bf16[256,512]{1,0:T(8,128)(2,1)S(1)}, u32[]{:S(2)}, u32[]{:S(2)}) collective-permute-start(bf16[256,512]{1,0:T(8,128)(2,1)S(1)} %constant_dynamic-slice_fusion), channel_id=1, source_target_pairs={{0,128},{128,256},{256,384},{384,0},{1,129},{129,257},{257,385},{3... | collective-permute-start | bytes 786440 | tf_op jit(solution)/shard_map/ppermute | solution.py:33
  106.6 2.6 %collective-permute-done.2 = bf16[256,512]{1,0:T(8,128)(2,1)S(1)} collective-permute-done((bf16[256,512]{1,0:T(8,128)(2,1)S(1)}, bf16[256,512]{1,0:T(8,128)(2,1)S(1)}, u32[]{:S(2)}, u32[]{:S(2)}) %collective-permute-start.2) | collective-permute-done | bytes 262176 | tf_op jit(solution)/shard_map/ppermute | solution.py:33
  109.2 18.4 %collective-permute-done.1 = bf16[256,512]{1,0:T(8,128)(2,1)S(1)} collective-permute-done((bf16[256,512]{1,0:T(8,128)(2,1)S(1)}, bf16[256,512]{1,0:T(8,128)(2,1)S(1)}, u32[]{:S(2)}, u32[]{:S(2)}) %collective-permute-start.1) | collective-permute-done | bytes 262176 | tf_op jit(solution)/shard_map/ppermute | solution.py:33
  127.5 5.7 %collective-permute-done = bf16[256,512]{1,0:T(8,128)(2,1)S(1)} collective-permute-done((bf16[256,512]{1,0:T(8,128)(2,1)S(1)}, bf16[256,512]{1,0:T(8,128)(2,1)S(1)}, u32[]{:S(2)}, u32[]{:S(2)}) %collective-permute-start) | collective-permute-done | bytes 262176 | tf_op jit(solution)/shard_map/ppermute | solution.py:33
  133.5 2.8 %collective-permute-start.3 = (bf16[3,256,512]{2,1,0:T(8,128)(2,1)S(1)}, bf16[3,256,512]{2,1,0:T(8,128)(2,1)S(1)}, u32[]{:S(2)}, u32[]{:S(2)}) collective-permute-start(bf16[3,256,512]{2,1,0:T(8,128)(2,1)S(1)} %pad_maximum_fusion.mine_ref), channel_id=1, source_target_pairs={{0,1},{1,0},{2,3},{3,2},{4,5},{5,4},{6,7},{7,6},{8,9},{9,8},{10,11... | collective-permute-start | bytes 2359304 | tf_op jit(solution)/shard_map/ppermute | solution.py:148
  137.6 3.3 %all-to-all-start.4 = ((bf16[4,32,512]{2,1,0:T(8,128)(2,1)}), bf16[4,32,512]{2,1,0:T(8,128)(2,1)S(1)}, u32[]{:S(2)}, u32[]{:S(2)}) async-start(bf16[4,32,512]{2,1,0:T(8,128)(2,1)} %broadcast_in_dim.5), calls=%async_computation.4 | async-start | bytes 262144 | tf_op jit(solution)/shard_map/all_to_all | solution.py:14
  142.0 1.1 copy-done.2
  144.2 1.1 copy-done.6
  146.8 12.5 %all_to_all.31.in_ref = bf16[4,32,2048]{2,1,0:T(8,128)(2,1)S(1)} all-to-all(bf16[4,32,2048]{2,1,0:T(8,128)(2,1)S(1)} %bitcast.36), channel_id=1, replica_groups=mesh['zh'=4,'x'=4,'y'=8,'zl'=2,'c'=2] {'x'}, dimensions={0} | all-to-all | bytes 1048576 | tf_op jit(solution)/shard_map/all_to_all | solution.py:14
  (27 shorter events, 7.8 us)
Async XLA Ops:
  0.6 1.2 copy-start
  4.6 35.3 %all-to-all-start = ((bf16[16,64,512]{2,1,0:T(8,128)(2,1)}), bf16[16,64,512]{2,1,0:T(8,128)(2,1)}, u32[]{:S(2)}, u32[]{:S(2)}) async-start(bf16[16,64,512]{2,1,0:T(8,128)(2,1)} %bitcast.1), calls=%async_computation | async-start | bytes 2097152 | tf_op jit(solution)/shard_map/all_to_all | solution.py:14
  18.1 1.6 copy-start.3
  42.3 22.6 %all-to-all-start.1 = ((bf16[16,64,512]{2,1,0:T(8,128)(2,1)}), bf16[16,64,512]{2,1,0:T(8,128)(2,1)}, u32[]{:S(2)}, u32[]{:S(2)}) async-start(bf16[16,64,512]{2,1,0:T(8,128)(2,1)} %broadcast_in_dim.4), calls=%async_computation.1 | async-start | bytes 2097152 | tf_op jit(solution)/shard_map/all_to_all | solution.py:14
  80.4 55.8 %copy-start.7 = (f32[32,512]{1,0:T(8,128)S(1)}, f32[32,512]{1,0:T(8,128)}, u32[]{:S(2)}) copy-start(f32[32,512]{1,0:T(8,128)} %param.8) | copy-start | bytes 196612
  80.4 55.9 %copy-start.8 = (f32[32,512]{1,0:T(8,128)S(1)}, f32[32,512]{1,0:T(8,128)}, u32[]{:S(2)}) copy-start(f32[32,512]{1,0:T(8,128)} %param.9) | copy-start | bytes 196612
  81.4 52.0 %all-to-all-start.3 = ((bf16[16,32,512]{2,1,0:T(8,128)(2,1)}), bf16[16,32,512]{2,1,0:T(8,128)(2,1)S(1)}, u32[]{:S(2)}, u32[]{:S(2)}) async-start(bf16[16,32,512]{2,1,0:T(8,128)(2,1)} %bitcast.10), calls=%async_computation.3 | async-start | bytes 1048576 | tf_op jit(solution)/shard_map/all_to_all | solution.py:14
  96.9 12.3 %collective-permute-start.2 = (bf16[256,512]{1,0:T(8,128)(2,1)S(1)}, bf16[256,512]{1,0:T(8,128)(2,1)S(1)}, u32[]{:S(2)}, u32[]{:S(2)}) collective-permute-start(bf16[256,512]{1,0:T(8,128)(2,1)S(1)} %constant_dynamic-slice_fusion), channel_id=1, source_target_pairs={{0,384},{128,0},{256,128},{384,256},{1,385},{129,1},{257,129},{385... | collective-permute-start | bytes 786440 | tf_op jit(solution)/shard_map/ppermute | solution.py:33
  100.1 27.4 %collective-permute-start.1 = (bf16[256,512]{1,0:T(8,128)(2,1)S(1)}, bf16[256,512]{1,0:T(8,128)(2,1)S(1)}, u32[]{:S(2)}, u32[]{:S(2)}) collective-permute-start(bf16[256,512]{1,0:T(8,128)(2,1)S(1)} %constant_dynamic-slice_fusion), channel_id=1, source_target_pairs={{0,256},{128,384},{256,0},{384,128},{1,257},{129,385},{257,1},{385... | collective-permute-start | bytes 786440 | tf_op jit(solution)/shard_map/ppermute | solution.py:33
  104.7 28.6 %collective-permute-start = (bf16[256,512]{1,0:T(8,128)(2,1)S(1)}, bf16[256,512]{1,0:T(8,128)(2,1)S(1)}, u32[]{:S(2)}, u32[]{:S(2)}) collective-permute-start(bf16[256,512]{1,0:T(8,128)(2,1)S(1)} %constant_dynamic-slice_fusion), channel_id=1, source_target_pairs={{0,128},{128,256},{256,384},{384,0},{1,129},{129,257},{257,385},{3... | collective-permute-start | bytes 786440 | tf_op jit(solution)/shard_map/ppermute | solution.py:33
  133.4 7.7 %copy-start.1 = (bf16[3,256,512]{2,1,0:T(8,128)(2,1)}, bf16[3,256,512]{2,1,0:T(8,128)(2,1)S(1)}, u32[]{:S(2)}) copy-start(bf16[3,256,512]{2,1,0:T(8,128)(2,1)S(1)} %pad_maximum_fusion.mine_ref) | copy-start | bytes 2359300
  133.5 7.6 %collective-permute-start.3 = (bf16[3,256,512]{2,1,0:T(8,128)(2,1)S(1)}, bf16[3,256,512]{2,1,0:T(8,128)(2,1)S(1)}, u32[]{:S(2)}, u32[]{:S(2)}) collective-permute-start(bf16[3,256,512]{2,1,0:T(8,128)(2,1)S(1)} %pad_maximum_fusion.mine_ref), channel_id=1, source_target_pairs={{0,1},{1,0},{2,3},{3,2},{4,5},{5,4},{6,7},{7,6},{8,9},{9,8},{10,11... | collective-permute-start | bytes 2359304 | tf_op jit(solution)/shard_map/ppermute | solution.py:148
  137.6 8.3 %all-to-all-start.4 = ((bf16[4,32,512]{2,1,0:T(8,128)(2,1)}), bf16[4,32,512]{2,1,0:T(8,128)(2,1)S(1)}, u32[]{:S(2)}, u32[]{:S(2)}) async-start(bf16[4,32,512]{2,1,0:T(8,128)(2,1)} %broadcast_in_dim.5), calls=%async_computation.4 | async-start | bytes 262144 | tf_op jit(solution)/shard_map/all_to_all | solution.py:14
  141.1 0.9 copy-start.5
  142.0 1.1 copy-start.2
  143.1 1.0 copy-start.4
  144.2 1.1 copy-start.6

commit v9 on v7

--- a/solution.py
+++ b/solution.py
@@ -79,12 +79,9 @@
 
 
 def lay_kernel(in_ref, out_ref):
-    n = in_ref.shape[0]
-    width = in_ref.shape[2] // n
-    for z in range(n):
-        for x in range(n):
-            at = (z * n + x) * width
-            out_ref[:, at : at + width] = in_ref[x, :, z * width : (z + 1) * width]
+    width = in_ref.shape[2]
+    for i in range(in_ref.shape[0]):
+        out_ref[:, i * width : (i + 1) * width] = in_ref[i]
 
 
 def lay(blocks):
@@ -102,15 +99,13 @@
 
 def local(tokens, tangent, projector, first_moment, second_moment):
     r = projector.shape[1]
-    share = projector.shape[0] // 16
-    at = (lax.axis_index("y") * 2 + lax.axis_index("c")) * share
-    piece = lax.dynamic_slice_in_dim(projector, at, share, 0)
-    wide = lax.all_gather(piece, ("zh", "y", "c"), axis=0, tiled=True)
     tt = turn(tangent)
     part = jnp.dot(tokens, projector, preferred_element_type=F32).astype(BF16)
-    part = scattered_sum(part, ("zh", "x"), 16).astype(BF16)
+    part = scattered_sum(part, "x", 4).astype(BF16)
     tt, part = lax.optimization_barrier((tt, part))
-    reduced = spread(part, ("zh", "x"), 16).reshape(-1, r)
+    part = scattered_sum(part, "zh", 4).astype(BF16)
+    part = spread(part, "zh", 4).reshape(-1, r)
+    reduced = spread(part, "x", 4).reshape(-1, r)
     grad = product(tt, reduced)
     grad = scattered_sum(grad, "c", 2).astype(BF16)
     gradient = scattered_sum(grad, ("y", "zl"), 16)
@@ -121,11 +116,11 @@
     second_fix = 1.0 - 0.999**STEP
     direction = (new_first / first_fix / (jnp.sqrt(new_second / second_fix) + 1e-08)).astype(BF16)
     rows = direction.shape[0]
-    directions = spread(direction, "x", 4).reshape(-1, r)
+    directions = spread(direction, ("zh", "x"), 16).reshape(-1, r)
     out = lax.dot_general(
-        directions, wide, (((1,), (1,)), ((), ())), preferred_element_type=F32
+        directions, projector, (((1,), (1,)), ((), ())), preferred_element_type=F32
     ).astype(BF16)
-    out = lay(swap(out.reshape(4, rows, -1), "x"))
+    out = lay(swap(out.reshape(16, rows, -1), ("zh", "x")))
     return (out, new_first, new_second)
 
 

time: 151 us -> 149 us (0.987)
  the two profiles are of different devices: /device:TPU:2 before, /device:TPU:24 now
where the time goes in v9:
time: 149 us; the launch traced here: 148 us
  blocking collectives  118 us (79%)
  waiting for transfers between devices  12.1 us (8%)
  starting transfers between devices  4.3 us (3%)
  Pallas kernels  4.29 us (3%)
  matrix products  3.24 us (2%)
  local copies, waits for them, and re-layouts  2.97 us (2%)
  other arithmetic  2.25 us (2%)
    all_to_all x7, blocking collectives, swap(): return lax.all_to_all(parts, axis, 0, 0)  118 us
    all_to_all x1, waiting for transfers between devices, swap(): return lax.all_to_all(parts, axis, 0, 0)  12.1 us
    all_to_all x1, starting transfers between devices, swap(): return lax.all_to_all(parts, axis, 0, 0)  4.3 us
  transfers between devices with their start and end apart: 1, of which 1 were waited for; matrix products, arithmetic and copies ran while one was open for 0% of the time, Pallas kernels for 1%

profile of v9, /device:TPU:24, one launch (start us, length us, event | category | flops | bytes accessed | tf_op | source)
XLA Modules:
  0.0 148.0 jit_solution(11570490657478457056)
XLA Ops:
  0.6 0.0 copy-start
  0.6 1.2 copy-done
  1.9 2.8 %convolution_convert_fusion = bf16[1024,512]{1,0:T(8,128)(2,1)} fusion(bf16[1024,512]{1,0:T(8,128)(2,1)S(1)} %copy-done, bf16[512,512]{1,0:T(8,128)(2,1)} %param.7), kind=kOutput, calls=%fused_computation | convolution fusion | flops 537395200 | bytes 2621440 | tf_op jit(solution)/shard_map/dot_general | solution.py:103
  4.6 4.3 %all-to-all-start = ((bf16[4,256,512]{2,1,0:T(8,128)(2,1)}), bf16[4,256,512]{2,1,0:T(8,128)(2,1)}, u32[]{:S(2)}, u32[]{:S(2)}) async-start(bf16[4,256,512]{2,1,0:T(8,128)(2,1)} %bitcast.1), calls=%async_computation | async-start | bytes 2097152 | tf_op jit(solution)/shard_map/all_to_all | solution.py:14
  8.9 1.6 %copy-done.1 = bf16[1024,1024]{1,0:T(8,128)(2,1)S(1)} copy-done((bf16[1024,1024]{1,0:T(8,128)(2,1)S(1)}, bf16[1024,1024]{1,0:T(8,128)(2,1)}, u32[]{:S(2)}) %copy-start.1) | copy-done | bytes 2097176
  10.5 1.7 %shard_map.76 = bf16[2,16,32,1024]{3,2,1,0:T(8,128)(2,1)S(1)} custom-call(bf16[1024,1024]{1,0:T(8,128)(2,1)S(1)} %copy-done.1), custom_call_target="tpu_custom_call" | custom-call | bytes 4194304 | tf_op jit(solution)/shard_map/pallas_call | solution.py:45
  12.3 12.1 %all-to-all-done = bf16[4,256,512]{2,1,0:T(8,128)(2,1)} async-done(((bf16[4,256,512]{2,1,0:T(8,128)(2,1)}), bf16[4,256,512]{2,1,0:T(8,128)(2,1)}, u32[]{:S(2)}, u32[]{:S(2)}) %all-to-all-start) | async-done | bytes 1048608 | tf_op jit(solution)/shard_map/all_to_all | solution.py:14
  24.3 1.3 fusion
  25.6 20.6 %all_to_all.40 = bf16[4,64,512]{2,1,0:T(8,128)(2,1)S(1)} all-to-all(bf16[4,64,512]{2,1,0:T(8,128)(2,1)S(1)} %bitcast.30), channel_id=1, replica_groups=mesh['zh'=4,'x'=4,'y'=8,'zl'=2,'c'=2] {'zh'}, dimensions={0} | all-to-all | bytes 524288 | tf_op jit(solution)/shard_map/all_to_all | solution.py:14
  46.3 12.5 %all_to_all.41 = bf16[4,64,512]{2,1,0:T(8,128)(2,1)S(1)} all-to-all(bf16[4,64,512]{2,1,0:T(8,128)(2,1)S(1)} %broadcast_in_dim.22), channel_id=1, replica_groups=mesh['zh'=4,'x'=4,'y'=8,'zl'=2,'c'=2] {'zh'}, dimensions={0} | all-to-all | bytes 524288 | tf_op jit(solution)/shard_map/all_to_all | solution.py:14
  58.8 0.1 broadcast_in_dim.24
  58.9 14.8 %all_to_all.42 = bf16[4,256,512]{2,1,0:T(8,128)(2,1)S(1)} all-to-all(bf16[4,256,512]{2,1,0:T(8,128)(2,1)S(1)} %broadcast_in_dim.24), channel_id=1, replica_groups=mesh['zh'=4,'x'=4,'y'=8,'zl'=2,'c'=2] {'x'}, dimensions={0} | all-to-all | bytes 2097152 | tf_op jit(solution)/shard_map/all_to_all | solution.py:14
  73.7 1.7 %shard_map.77 = bf16[1024,512]{1,0:T(8,128)(2,1)S(1)} custom-call(bf16[1024,1024]{1,0:T(8,128)(2,1)S(1)} %bitcast.24, bf16[1024,512]{1,0:T(8,128)(2,1)S(1)} %bitcast.25), custom_call_target="tpu_custom_call" | custom-call | flops 1073741824 | bytes 4194304 | tf_op jit(solution)/shard_map/pallas_call | solution.py:69
  75.5 0.0 copy-start.3
  75.5 0.0 copy-start.4
  75.5 4.7 %all_to_all.43 = bf16[2,512,512]{2,1,0:T(8,128)(2,1)S(1)} all-to-all(bf16[2,512,512]{2,1,0:T(8,128)(2,1)S(1)} %bitcast.26), channel_id=1, replica_groups=mesh['zh'=4,'x'=4,'y'=8,'zl'=2,'c'=2] {'c'}, dimensions={0} | all-to-all | bytes 2097152 | tf_op jit(solution)/shard_map/all_to_all | solution.py:14
  80.2 0.1 add_convert_fusion
  80.3 0.0 copy-start.2
  80.4 23.1 %all_to_all.44 = bf16[16,32,512]{2,1,0:T(8,128)(2,1)S(1)} all-to-all(bf16[16,32,512]{2,1,0:T(8,128)(2,1)S(1)} %bitcast.27), channel_id=1, replica_groups=mesh['zh'=4,'x'=4,'y'=8,'zl'=2,'c'=2] {'y','zl'}, dimensions={0} | all-to-all | bytes 1048576 | tf_op jit(solution)/shard_map/all_to_all | solution.py:14
  103.4 0.8 divide_convert_fusion
  104.3 21.2 %all_to_all.45 = bf16[16,32,512]{2,1,0:T(8,128)(2,1)S(1)} all-to-all(bf16[16,32,512]{2,1,0:T(8,128)(2,1)S(1)} %broadcast_in_dim.25), channel_id=1, replica_groups=mesh['zh'=4,'x'=4,'y'=8,'zl'=2,'c'=2] {'zh','x'}, dimensions={0} | all-to-all | bytes 1048576 | tf_op jit(solution)/shard_map/all_to_all | solution.py:14
  125.5 0.5 convolution_convert_fusion.1
  126.0 21.2 %all_to_all.46.in_ref = bf16[16,32,512]{2,1,0:T(8,128)(2,1)S(1)} all-to-all(bf16[16,32,512]{2,1,0:T(8,128)(2,1)S(1)} %bitcast.29), channel_id=1, replica_groups=mesh['zh'=4,'x'=4,'y'=8,'zl'=2,'c'=2] {'zh','x'}, dimensions={0} | all-to-all | bytes 1048576 | tf_op jit(solution)/shard_map/all_to_all | solution.py:14
  147.2 0.8 shard_map.78
  (7 shorter events, 0.1 us)
Async XLA Ops:
  0.6 1.2 copy-start
  4.6 19.7 %all-to-all-start = ((bf16[4,256,512]{2,1,0:T(8,128)(2,1)}), bf16[4,256,512]{2,1,0:T(8,128)(2,1)}, u32[]{:S(2)}, u32[]{:S(2)}) async-start(bf16[4,256,512]{2,1,0:T(8,128)(2,1)} %bitcast.1), calls=%async_computation | async-start | bytes 2097152 | tf_op jit(solution)/shard_map/all_to_all | solution.py:14
  8.9 1.6 %copy-start.1 = (bf16[1024,1024]{1,0:T(8,128)(2,1)S(1)}, bf16[1024,1024]{1,0:T(8,128)(2,1)}, u32[]{:S(2)}) copy-start(bf16[1024,1024]{1,0:T(8,128)(2,1)} %in_ref.1) | copy-start | bytes 6291460
  75.5 28.0 %copy-start.3 = (f32[32,512]{1,0:T(8,128)S(1)}, f32[32,512]{1,0:T(8,128)}, u32[]{:S(2)}) copy-start(f32[32,512]{1,0:T(8,128)} %param.8) | copy-start | bytes 196612
  75.5 28.0 %copy-start.4 = (f32[32,512]{1,0:T(8,128)S(1)}, f32[32,512]{1,0:T(8,128)}, u32[]{:S(2)}) copy-start(f32[32,512]{1,0:T(8,128)} %param.9) | copy-start | bytes 196612
  80.3 45.2 %copy-start.2 = (bf16[512,512]{1,0:T(8,128)(2,1)S(1)}, bf16[512,512]{1,0:T(8,128)(2,1)}, u32[]{:S(2)}) copy-start(bf16[512,512]{1,0:T(8,128)(2,1)} %param.7) | copy-start | bytes 1572868

commit v10 on v9

--- a/solution.py
+++ b/solution.py
@@ -63,6 +63,12 @@
         out_ref[at] = jnp.dot(a_ref[at], b_ref[...], preferred_element_type=F32).astype(BF16)
 
 
+def cost(m, k, n):
+    return pl.CostEstimate(
+        flops=2 * m * k * n, bytes_accessed=2 * (m * k + k * n + m * n), transcendentals=0
+    )
+
+
 def product(a, b):
     vmem = pl.BlockSpec(memory_space=pltpu.VMEM)
     m, k, n = a.shape[0], a.shape[1], b.shape[1]
@@ -71,17 +77,47 @@
         in_specs=[vmem, vmem],
         out_specs=vmem,
         out_shape=jax.ShapeDtypeStruct((m, n), BF16),
-        cost_estimate=pl.CostEstimate(
-            flops=2 * m * k * n, bytes_accessed=2 * (m * k + k * n + m * n), transcendentals=0
-        ),
+        cost_estimate=cost(m, k, n),
         compiler_params=pltpu.CompilerParams(vmem_limit_bytes=16 * 2**20),
     )(a, b)
 
 
+def rows_kernel(at_ref, dir_ref, own_ref, near_ref, far_ref, out_ref):
+    own, core = at_ref[0], at_ref[1]
+    width = own_ref.shape[0]
+    half = width // 2
+
+    def fill(ref, at):
+        out_ref[:, pl.ds(pl.multiple_of(at, half), ref.shape[0])] = lax.dot_general(
+            dir_ref[...], ref[...], (((1,), (1,)), ((), ())), preferred_element_type=F32
+        ).astype(BF16)
+
+    fill(own_ref, own * width)
+    fill(near_ref, (1 - own) * width + core * half)
+    fill(far_ref, (1 - own) * width + (1 - core) * half)
+
+
+def update_rows(at, directions, own, near, far):
+    m, k = directions.shape
+    n = 2 * own.shape[0]
+    vmem = pl.BlockSpec(memory_space=pltpu.VMEM)
+    return pl.pallas_call(
+        rows_kernel,
+        in_specs=[pl.BlockSpec(memory_space=pltpu.SMEM)] + [vmem] * 4,
+        out_specs=vmem,
+        out_shape=jax.ShapeDtypeStruct((m, n), BF16),
+        cost_estimate=cost(m, k, n),
+        compiler_params=pltpu.CompilerParams(vmem_limit_bytes=16 * 2**20),
+    )(at, directions, own, near, far)
+
+
 def lay_kernel(in_ref, out_ref):
-    width = in_ref.shape[2]
-    for i in range(in_ref.shape[0]):
-        out_ref[:, i * width : (i + 1) * width] = in_ref[i]
+    n, _, columns = in_ref.shape
+    width = columns // 2
+    for half in range(2):
+        for i in range(n):
+            at = (half * n + i) * width
+            out_ref[:, at : at + width] = in_ref[i, :, half * width : (half + 1) * width]
 
 
 def lay(blocks):
@@ -99,13 +135,22 @@
 
 def local(tokens, tangent, projector, first_moment, second_moment):
     r = projector.shape[1]
+    za, core = lax.axis_index("za"), lax.axis_index("c")
+    z = ("za", "zb")
     tt = turn(tangent)
+    half = projector.shape[0] // 2
+    near = lax.ppermute(
+        lax.dynamic_slice_in_dim(projector, core * half, half, 0), "za", [(0, 1), (1, 0)]
+    )
     part = jnp.dot(tokens, projector, preferred_element_type=F32).astype(BF16)
     part = scattered_sum(part, "x", 4).astype(BF16)
-    tt, part = lax.optimization_barrier((tt, part))
-    part = scattered_sum(part, "zh", 4).astype(BF16)
-    part = spread(part, "zh", 4).reshape(-1, r)
+    near, tt, part = lax.optimization_barrier((near, tt, part))
+    part = scattered_sum(part, z, 4).astype(BF16)
+    part = spread(part, z, 4).reshape(-1, r)
+    near, part = lax.optimization_barrier((near, part))
+    far = lax.ppermute(near, "c", [(0, 1), (1, 0)])
     reduced = spread(part, "x", 4).reshape(-1, r)
+    far, reduced = lax.optimization_barrier((far, reduced))
     grad = product(tt, reduced)
     grad = scattered_sum(grad, "c", 2).astype(BF16)
     gradient = scattered_sum(grad, ("y", "zl"), 16)
@@ -116,17 +161,16 @@
     second_fix = 1.0 - 0.999**STEP
     direction = (new_first / first_fix / (jnp.sqrt(new_second / second_fix) + 1e-08)).astype(BF16)
     rows = direction.shape[0]
-    directions = spread(direction, ("zh", "x"), 16).reshape(-1, r)
-    out = lax.dot_general(
-        directions, projector, (((1,), (1,)), ((), ())), preferred_element_type=F32
-    ).astype(BF16)
-    out = lay(swap(out.reshape(16, rows, -1), ("zh", "x")))
+    directions = spread(direction, ("zb", "x"), 8).reshape(-1, r)
+    at = jnp.stack([za, core]).astype(jnp.int32)
+    out = update_rows(at, directions, projector, near, far)
+    out = lay(swap(out.reshape(8, rows, -1), ("zb", "x")))
     return (out, new_first, new_second)
 
 
 def solution(mesh):
-    fine = Mesh(mesh.devices.reshape(4, 4, 8, 2, 2), ("zh", "x", "y", "zl", "c"))
-    dp, fsdp = ("zh", "x"), ("y", "zl", "c")
+    fine = Mesh(mesh.devices.reshape(2, 2, 4, 8, 2, 2), ("za", "zb", "x", "y", "zl", "c"))
+    dp, fsdp = ("za", "zb", "x"), ("y", "zl", "c")
     rows = P(dp + fsdp, None)
     return jax.shard_map(
         local,

time: 149 us -> 148 us (level)
  blocking collectives: 118 us -> 76.1 us
  starting transfers between devices: 4.3 us -> 25.3 us
  waiting for transfers between devices: 12.1 us -> 27.4 us
  local copies, waits for them, and re-layouts: 2.97 us -> 6.07 us
  Pallas kernels: 4.29 us -> 6.53 us
    all_to_all x7 -> x5, blocking collectives: 118 us -> 76.1 us  [swap(): return lax.all_to_all(parts, axis, 0, 0)]
    ppermute x0 -> x2, starting transfers between devices: none -> 12.8 us  [the longest x1 10.9 us: local(): lax.ppermute(lax.dynamic_slice_in_dim(projector, core * half, half, 0), '...]
    all_to_all x1 -> x3, starting transfers between devices: 4.3 us -> 12.5 us  [swap(): return lax.all_to_all(parts, axis, 0, 0)]
    ppermute x0 -> x2, waiting for transfers between devices: none -> 7.88 us  [the longest x1 6.38 us: local(): lax.ppermute(lax.dynamic_slice_in_dim(projector, core * half, half, 0), '...]
    all_to_all x1 -> x3, waiting for transfers between devices: 12.1 us -> 19.6 us  [swap(): return lax.all_to_all(parts, axis, 0, 0)]
    broadcast_in_dim x3, local copies, waits for them, and re-layouts: 0.14 us -> 1.81 us  [spread(): return swap(jnp.broadcast_to(block[None], (n,) + block.shape), axis)]
    unnamed x10 -> x16, local copies, waits for them, and re-layouts: 2.83 us -> 3.54 us
  transfers between devices with their start and end apart: 1 -> 5, of which waited for: 1 -> 5; matrix products, arithmetic and copies ran while one was open for 0% -> 1% of each run, Pallas kernels for 1% -> 1%
where the time goes in v10:
time: 148 us; the launch traced here: 147 us
  blocking collectives  76.1 us (51%)
  waiting for transfers between devices  27.4 us (19%)
  starting transfers between devices  25.3 us (17%)
  Pallas kernels  6.53 us (4%)
  local copies, waits for them, and re-layouts  6.07 us (4%)
  matrix products  2.73 us (2%)
  other arithmetic  2.33 us (2%)
    all_to_all x5, blocking collectives, swap(): return lax.all_to_all(parts, axis, 0, 0)  76.1 us
    all_to_all x3, waiting for transfers between devices, swap(): return lax.all_to_all(parts, axis, 0, 0)  19.6 us
    all_to_all x3, starting transfers between devices, swap(): return lax.all_to_all(parts, axis, 0, 0)  12.5 us
    ppermute x1, starting transfers between devices, local(): lax.ppermute(lax.dynamic_slice_in_dim(projector, core * half, half, 0), '...  10.9 us
    ppermute x1, waiting for transfers between devices, local(): lax.ppermute(lax.dynamic_slice_in_dim(projector, core * half, half, 0), '...  6.38 us
    unnamed x16, local copies, waits for them, and re-layouts  3.54 us
    pallas_call x1, Pallas kernels, product(): pl.pallas_call(product_kernel, in_specs=[vmem, vmem], out_specs=vmem, out...  2.97 us
  transfers between devices with their start and end apart: 5, of which 5 were waited for; matrix products, arithmetic and copies ran while one was open for 1% of the time, Pallas kernels for 1%

profile of v10, /device:TPU:24, one launch (start us, length us, event | category | flops | bytes accessed | tf_op | source)
XLA Modules:
  0.0 147.2 jit_solution(11771885585843236567)
XLA Ops:
  0.7 1.2 copy-done
  1.9 2.7 %convolution_convert_fusion = bf16[1024,512]{1,0:T(8,128)(2,1)} fusion(bf16[1024,512]{1,0:T(8,128)(2,1)S(1)} %copy-done, bf16[512,512]{1,0:T(8,128)(2,1)} %own_ref.1), kind=kOutput, calls=%fused_computation | convolution fusion | flops 537395200 | bytes 2621440 | tf_op jit(solution)/shard_map/dot_general | solution.py:145
  4.6 4.3 %all-to-all-start = ((bf16[4,256,512]{2,1,0:T(8,128)(2,1)}), bf16[4,256,512]{2,1,0:T(8,128)(2,1)}, u32[]{:S(2)}, u32[]{:S(2)}) async-start(bf16[4,256,512]{2,1,0:T(8,128)(2,1)} %bitcast.3), calls=%async_computation | async-start | bytes 2097152 | tf_op jit(solution)/shard_map/all_to_all | solution.py:14
  9.6 10.9 %collective-permute-start = (bf16[256,512]{1,0:T(8,128)(2,1)}, bf16[256,512]{1,0:T(8,128)(2,1)S(1)}, u32[]{:S(2)}, u32[]{:S(2)}) collective-permute-start(bf16[256,512]{1,0:T(8,128)(2,1)} %constant_dynamic-slice_fusion), channel_id=1, source_target_pairs={{0,256},{256,0},{1,257},{257,1},{2,258},{258,2},{3,259},{259,3},{4... | collective-permute-start | bytes 786440 | tf_op jit(solution)/shard_map/ppermute | solution.py:142
  20.5 1.6 %copy-done.1 = bf16[1024,1024]{1,0:T(8,128)(2,1)S(1)} copy-done((bf16[1024,1024]{1,0:T(8,128)(2,1)S(1)}, bf16[1024,1024]{1,0:T(8,128)(2,1)}, u32[]{:S(2)}) %copy-start.1) | copy-done | bytes 2097176
  22.1 1.7 %shard_map.76 = bf16[2,16,32,1024]{3,2,1,0:T(8,128)(2,1)S(1)} custom-call(bf16[1024,1024]{1,0:T(8,128)(2,1)S(1)} %copy-done.1), custom_call_target="tpu_custom_call" | custom-call | bytes 4194304 | tf_op jit(solution)/shard_map/pallas_call | solution.py:45
  24.3 1.3 fusion
  25.6 6.4 %collective-permute-done.near_ref = bf16[256,512]{1,0:T(8,128)(2,1)S(1)} collective-permute-done((bf16[256,512]{1,0:T(8,128)(2,1)}, bf16[256,512]{1,0:T(8,128)(2,1)S(1)}, u32[]{:S(2)}, u32[]{:S(2)}) %collective-permute-start) | collective-permute-done | bytes 262176 | tf_op jit(solution)/shard_map/ppermute | solution.py:142
  32.0 18.1 %all_to_all.40 = bf16[4,64,512]{2,1,0:T(8,128)(2,1)S(1)} all-to-all(bf16[4,64,512]{2,1,0:T(8,128)(2,1)S(1)} %bitcast.29), channel_id=1, replica_groups=mesh['za'=2,'zb'=2,'x'=4,'y'=8,'zl'=2,'c'=2] {'za','zb'}, dimensions={0} | all-to-all | bytes 524288 | tf_op jit(solution)/shard_map/all_to_all | solution.py:14
  50.1 12.4 %all_to_all.41 = bf16[4,64,512]{2,1,0:T(8,128)(2,1)S(1)} all-to-all(bf16[4,64,512]{2,1,0:T(8,128)(2,1)S(1)} %broadcast_in_dim.9), channel_id=1, replica_groups=mesh['za'=2,'zb'=2,'x'=4,'y'=8,'zl'=2,'c'=2] {'za','zb'}, dimensions={0} | all-to-all | bytes 524288 | tf_op jit(solution)/shard_map/all_to_all | solution.py:14
  62.5 1.1 broadcast_in_dim.10
  63.6 4.3 %all-to-all-start.3 = ((bf16[4,256,512]{2,1,0:T(8,128)(2,1)}), bf16[4,256,512]{2,1,0:T(8,128)(2,1)}, u32[]{:S(2)}, u32[]{:S(2)}) async-start(bf16[4,256,512]{2,1,0:T(8,128)(2,1)} %broadcast_in_dim.10), calls=%async_computation.3 | async-start | bytes 2097152 | tf_op jit(solution)/shard_map/all_to_all | solution.py:14
  67.9 1.9 %collective-permute-start.1 = (bf16[256,512]{1,0:T(8,128)(2,1)S(1)}, bf16[256,512]{1,0:T(8,128)(2,1)S(1)}, u32[]{:S(2)}, u32[]{:S(2)}) collective-permute-start(bf16[256,512]{1,0:T(8,128)(2,1)S(1)} %collective-permute-done.near_ref), channel_id=1, source_target_pairs={{0,1},{1,0},{2,3},{3,2},{4,5},{5,4},{6,7},{7,6},{8,9},{9,8},{10,11... | collective-permute-start | bytes 786440 | tf_op jit(solution)/shard_map/ppermute | solution.py:151
  69.8 1.5 %collective-permute-done.1.far_ref = bf16[256,512]{1,0:T(8,128)(2,1)S(1)} collective-permute-done((bf16[256,512]{1,0:T(8,128)(2,1)S(1)}, bf16[256,512]{1,0:T(8,128)(2,1)S(1)}, u32[]{:S(2)}, u32[]{:S(2)}) %collective-permute-start.1) | collective-permute-done | bytes 262176 | tf_op jit(solution)/shard_map/ppermute | solution.py:151
  72.1 8.5 %all-to-all-done.3 = bf16[4,256,512]{2,1,0:T(8,128)(2,1)} async-done(((bf16[4,256,512]{2,1,0:T(8,128)(2,1)}), bf16[4,256,512]{2,1,0:T(8,128)(2,1)}, u32[]{:S(2)}, u32[]{:S(2)}) %all-to-all-start.3) | async-done | bytes 1048608 | tf_op jit(solution)/shard_map/all_to_all | solution.py:14
  80.5 3.0 %shard_map.77 = bf16[1024,512]{1,0:T(8,128)(2,1)S(1)} custom-call(bf16[1024,1024]{1,0:T(8,128)(2,1)S(1)} %bitcast.24, bf16[1024,512]{1,0:T(8,128)(2,1)} %bitcast.8.b_ref), custom_call_target="tpu_custom_call" | custom-call | flops 1073741824 | bytes 4194304 | tf_op jit(solution)/shard_map/pallas_call | solution.py:75
  83.5 4.7 %all_to_all.42 = bf16[2,512,512]{2,1,0:T(8,128)(2,1)S(1)} all-to-all(bf16[2,512,512]{2,1,0:T(8,128)(2,1)S(1)} %bitcast.25), channel_id=1, replica_groups=mesh['za'=2,'zb'=2,'x'=4,'y'=8,'zl'=2,'c'=2] {'c'}, dimensions={0} | all-to-all | bytes 2097152 | tf_op jit(solution)/shard_map/all_to_all | solution.py:14
  88.4 23.2 %all_to_all.43 = bf16[16,32,512]{2,1,0:T(8,128)(2,1)S(1)} all-to-all(bf16[16,32,512]{2,1,0:T(8,128)(2,1)S(1)} %bitcast.28), channel_id=1, replica_groups=mesh['za'=2,'zb'=2,'x'=4,'y'=8,'zl'=2,'c'=2] {'y','zl'}, dimensions={0} | all-to-all | bytes 1048576 | tf_op jit(solution)/shard_map/all_to_all | solution.py:14
  111.5 0.8 divide_convert_fusion
  113.0 3.8 %all-to-all-start.6 = ((bf16[8,32,512]{2,1,0:T(8,128)(2,1)}), bf16[8,32,512]{2,1,0:T(8,128)(2,1)S(1)}, u32[]{:S(2)}, u32[]{:S(2)}) async-start(bf16[8,32,512]{2,1,0:T(8,128)(2,1)} %broadcast_in_dim.11), calls=%async_computation.6 | async-start | bytes 524288 | tf_op jit(solution)/shard_map/all_to_all | solution.py:14
  116.9 10.7 %all-to-all-done.6 = bf16[8,32,512]{2,1,0:T(8,128)(2,1)S(1)} async-done(((bf16[8,32,512]{2,1,0:T(8,128)(2,1)}), bf16[8,32,512]{2,1,0:T(8,128)(2,1)S(1)}, u32[]{:S(2)}, u32[]{:S(2)}) %all-to-all-start.6) | async-done | bytes 262176 | tf_op jit(solution)/shard_map/all_to_all | solution.py:14
  127.6 1.0 shard_map.78
  128.6 17.8 %all_to_all.44.in_ref = bf16[8,32,1024]{2,1,0:T(8,128)(2,1)S(1)} all-to-all(bf16[8,32,1024]{2,1,0:T(8,128)(2,1)S(1)} %bitcast.26), channel_id=1, replica_groups=mesh['za'=2,'zb'=2,'x'=4,'y'=8,'zl'=2,'c'=2] {'zb','x'}, dimensions={0} | all-to-all | bytes 1048576 | tf_op jit(solution)/shard_map/all_to_all | solution.py:14
  146.4 0.8 shard_map.79
  (21 shorter events, 2.9 us)
Async XLA Ops:
  0.6 1.2 copy-start
  0.6 8.2 %copy-start.2 = (bf16[512,512]{1,0:T(8,128)(2,1)S(1)}, bf16[512,512]{1,0:T(8,128)(2,1)}, u32[]{:S(2)}) copy-start(bf16[512,512]{1,0:T(8,128)(2,1)} %own_ref.1) | copy-start | bytes 1572868
  4.6 19.7 %all-to-all-start = ((bf16[4,256,512]{2,1,0:T(8,128)(2,1)}), bf16[4,256,512]{2,1,0:T(8,128)(2,1)}, u32[]{:S(2)}, u32[]{:S(2)}) async-start(bf16[4,256,512]{2,1,0:T(8,128)(2,1)} %bitcast.3), calls=%async_computation | async-start | bytes 2097152 | tf_op jit(solution)/shard_map/all_to_all | solution.py:14
  9.6 22.4 %collective-permute-start = (bf16[256,512]{1,0:T(8,128)(2,1)}, bf16[256,512]{1,0:T(8,128)(2,1)S(1)}, u32[]{:S(2)}, u32[]{:S(2)}) collective-permute-start(bf16[256,512]{1,0:T(8,128)(2,1)} %constant_dynamic-slice_fusion), channel_id=1, source_target_pairs={{0,256},{256,0},{1,257},{257,1},{2,258},{258,2},{3,259},{259,3},{4... | collective-permute-start | bytes 786440 | tf_op jit(solution)/shard_map/ppermute | solution.py:142
  20.5 1.6 %copy-start.1 = (bf16[1024,1024]{1,0:T(8,128)(2,1)S(1)}, bf16[1024,1024]{1,0:T(8,128)(2,1)}, u32[]{:S(2)}) copy-start(bf16[1024,1024]{1,0:T(8,128)(2,1)} %in_ref.1) | copy-start | bytes 6291460
  63.6 16.9 %all-to-all-start.3 = ((bf16[4,256,512]{2,1,0:T(8,128)(2,1)}), bf16[4,256,512]{2,1,0:T(8,128)(2,1)}, u32[]{:S(2)}, u32[]{:S(2)}) async-start(bf16[4,256,512]{2,1,0:T(8,128)(2,1)} %broadcast_in_dim.10), calls=%async_computation.3 | async-start | bytes 2097152 | tf_op jit(solution)/shard_map/all_to_all | solution.py:14
  67.9 3.4 %collective-permute-start.1 = (bf16[256,512]{1,0:T(8,128)(2,1)S(1)}, bf16[256,512]{1,0:T(8,128)(2,1)S(1)}, u32[]{:S(2)}, u32[]{:S(2)}) collective-permute-start(bf16[256,512]{1,0:T(8,128)(2,1)S(1)} %collective-permute-done.near_ref), channel_id=1, source_target_pairs={{0,1},{1,0},{2,3},{3,2},{4,5},{5,4},{6,7},{7,6},{8,9},{9,8},{10,11... | collective-permute-start | bytes 786440 | tf_op jit(solution)/shard_map/ppermute | solution.py:151
  71.3 0.7 copy-start.4
  83.5 28.0 %copy-start.6 = (f32[32,512]{1,0:T(8,128)S(1)}, f32[32,512]{1,0:T(8,128)}, u32[]{:S(2)}) copy-start(f32[32,512]{1,0:T(8,128)} %param.8) | copy-start | bytes 196612
  83.5 28.0 %copy-start.7 = (f32[32,512]{1,0:T(8,128)S(1)}, f32[32,512]{1,0:T(8,128)}, u32[]{:S(2)}) copy-start(f32[32,512]{1,0:T(8,128)} %param.9) | copy-start | bytes 196612
  88.2 39.4 %copy-start.3 = (bf16[512,512]{1,0:T(8,128)(2,1)S(1)}, bf16[512,512]{1,0:T(8,128)(2,1)}, u32[]{:S(2)}) copy-start(bf16[512,512]{1,0:T(8,128)(2,1)} %own_ref.1) | copy-start | bytes 1572868
  88.2 39.4 %copy-start.5 = (bf16[256,512]{1,0:T(8,128)(2,1)S(1)}, bf16[256,512]{1,0:T(8,128)(2,1)}, u32[]{:S(2)}) copy-start(bf16[256,512]{1,0:T(8,128)(2,1)} %copy-done.4) | copy-start | bytes 786436
  113.0 14.6 %all-to-all-start.6 = ((bf16[8,32,512]{2,1,0:T(8,128)(2,1)}), bf16[8,32,512]{2,1,0:T(8,128)(2,1)S(1)}, u32[]{:S(2)}, u32[]{:S(2)}) async-start(bf16[8,32,512]{2,1,0:T(8,128)(2,1)} %broadcast_in_dim.11), calls=%async_computation.6 | async-start | bytes 524288 | tf_op jit(solution)/shard_map/all_to_all | solution.py:14

commit v11 on v7

--- a/solution.py
+++ b/solution.py
@@ -27,6 +27,10 @@
 
 def spread(block, axis, n):
     return swap(jnp.broadcast_to(block[None], (n,) + block.shape), axis)
+
+
+def back(block, axis, n, k):
+    return lax.ppermute(block, axis, [(i, (i + k) % n) for i in range(n)])
 
 
 def turn_kernel(in_ref, out_ref):
@@ -63,6 +67,12 @@
         out_ref[at] = jnp.dot(a_ref[at], b_ref[...], preferred_element_type=F32).astype(BF16)
 
 
+def cost(m, k, n):
+    return pl.CostEstimate(
+        flops=2 * m * k * n, bytes_accessed=2 * (m * k + k * n + m * n), transcendentals=0
+    )
+
+
 def product(a, b):
     vmem = pl.BlockSpec(memory_space=pltpu.VMEM)
     m, k, n = a.shape[0], a.shape[1], b.shape[1]
@@ -71,11 +81,40 @@
         in_specs=[vmem, vmem],
         out_specs=vmem,
         out_shape=jax.ShapeDtypeStruct((m, n), BF16),
-        cost_estimate=pl.CostEstimate(
-            flops=2 * m * k * n, bytes_accessed=2 * (m * k + k * n + m * n), transcendentals=0
-        ),
+        cost_estimate=cost(m, k, n),
         compiler_params=pltpu.CompilerParams(vmem_limit_bytes=16 * 2**20),
     )(a, b)
+
+
+def rows_kernel(at_ref, dir_ref, own_ref, mine_ref, other_ref, out_ref):
+    z, core = at_ref[0], at_ref[1]
+    width = own_ref.shape[0]
+    half = width // 2
+
+    def fill(rows, at):
+        out_ref[:, pl.ds(pl.multiple_of(at, half), rows.shape[0])] = lax.dot_general(
+            dir_ref[...], rows, (((1,), (1,)), ((), ())), preferred_element_type=F32
+        ).astype(BF16)
+
+    fill(own_ref[...], z * width)
+    for k in range(3):
+        at = lax.rem(z + 3 - k, 4) * width
+        fill(mine_ref[k], at + core * half)
+        fill(other_ref[k], at + (1 - core) * half)
+
+
+def update_rows(at, directions, own, mine, other):
+    m, k = directions.shape
+    n = 4 * own.shape[0]
+    vmem = pl.BlockSpec(memory_space=pltpu.VMEM)
+    return pl.pallas_call(
+        rows_kernel,
+        in_specs=[pl.BlockSpec(memory_space=pltpu.SMEM)] + [vmem] * 4,
+        out_specs=vmem,
+        out_shape=jax.ShapeDtypeStruct((m, n), BF16),
+        cost_estimate=cost(m, k, n),
+        compiler_params=pltpu.CompilerParams(vmem_limit_bytes=16 * 2**20),
+    )(at, directions, own, mine, other)
 
 
 def lay_kernel(in_ref, out_ref):
@@ -102,15 +141,23 @@
 
 def local(tokens, tangent, projector, first_moment, second_moment):
     r = projector.shape[1]
-    share = projector.shape[0] // 16
-    at = (lax.axis_index("y") * 2 + lax.axis_index("c")) * share
-    piece = lax.dynamic_slice_in_dim(projector, at, share, 0)
-    wide = lax.all_gather(piece, ("zh", "y", "c"), axis=0, tiled=True)
+    z, core = lax.axis_index("zh"), lax.axis_index("c")
     tt = turn(tangent)
+    half = projector.shape[0] // 2
+    share = lax.dynamic_slice_in_dim(projector, core * half, half, 0)
+    one, three = back(share, "zh", 4, 1), back(share, "zh", 4, 3)
     part = jnp.dot(tokens, projector, preferred_element_type=F32).astype(BF16)
-    part = scattered_sum(part, ("zh", "x"), 16).astype(BF16)
-    tt, part = lax.optimization_barrier((tt, part))
-    reduced = spread(part, ("zh", "x"), 16).reshape(-1, r)
+    part = scattered_sum(part, "x", 4).astype(BF16)
+    one, three, tt, share, part = lax.optimization_barrier((one, three, tt, share, part))
+    two = back(share, "zh", 4, 2)
+    part = scattered_sum(part, "zh", 4).astype(BF16)
+    one, two, three, part = lax.optimization_barrier((one, two, three, part))
+    mine = jnp.stack([one, two, three])
+    other = lax.ppermute(mine, "c", [(0, 1), (1, 0)])
+    part = spread(part, "zh", 4).reshape(-1, r)
+    at = jnp.stack([z, core]).astype(jnp.int32)
+    at, mine, other, part = lax.optimization_barrier((at, mine, other, part))
+    reduced = spread(part, "x", 4).reshape(-1, r)
     grad = product(tt, reduced)
     grad = scattered_sum(grad, "c", 2).astype(BF16)
     gradient = scattered_sum(grad, ("y", "zl"), 16)
@@ -122,9 +169,7 @@
     direction = (new_first / first_fix / (jnp.sqrt(new_second / second_fix) + 1e-08)).astype(BF16)
     rows = direction.shape[0]
     directions = spread(direction, "x", 4).reshape(-1, r)
-    out = lax.dot_general(
-        directions, wide, (((1,), (1,)), ((), ())), preferred_element_type=F32
-    ).astype(BF16)
+    out = update_rows(at, directions, projector, mine, other)
     out = lay(swap(out.reshape(4, rows, -1), "x"))
     return (out, new_first, new_second)
 

time: 151 us -> 155 us (1.026)
  starting transfers between devices: 18.4 us -> 38 us
  between operations: 14.1 us -> 0.78 us
  blocking collectives: 79.4 us -> 68.9 us
  waiting for transfers between devices: 21.7 us -> 28.6 us
  other arithmetic: 2.28 us -> 5.12 us
  matrix products: 5.15 us -> 2.75 us
  Pallas kernels: 4.29 us -> 6.48 us
    ppermute x0 -> x4, starting transfers between devices: none -> 17.3 us  [the longest x3 15.4 us: back(): return lax.ppermute(block, axis, [(i, (i + k) % n) for i in range(n)])]
    ppermute x0 -> x4, waiting for transfers between devices: none -> 14.1 us  [the longest x3 14.1 us: back(): return lax.ppermute(block, axis, [(i, (i + k) % n) for i in range(n)])]
    all_to_all x4 -> x5, blocking collectives: 79.4 us -> 68.9 us  [swap(): return lax.all_to_all(parts, axis, 0, 0)]
    all_to_all x2 -> x3, waiting for transfers between devices: 21.3 us -> 14.5 us  [swap(): return lax.all_to_all(parts, axis, 0, 0)]
    dot_general x1 -> x0, matrix products: 2.4 us -> none  [local(): lax.dot_general(directions, wide, (((1,), (1,)), ((), ())), preferred_ele...]
    all_to_all x2 -> x3, starting transfers between devices: 18.4 us -> 20.7 us  [swap(): return lax.all_to_all(parts, axis, 0, 0)]
    pallas_call x0 -> x1, Pallas kernels: none -> 2.19 us  [update_rows(): pl.pallas_call(rows_kernel, in_specs=[pl.BlockSpec(memory_space=pltpu.SME...]
    another operation x0 -> x2, other arithmetic: none -> 2.17 us  [the longest x1 2.09 us: local(): mine = jnp.stack([one, two, three])]
  transfers between devices with their start and end apart: 3 -> 7, of which waited for: 3 -> 5; matrix products, arithmetic and copies ran while one was open for 3% -> 2% of each run, Pallas kernels for 2% -> 1%
where the time goes in v11:
time: 155 us; the launch traced here: 154 us
  blocking collectives  68.9 us (44%)
  starting transfers between devices  38 us (25%)
  waiting for transfers between devices  28.6 us (18%)
  Pallas kernels  6.48 us (4%)
  other arithmetic  5.12 us (3%)
  local copies, waits for them, and re-layouts  3.65 us (2%)
  matrix products  2.75 us (2%)
    all_to_all x5, blocking collectives, swap(): return lax.all_to_all(parts, axis, 0, 0)  68.9 us
    all_to_all x3, starting transfers between devices, swap(): return lax.all_to_all(parts, axis, 0, 0)  20.7 us
    ppermute x3, starting transfers between devices, back(): return lax.ppermute(block, axis, [(i, (i + k) % n) for i in range(n)])  15.4 us
    all_to_all x3, waiting for transfers between devices, swap(): return lax.all_to_all(parts, axis, 0, 0)  14.5 us
    ppermute x3, waiting for transfers between devices, back(): return lax.ppermute(block, axis, [(i, (i + k) % n) for i in range(n)])  14.1 us
  transfers between devices with their start and end apart: 7, of which 5 were waited for; matrix products, arithmetic and copies ran while one was open for 2% of the time, Pallas kernels for 1%

profile of v11, /device:TPU:2, one launch (start us, length us, event | category | flops | bytes accessed | tf_op | source)
XLA Modules:
  0.0 154.3 jit_solution(3673446295286785269)
XLA Ops:
  1.9 2.8 %convolution_convert_fusion = bf16[1024,512]{1,0:T(8,128)(2,1)} fusion(bf16[1024,512]{1,0:T(8,128)(2,1)S(1)} %copy-done, bf16[512,512]{1,0:T(8,128)(2,1)} %own_ref.1), kind=kOutput, calls=%fused_computation | convolution fusion | flops 537395200 | bytes 2621440 | tf_op jit(solution)/shard_map/dot_general | solution.py:149
  4.6 10.1 %all-to-all-start = ((bf16[4,256,512]{2,1,0:T(8,128)(2,1)}), bf16[4,256,512]{2,1,0:T(8,128)(2,1)}, u32[]{:S(2)}, u32[]{:S(2)}) async-start(bf16[4,256,512]{2,1,0:T(8,128)(2,1)} %bitcast.3), calls=%async_computation | async-start | bytes 2097152 | tf_op jit(solution)/shard_map/all_to_all | solution.py:14
  14.7 5.7 %collective-permute-start.1 = (bf16[256,512]{1,0:T(8,128)(2,1)S(1)}, bf16[256,512]{1,0:T(8,128)(2,1)}, u32[]{:S(2)}, u32[]{:S(2)}) collective-permute-start(bf16[256,512]{1,0:T(8,128)(2,1)S(1)} %constant_dynamic-slice_fusion), channel_id=1, source_target_pairs={{0,384},{128,0},{256,128},{384,256},{1,385},{129,1},{257,129},{385... | collective-permute-start | bytes 786440 | tf_op jit(solution)/shard_map/ppermute | solution.py:33
  20.4 1.9 %collective-permute-start = (bf16[256,512]{1,0:T(8,128)(2,1)S(1)}, bf16[256,512]{1,0:T(8,128)(2,1)}, u32[]{:S(2)}, u32[]{:S(2)}) collective-permute-start(bf16[256,512]{1,0:T(8,128)(2,1)S(1)} %constant_dynamic-slice_fusion), channel_id=1, source_target_pairs={{0,128},{128,256},{256,384},{384,0},{1,129},{129,257},{257,385},{3... | collective-permute-start | bytes 786440 | tf_op jit(solution)/shard_map/ppermute | solution.py:33
  22.4 1.6 %copy-done.1 = bf16[1024,1024]{1,0:T(8,128)(2,1)S(1)} copy-done((bf16[1024,1024]{1,0:T(8,128)(2,1)S(1)}, bf16[1024,1024]{1,0:T(8,128)(2,1)}, u32[]{:S(2)}) %copy-start.1) | copy-done | bytes 2097176
  23.9 1.7 %shard_map.76 = bf16[2,16,32,1024]{3,2,1,0:T(8,128)(2,1)S(1)} custom-call(bf16[1024,1024]{1,0:T(8,128)(2,1)S(1)} %copy-done.1), custom_call_target="tpu_custom_call" | custom-call | bytes 4194304 | tf_op jit(solution)/shard_map/pallas_call | solution.py:49
  25.7 2.0 %fusion = bf16[256,512]{1,0:T(8,128)(2,1)} fusion(bf16[4,256,512]{2,1,0:T(8,128)(2,1)} %all-to-all-done), kind=kLoop, calls=%fused_computation.4 | loop fusion | flops 1048576 | bytes 1310720 | tf_op jit(solution)/shard_map/add | solution.py:20
  27.7 3.5 %collective-permute-done.1 = bf16[256,512]{1,0:T(8,128)(2,1)} collective-permute-done((bf16[256,512]{1,0:T(8,128)(2,1)S(1)}, bf16[256,512]{1,0:T(8,128)(2,1)}, u32[]{:S(2)}, u32[]{:S(2)}) %collective-permute-start.1) | collective-permute-done | bytes 262176 | tf_op jit(solution)/shard_map/ppermute | solution.py:33
  31.2 6.3 %collective-permute-done = bf16[256,512]{1,0:T(8,128)(2,1)} collective-permute-done((bf16[256,512]{1,0:T(8,128)(2,1)S(1)}, bf16[256,512]{1,0:T(8,128)(2,1)}, u32[]{:S(2)}, u32[]{:S(2)}) %collective-permute-start) | collective-permute-done | bytes 262176 | tf_op jit(solution)/shard_map/ppermute | solution.py:33
  37.5 3.4 %all-to-all-start.1 = ((bf16[4,64,512]{2,1,0:T(8,128)(2,1)}), bf16[4,64,512]{2,1,0:T(8,128)(2,1)S(1)}, u32[]{:S(2)}, u32[]{:S(2)}) async-start(bf16[4,64,512]{2,1,0:T(8,128)(2,1)} %bitcast.5), calls=%async_computation.1 | async-start | bytes 524288 | tf_op jit(solution)/shard_map/all_to_all | solution.py:14
  40.9 7.8 %collective-permute-start.2 = (bf16[256,512]{1,0:T(8,128)(2,1)}, bf16[256,512]{1,0:T(8,128)(2,1)}, u32[]{:S(2)}, u32[]{:S(2)}) collective-permute-start(bf16[256,512]{1,0:T(8,128)(2,1)} %copy-done.4), channel_id=1, source_target_pairs={{0,256},{128,384},{256,0},{384,128},{1,257},{129,385},{257,1},{385... | collective-permute-start | bytes 786440 | tf_op jit(solution)/shard_map/ppermute | solution.py:33
  48.7 3.5 %all-to-all-done.1 = bf16[4,64,512]{2,1,0:T(8,128)(2,1)S(1)} async-done(((bf16[4,64,512]{2,1,0:T(8,128)(2,1)}), bf16[4,64,512]{2,1,0:T(8,128)(2,1)S(1)}, u32[]{:S(2)}, u32[]{:S(2)}) %all-to-all-start.1) | async-done | bytes 262176 | tf_op jit(solution)/shard_map/all_to_all | solution.py:14
  52.2 4.3 %collective-permute-done.2 = bf16[256,512]{1,0:T(8,128)(2,1)} collective-permute-done((bf16[256,512]{1,0:T(8,128)(2,1)}, bf16[256,512]{1,0:T(8,128)(2,1)}, u32[]{:S(2)}, u32[]{:S(2)}) %collective-permute-start.2) | collective-permute-done | bytes 262176 | tf_op jit(solution)/shard_map/ppermute | solution.py:33
  56.5 2.1 %pad_maximum_fusion.mine_ref = bf16[3,256,512]{2,1,0:T(8,128)(2,1)} fusion(bf16[1,256,512]{2,1,0:T(8,128)(2,1)} %bitcast.9, bf16[1,256,512]{2,1,0:T(8,128)(2,1)} %bitcast.8, bf16[1,256,512]{2,1,0:T(8,128)(2,1)} %bitcast.7), kind=kLoop, calls=%fused_computation.2 | loop fusion | flops 786432 | bytes 1572864 | tf_op jit(solution)/shard_map/stack | solution.py:155
  58.6 1.9 %collective-permute-start.3 = (bf16[3,256,512]{2,1,0:T(8,128)(2,1)}, bf16[3,256,512]{2,1,0:T(8,128)(2,1)}, u32[]{:S(2)}, u32[]{:S(2)}) collective-permute-start(bf16[3,256,512]{2,1,0:T(8,128)(2,1)} %pad_maximum_fusion.mine_ref), channel_id=1, source_target_pairs={{0,1},{1,0},{2,3},{3,2},{4,5},{5,4},{6,7},{7,6},{8,9},{9,8},{10,11... | collective-permute-start | bytes 2359304 | tf_op jit(solution)/shard_map/ppermute | solution.py:156
  61.3 7.2 %all-to-all-start.2 = ((bf16[4,64,512]{2,1,0:T(8,128)(2,1)}), bf16[4,64,512]{2,1,0:T(8,128)(2,1)S(1)}, u32[]{:S(2)}, u32[]{:S(2)}) async-start(bf16[4,64,512]{2,1,0:T(8,128)(2,1)} %broadcast_in_dim.6), calls=%async_computation.2 | async-start | bytes 524288 | tf_op jit(solution)/shard_map/all_to_all | solution.py:14
  68.5 11.0 %all-to-all-done.2 = bf16[4,64,512]{2,1,0:T(8,128)(2,1)S(1)} async-done(((bf16[4,64,512]{2,1,0:T(8,128)(2,1)}), bf16[4,64,512]{2,1,0:T(8,128)(2,1)S(1)}, u32[]{:S(2)}, u32[]{:S(2)}) %all-to-all-start.2) | async-done | bytes 262176 | tf_op jit(solution)/shard_map/all_to_all | solution.py:14
  79.6 16.4 %all_to_all.40 = bf16[4,256,512]{2,1,0:T(8,128)(2,1)S(1)} all-to-all(bf16[4,256,512]{2,1,0:T(8,128)(2,1)S(1)} %broadcast_in_dim.7), channel_id=1, replica_groups=mesh['zh'=4,'x'=4,'y'=8,'zl'=2,'c'=2] {'x'}, dimensions={0} | all-to-all | bytes 2097152 | tf_op jit(solution)/shard_map/all_to_all | solution.py:14
  96.0 1.7 %shard_map.77 = bf16[1024,512]{1,0:T(8,128)(2,1)S(1)} custom-call(bf16[1024,1024]{1,0:T(8,128)(2,1)S(1)} %bitcast.27, bf16[1024,512]{1,0:T(8,128)(2,1)S(1)} %bitcast.28), custom_call_target="tpu_custom_call" | custom-call | flops 1073741824 | bytes 4194304 | tf_op jit(solution)/shard_map/pallas_call | solution.py:79
  97.8 4.7 %all_to_all.41 = bf16[2,512,512]{2,1,0:T(8,128)(2,1)S(1)} all-to-all(bf16[2,512,512]{2,1,0:T(8,128)(2,1)S(1)} %bitcast.29), channel_id=1, replica_groups=mesh['zh'=4,'x'=4,'y'=8,'zl'=2,'c'=2] {'c'}, dimensions={0} | all-to-all | bytes 2097152 | tf_op jit(solution)/shard_map/all_to_all | solution.py:14
  102.7 28.9 %all_to_all.42 = bf16[16,32,512]{2,1,0:T(8,128)(2,1)S(1)} all-to-all(bf16[16,32,512]{2,1,0:T(8,128)(2,1)S(1)} %bitcast.32), channel_id=1, replica_groups=mesh['zh'=4,'x'=4,'y'=8,'zl'=2,'c'=2] {'y','zl'}, dimensions={0} | all-to-all | bytes 1048576 | tf_op jit(solution)/shard_map/all_to_all | solution.py:14
  132.4 8.4 %all_to_all.43 = bf16[4,32,512]{2,1,0:T(8,128)(2,1)S(1)} all-to-all(bf16[4,32,512]{2,1,0:T(8,128)(2,1)S(1)} %broadcast_in_dim.8), channel_id=1, replica_groups=mesh['zh'=4,'x'=4,'y'=8,'zl'=2,'c'=2] {'x'}, dimensions={0} | all-to-all | bytes 262144 | tf_op jit(solution)/shard_map/all_to_all | solution.py:14
  140.8 2.2 %shard_map.78 = bf16[128,2048]{1,0:T(8,128)(2,1)S(1)} custom-call(s32[2]{0:T(128)S(1)} %pad_add_fusion.at_ref, bf16[128,512]{1,0:T(8,128)(2,1)S(1)} %bitcast.31, bf16[512,512]{1,0:T(8,128)(2,1)S(1)} %copy-done.3, bf16[3,256,512]{2,1,0:T(8,128)(2,1)} %pad_maximum_fusion.mine_ref, bf16[3,256,512]{2,1,0:T(8,128)(2,1)} %collective-permute-done.3.other_ref), custom_call_target="tpu_custom_call" | custom-call | flops 268435456 | bytes 2752512 | tf_op jit(solution)/shard_map/pallas_call | solution.py:110
  143.0 10.5 %all_to_all.44.in_ref = bf16[4,32,2048]{2,1,0:T(8,128)(2,1)S(1)} all-to-all(bf16[4,32,2048]{2,1,0:T(8,128)(2,1)S(1)} %bitcast.30), channel_id=1, replica_groups=mesh['zh'=4,'x'=4,'y'=8,'zl'=2,'c'=2] {'x'}, dimensions={0} | all-to-all | bytes 1048576 | tf_op jit(solution)/shard_map/all_to_all | solution.py:14
  (24 shorter events, 3.9 us)
Async XLA Ops:
  0.6 1.2 copy-start
  0.6 14.1 %copy-start.2 = (bf16[512,512]{1,0:T(8,128)(2,1)S(1)}, bf16[512,512]{1,0:T(8,128)(2,1)}, u32[]{:S(2)}) copy-start(bf16[512,512]{1,0:T(8,128)(2,1)} %own_ref.1) | copy-start | bytes 1572868
  4.6 21.1 %all-to-all-start = ((bf16[4,256,512]{2,1,0:T(8,128)(2,1)}), bf16[4,256,512]{2,1,0:T(8,128)(2,1)}, u32[]{:S(2)}, u32[]{:S(2)}) async-start(bf16[4,256,512]{2,1,0:T(8,128)(2,1)} %bitcast.3), calls=%async_computation | async-start | bytes 2097152 | tf_op jit(solution)/shard_map/all_to_all | solution.py:14
  14.7 13.0 %copy-start.4 = (bf16[256,512]{1,0:T(8,128)(2,1)}, bf16[256,512]{1,0:T(8,128)(2,1)S(1)}, u32[]{:S(2)}) copy-start(bf16[256,512]{1,0:T(8,128)(2,1)S(1)} %constant_dynamic-slice_fusion) | copy-start | bytes 786436
  14.7 16.4 %collective-permute-start.1 = (bf16[256,512]{1,0:T(8,128)(2,1)S(1)}, bf16[256,512]{1,0:T(8,128)(2,1)}, u32[]{:S(2)}, u32[]{:S(2)}) collective-permute-start(bf16[256,512]{1,0:T(8,128)(2,1)S(1)} %constant_dynamic-slice_fusion), channel_id=1, source_target_pairs={{0,384},{128,0},{256,128},{384,256},{1,385},{129,1},{257,129},{385... | collective-permute-start | bytes 786440 | tf_op jit(solution)/shard_map/ppermute | solution.py:33
  20.4 17.1 %collective-permute-start = (bf16[256,512]{1,0:T(8,128)(2,1)S(1)}, bf16[256,512]{1,0:T(8,128)(2,1)}, u32[]{:S(2)}, u32[]{:S(2)}) collective-permute-start(bf16[256,512]{1,0:T(8,128)(2,1)S(1)} %constant_dynamic-slice_fusion), channel_id=1, source_target_pairs={{0,128},{128,256},{256,384},{384,0},{1,129},{129,257},{257,385},{3... | collective-permute-start | bytes 786440 | tf_op jit(solution)/shard_map/ppermute | solution.py:33
  22.3 1.6 %copy-start.1 = (bf16[1024,1024]{1,0:T(8,128)(2,1)S(1)}, bf16[1024,1024]{1,0:T(8,128)(2,1)}, u32[]{:S(2)}) copy-start(bf16[1024,1024]{1,0:T(8,128)(2,1)} %in_ref.1) | copy-start | bytes 6291460
  37.5 14.7 %all-to-all-start.1 = ((bf16[4,64,512]{2,1,0:T(8,128)(2,1)}), bf16[4,64,512]{2,1,0:T(8,128)(2,1)S(1)}, u32[]{:S(2)}, u32[]{:S(2)}) async-start(bf16[4,64,512]{2,1,0:T(8,128)(2,1)} %bitcast.5), calls=%async_computation.1 | async-start | bytes 524288 | tf_op jit(solution)/shard_map/all_to_all | solution.py:14
  40.9 15.6 %collective-permute-start.2 = (bf16[256,512]{1,0:T(8,128)(2,1)}, bf16[256,512]{1,0:T(8,128)(2,1)}, u32[]{:S(2)}, u32[]{:S(2)}) collective-permute-start(bf16[256,512]{1,0:T(8,128)(2,1)} %copy-done.4), channel_id=1, source_target_pairs={{0,256},{128,384},{256,0},{384,128},{1,257},{129,385},{257,1},{385... | collective-permute-start | bytes 786440 | tf_op jit(solution)/shard_map/ppermute | solution.py:33
  58.6 20.9 %collective-permute-start.3 = (bf16[3,256,512]{2,1,0:T(8,128)(2,1)}, bf16[3,256,512]{2,1,0:T(8,128)(2,1)}, u32[]{:S(2)}, u32[]{:S(2)}) collective-permute-start(bf16[3,256,512]{2,1,0:T(8,128)(2,1)} %pad_maximum_fusion.mine_ref), channel_id=1, source_target_pairs={{0,1},{1,0},{2,3},{3,2},{4,5},{5,4},{6,7},{7,6},{8,9},{9,8},{10,11... | collective-permute-start | bytes 2359304 | tf_op jit(solution)/shard_map/ppermute | solution.py:156
  61.3 18.3 %all-to-all-start.2 = ((bf16[4,64,512]{2,1,0:T(8,128)(2,1)}), bf16[4,64,512]{2,1,0:T(8,128)(2,1)S(1)}, u32[]{:S(2)}, u32[]{:S(2)}) async-start(bf16[4,64,512]{2,1,0:T(8,128)(2,1)} %broadcast_in_dim.6), calls=%async_computation.2 | async-start | bytes 524288 | tf_op jit(solution)/shard_map/all_to_all | solution.py:14
  97.8 33.8 %copy-start.5 = (f32[32,512]{1,0:T(8,128)S(1)}, f32[32,512]{1,0:T(8,128)}, u32[]{:S(2)}) copy-start(f32[32,512]{1,0:T(8,128)} %param.8) | copy-start | bytes 196612
  97.8 33.8 %copy-start.6 = (f32[32,512]{1,0:T(8,128)S(1)}, f32[32,512]{1,0:T(8,128)}, u32[]{:S(2)}) copy-start(f32[32,512]{1,0:T(8,128)} %param.9) | copy-start | bytes 196612
  102.5 38.2 %copy-start.3 = (bf16[512,512]{1,0:T(8,128)(2,1)S(1)}, bf16[512,512]{1,0:T(8,128)(2,1)}, u32[]{:S(2)}) copy-start(bf16[512,512]{1,0:T(8,128)(2,1)} %own_ref.1) | copy-start | bytes 1572868

commit v12 on v10

--- a/solution.py
+++ b/solution.py
@@ -82,33 +82,47 @@
     )(a, b)
 
 
-def rows_kernel(at_ref, dir_ref, own_ref, near_ref, far_ref, out_ref):
-    own, core = at_ref[0], at_ref[1]
+def first_kernel(a_ref, b_ref, out_ref):
+    out_ref[...] = jnp.dot(a_ref[...], b_ref[...], preferred_element_type=F32).astype(BF16)
+
+
+def first_product(a, b):
+    m, k, n = a.shape[0], a.shape[1], b.shape[1]
+    return pl.pallas_call(
+        first_kernel,
+        grid=(4,),
+        in_specs=[
+            pl.BlockSpec((m // 4, k), lambda i: (i, 0)),
+            pl.BlockSpec((k, n), lambda i: (0, 0)),
+        ],
+        out_specs=pl.BlockSpec((m // 4, n), lambda i: (i, 0)),
+        out_shape=jax.ShapeDtypeStruct((m, n), BF16),
+        cost_estimate=cost(m, k, n),
+        compiler_params=pltpu.CompilerParams(vmem_limit_bytes=60 * 2**20),
+    )(a, b)
+
+
+def rows_kernel(at_ref, dir_ref, own_ref, far_ref, out_ref):
+    own = at_ref[0]
     width = own_ref.shape[0]
-    half = width // 2
-
-    def fill(ref, at):
-        out_ref[:, pl.ds(pl.multiple_of(at, half), ref.shape[0])] = lax.dot_general(
+    for ref, at in ((own_ref, own), (far_ref, 1 - own)):
+        out_ref[:, pl.ds(pl.multiple_of(at * width, width), width)] = lax.dot_general(
             dir_ref[...], ref[...], (((1,), (1,)), ((), ())), preferred_element_type=F32
         ).astype(BF16)
 
-    fill(own_ref, own * width)
-    fill(near_ref, (1 - own) * width + core * half)
-    fill(far_ref, (1 - own) * width + (1 - core) * half)
 
-
-def update_rows(at, directions, own, near, far):
+def update_rows(at, directions, own, far):
     m, k = directions.shape
     n = 2 * own.shape[0]
     vmem = pl.BlockSpec(memory_space=pltpu.VMEM)
     return pl.pallas_call(
         rows_kernel,
-        in_specs=[pl.BlockSpec(memory_space=pltpu.SMEM)] + [vmem] * 4,
+        in_specs=[pl.BlockSpec(memory_space=pltpu.SMEM)] + [vmem] * 3,
         out_specs=vmem,
         out_shape=jax.ShapeDtypeStruct((m, n), BF16),
         cost_estimate=cost(m, k, n),
         compiler_params=pltpu.CompilerParams(vmem_limit_bytes=16 * 2**20),
-    )(at, directions, own, near, far)
+    )(at, directions, own, far)
 
 
 def lay_kernel(in_ref, out_ref):
@@ -135,22 +149,16 @@
 
 def local(tokens, tangent, projector, first_moment, second_moment):
     r = projector.shape[1]
-    za, core = lax.axis_index("za"), lax.axis_index("c")
     z = ("za", "zb")
+    at = lax.axis_index("za").reshape(1).astype(jnp.int32)
     tt = turn(tangent)
-    half = projector.shape[0] // 2
-    near = lax.ppermute(
-        lax.dynamic_slice_in_dim(projector, core * half, half, 0), "za", [(0, 1), (1, 0)]
-    )
-    part = jnp.dot(tokens, projector, preferred_element_type=F32).astype(BF16)
+    far = lax.ppermute(projector, "za", [(0, 1), (1, 0)])
+    part = first_product(tokens, projector)
     part = scattered_sum(part, "x", 4).astype(BF16)
-    near, tt, part = lax.optimization_barrier((near, tt, part))
+    at, far, tt, part = lax.optimization_barrier((at, far, tt, part))
     part = scattered_sum(part, z, 4).astype(BF16)
     part = spread(part, z, 4).reshape(-1, r)
-    near, part = lax.optimization_barrier((near, part))
-    far = lax.ppermute(near, "c", [(0, 1), (1, 0)])
     reduced = spread(part, "x", 4).reshape(-1, r)
-    far, reduced = lax.optimization_barrier((far, reduced))
     grad = product(tt, reduced)
     grad = scattered_sum(grad, "c", 2).astype(BF16)
     gradient = scattered_sum(grad, ("y", "zl"), 16)
@@ -162,8 +170,7 @@
     direction = (new_first / first_fix / (jnp.sqrt(new_second / second_fix) + 1e-08)).astype(BF16)
     rows = direction.shape[0]
     directions = spread(direction, ("zb", "x"), 8).reshape(-1, r)
-    at = jnp.stack([za, core]).astype(jnp.int32)
-    out = update_rows(at, directions, projector, near, far)
+    out = update_rows(at, directions, projector, far)
     out = lay(swap(out.reshape(8, rows, -1), ("zb", "x")))
     return (out, new_first, new_second)
 

time: 148 us -> 153 us (1.034)
  blocking collectives: 76.1 us -> 116 us
  waiting for transfers between devices: 27.4 us -> 7.4 us
  starting transfers between devices: 25.3 us -> 15.2 us
  local copies, waits for them, and re-layouts: 6.07 us -> 1.72 us
  matrix products: 2.73 us -> 0 us
  Pallas kernels: 6.53 us -> 8.92 us
    all_to_all x5 -> x7, blocking collectives: 76.1 us -> 116 us  [swap(): return lax.all_to_all(parts, axis, 0, 0)]
    all_to_all x3 -> x1, waiting for transfers between devices: 19.6 us -> 1.14 us  [swap(): return lax.all_to_all(parts, axis, 0, 0)]
    all_to_all x3 -> x1, starting transfers between devices: 12.5 us -> 4.29 us  [swap(): return lax.all_to_all(parts, axis, 0, 0)]
    pallas_call x0 -> x1, Pallas kernels: none -> 4.16 us  [first_product(): pl.pallas_call(first_kernel, grid=(4,), in_specs=[pl.BlockSpec((m // 4, k...]
    dot_general x1 -> x0, matrix products: 2.73 us -> none  [local(): part = jnp.dot(tokens, projector, preferred_element_type=F32).astype(BF16)]
    unnamed x16 -> x8, local copies, waits for them, and re-layouts: 3.54 us -> 1.6 us
    ppermute x2 -> x1, starting transfers between devices: 12.8 us -> 10.9 us  [local(): far = lax.ppermute(projector, 'za', [(0, 1), (1, 0)])]
    broadcast_in_dim x3, local copies, waits for them, and re-layouts: 1.81 us -> 0.11 us  [spread(): return swap(jnp.broadcast_to(block[None], (n,) + block.shape), axis)]
  transfers between devices with their start and end apart: 5 -> 2, of which waited for: 5 -> 2; matrix products, arithmetic and copies ran while one was open for 1% -> 1% of each run, Pallas kernels for 1% -> 1%
where the time goes in v12:
time: 153 us; the launch traced here: 152 us
  blocking collectives  116 us (76%)
  starting transfers between devices  15.2 us (10%)
  Pallas kernels  8.92 us (6%)
  waiting for transfers between devices  7.4 us (5%)
  other arithmetic  2.25 us (1%)
  local copies, waits for them, and re-layouts  1.72 us (1%)
    all_to_all x7, blocking collectives, swap(): return lax.all_to_all(parts, axis, 0, 0)  116 us
    ppermute x1, starting transfers between devices, local(): far = lax.ppermute(projector, 'za', [(0, 1), (1, 0)])  10.9 us
    ppermute x1, waiting for transfers between devices, local(): far = lax.ppermute(projector, 'za', [(0, 1), (1, 0)])  6.25 us
    all_to_all x1, starting transfers between devices, swap(): return lax.all_to_all(parts, axis, 0, 0)  4.29 us
    pallas_call x1, Pallas kernels, first_product(): pl.pallas_call(first_kernel, grid=(4,), in_specs=[pl.BlockSpec((m // 4, k...  4.16 us
  transfers between devices with their start and end apart: 2, of which 2 were waited for; matrix products, arithmetic and copies ran while one was open for 1% of the time, Pallas kernels for 1%

profile of v12, /device:TPU:24, one launch (start us, length us, event | category | flops | bytes accessed | tf_op | source)
XLA Modules:
  0.0 152.4 jit_solution(11754905570805060665)
XLA Ops:
  0.6 4.2 %shard_map.77 = bf16[1024,512]{1,0:T(8,128)(2,1)} custom-call(bf16[1024,512]{1,0:T(8,128)(2,1)} %a_ref.1, bf16[512,512]{1,0:T(8,128)(2,1)} %own_ref.1), custom_call_target="tpu_custom_call" | custom-call | flops 536870912 | bytes 2621440 | tf_op jit(solution)/shard_map/pallas_call | solution.py:91
  4.8 4.3 %all-to-all-start = ((bf16[4,256,512]{2,1,0:T(8,128)(2,1)}), bf16[4,256,512]{2,1,0:T(8,128)(2,1)}, u32[]{:S(2)}, u32[]{:S(2)}) async-start(bf16[4,256,512]{2,1,0:T(8,128)(2,1)} %bitcast.26), calls=%async_computation | async-start | bytes 2097152 | tf_op jit(solution)/shard_map/all_to_all | solution.py:14
  9.1 10.9 %collective-permute-start = (bf16[512,512]{1,0:T(8,128)(2,1)S(1)}, bf16[512,512]{1,0:T(8,128)(2,1)S(1)}, u32[]{:S(2)}, u32[]{:S(2)}) collective-permute-start(bf16[512,512]{1,0:T(8,128)(2,1)S(1)} %copy-done.1), channel_id=1, source_target_pairs={{0,256},{256,0},{1,257},{257,1},{2,258},{258,2},{3,259},{259,3},{4... | collective-permute-start | bytes 1572872 | tf_op jit(solution)/shard_map/ppermute | solution.py:155
  20.0 0.0 copy-start
  20.0 1.6 %copy-done = bf16[1024,1024]{1,0:T(8,128)(2,1)S(1)} copy-done((bf16[1024,1024]{1,0:T(8,128)(2,1)S(1)}, bf16[1024,1024]{1,0:T(8,128)(2,1)}, u32[]{:S(2)}) %copy-start) | copy-done | bytes 2097176
  21.6 1.7 %shard_map.76 = bf16[2,16,32,1024]{3,2,1,0:T(8,128)(2,1)S(1)} custom-call(bf16[1024,1024]{1,0:T(8,128)(2,1)S(1)} %copy-done), custom_call_target="tpu_custom_call" | custom-call | bytes 4194304 | tf_op jit(solution)/shard_map/pallas_call | solution.py:45
  23.3 1.1 all-to-all-done
  24.5 1.3 fusion
  25.8 6.3 %collective-permute-done.far_ref = bf16[512,512]{1,0:T(8,128)(2,1)S(1)} collective-permute-done((bf16[512,512]{1,0:T(8,128)(2,1)S(1)}, bf16[512,512]{1,0:T(8,128)(2,1)S(1)}, u32[]{:S(2)}, u32[]{:S(2)}) %collective-permute-start) | collective-permute-done | bytes 524320 | tf_op jit(solution)/shard_map/ppermute | solution.py:155
  32.1 28.6 %all_to_all.40 = bf16[4,64,512]{2,1,0:T(8,128)(2,1)S(1)} all-to-all(bf16[4,64,512]{2,1,0:T(8,128)(2,1)S(1)} %bitcast.28), channel_id=1, replica_groups=mesh['za'=2,'zb'=2,'x'=4,'y'=8,'zl'=2,'c'=2] {'za','zb'}, dimensions={0} | all-to-all | bytes 524288 | tf_op jit(solution)/shard_map/all_to_all | solution.py:14
  60.7 12.5 %all_to_all.41 = bf16[4,64,512]{2,1,0:T(8,128)(2,1)S(1)} all-to-all(bf16[4,64,512]{2,1,0:T(8,128)(2,1)S(1)} %broadcast_in_dim.22), channel_id=1, replica_groups=mesh['za'=2,'zb'=2,'x'=4,'y'=8,'zl'=2,'c'=2] {'za','zb'}, dimensions={0} | all-to-all | bytes 524288 | tf_op jit(solution)/shard_map/all_to_all | solution.py:14
  73.2 0.1 broadcast_in_dim.24
  73.3 16.6 %all_to_all.42 = bf16[4,256,512]{2,1,0:T(8,128)(2,1)S(1)} all-to-all(bf16[4,256,512]{2,1,0:T(8,128)(2,1)S(1)} %broadcast_in_dim.24), channel_id=1, replica_groups=mesh['za'=2,'zb'=2,'x'=4,'y'=8,'zl'=2,'c'=2] {'x'}, dimensions={0} | all-to-all | bytes 2097152 | tf_op jit(solution)/shard_map/all_to_all | solution.py:14
  89.9 1.7 %shard_map.78 = bf16[1024,512]{1,0:T(8,128)(2,1)S(1)} custom-call(bf16[1024,1024]{1,0:T(8,128)(2,1)S(1)} %bitcast.21, bf16[1024,512]{1,0:T(8,128)(2,1)S(1)} %bitcast.22), custom_call_target="tpu_custom_call" | custom-call | flops 1073741824 | bytes 4194304 | tf_op jit(solution)/shard_map/pallas_call | solution.py:75
  91.6 0.0 copy-start.2
  91.6 0.0 copy-start.3
  91.7 4.7 %all_to_all.43 = bf16[2,512,512]{2,1,0:T(8,128)(2,1)S(1)} all-to-all(bf16[2,512,512]{2,1,0:T(8,128)(2,1)S(1)} %bitcast.23), channel_id=1, replica_groups=mesh['za'=2,'zb'=2,'x'=4,'y'=8,'zl'=2,'c'=2] {'c'}, dimensions={0} | all-to-all | bytes 2097152 | tf_op jit(solution)/shard_map/all_to_all | solution.py:14
  96.4 0.1 add_convert_fusion
  96.5 22.6 %all_to_all.44 = bf16[16,32,512]{2,1,0:T(8,128)(2,1)S(1)} all-to-all(bf16[16,32,512]{2,1,0:T(8,128)(2,1)S(1)} %bitcast.27), channel_id=1, replica_groups=mesh['za'=2,'zb'=2,'x'=4,'y'=8,'zl'=2,'c'=2] {'y','zl'}, dimensions={0} | all-to-all | bytes 1048576 | tf_op jit(solution)/shard_map/all_to_all | solution.py:14
  119.1 0.8 divide_convert_fusion
  119.9 13.4 %all_to_all.45 = bf16[8,32,512]{2,1,0:T(8,128)(2,1)S(1)} all-to-all(bf16[8,32,512]{2,1,0:T(8,128)(2,1)S(1)} %broadcast_in_dim.25), channel_id=1, replica_groups=mesh['za'=2,'zb'=2,'x'=4,'y'=8,'zl'=2,'c'=2] {'zb','x'}, dimensions={0} | all-to-all | bytes 524288 | tf_op jit(solution)/shard_map/all_to_all | solution.py:14
  133.3 0.5 shard_map.79
  133.8 17.9 %all_to_all.46.in_ref = bf16[8,32,1024]{2,1,0:T(8,128)(2,1)S(1)} all-to-all(bf16[8,32,1024]{2,1,0:T(8,128)(2,1)S(1)} %bitcast.24), channel_id=1, replica_groups=mesh['za'=2,'zb'=2,'x'=4,'y'=8,'zl'=2,'c'=2] {'zb','x'}, dimensions={0} | all-to-all | bytes 1048576 | tf_op jit(solution)/shard_map/all_to_all | solution.py:14
  151.6 0.8 shard_map.80
  (7 shorter events, 0.1 us)
Async XLA Ops:
  0.6 8.5 %copy-start.1 = (bf16[512,512]{1,0:T(8,128)(2,1)S(1)}, bf16[512,512]{1,0:T(8,128)(2,1)}, u32[]{:S(2)}) copy-start(bf16[512,512]{1,0:T(8,128)(2,1)} %own_ref.1) | copy-start | bytes 1572868
  4.8 19.7 %all-to-all-start = ((bf16[4,256,512]{2,1,0:T(8,128)(2,1)}), bf16[4,256,512]{2,1,0:T(8,128)(2,1)}, u32[]{:S(2)}, u32[]{:S(2)}) async-start(bf16[4,256,512]{2,1,0:T(8,128)(2,1)} %bitcast.26), calls=%async_computation | async-start | bytes 2097152 | tf_op jit(solution)/shard_map/all_to_all | solution.py:14
  9.1 23.0 %collective-permute-start = (bf16[512,512]{1,0:T(8,128)(2,1)S(1)}, bf16[512,512]{1,0:T(8,128)(2,1)S(1)}, u32[]{:S(2)}, u32[]{:S(2)}) collective-permute-start(bf16[512,512]{1,0:T(8,128)(2,1)S(1)} %copy-done.1), channel_id=1, source_target_pairs={{0,256},{256,0},{1,257},{257,1},{2,258},{258,2},{3,259},{259,3},{4... | collective-permute-start | bytes 1572872 | tf_op jit(solution)/shard_map/ppermute | solution.py:155
  20.0 1.6 %copy-start = (bf16[1024,1024]{1,0:T(8,128)(2,1)S(1)}, bf16[1024,1024]{1,0:T(8,128)(2,1)}, u32[]{:S(2)}) copy-start(bf16[1024,1024]{1,0:T(8,128)(2,1)} %in_ref.1) | copy-start | bytes 6291460
  91.6 27.4 %copy-start.2 = (f32[32,512]{1,0:T(8,128)S(1)}, f32[32,512]{1,0:T(8,128)}, u32[]{:S(2)}) copy-start(f32[32,512]{1,0:T(8,128)} %param.8) | copy-start | bytes 196612
  91.6 27.4 %copy-start.3 = (f32[32,512]{1,0:T(8,128)S(1)}, f32[32,512]{1,0:T(8,128)}, u32[]{:S(2)}) copy-start(f32[32,512]{1,0:T(8,128)} %param.9) | copy-start | bytes 196612

commit v13 on v9

--- a/solution.py
+++ b/solution.py
@@ -27,6 +27,10 @@
 
 def spread(block, axis, n):
     return swap(jnp.broadcast_to(block[None], (n,) + block.shape), axis)
+
+
+def back(block, axis, n, k):
+    return lax.ppermute(block, axis, [(i, (i + k) % n) for i in range(n)])
 
 
 def turn_kernel(in_ref, out_ref):
@@ -63,6 +67,12 @@
         out_ref[at] = jnp.dot(a_ref[at], b_ref[...], preferred_element_type=F32).astype(BF16)
 
 
+def cost(m, k, n):
+    return pl.CostEstimate(
+        flops=2 * m * k * n, bytes_accessed=2 * (m * k + k * n + m * n), transcendentals=0
+    )
+
+
 def product(a, b):
     vmem = pl.BlockSpec(memory_space=pltpu.VMEM)
     m, k, n = a.shape[0], a.shape[1], b.shape[1]
@@ -71,17 +81,42 @@
         in_specs=[vmem, vmem],
         out_specs=vmem,
         out_shape=jax.ShapeDtypeStruct((m, n), BF16),
-        cost_estimate=pl.CostEstimate(
-            flops=2 * m * k * n, bytes_accessed=2 * (m * k + k * n + m * n), transcendentals=0
-        ),
+        cost_estimate=cost(m, k, n),
         compiler_params=pltpu.CompilerParams(vmem_limit_bytes=16 * 2**20),
     )(a, b)
 
 
+def rows_kernel(z_ref, dir_ref, *refs):
+    out_ref = refs[-1]
+    width = refs[0].shape[0]
+    for k, ref in enumerate(refs[:-1]):
+        at = lax.rem(z_ref[0] + 4 - k, 4) * width
+        out_ref[:, pl.ds(pl.multiple_of(at, width), width)] = lax.dot_general(
+            dir_ref[...], ref[...], (((1,), (1,)), ((), ())), preferred_element_type=F32
+        ).astype(BF16)
+
+
+def update_rows(z, directions, shares):
+    m, k = directions.shape
+    n = 4 * shares[0].shape[0]
+    vmem = pl.BlockSpec(memory_space=pltpu.VMEM)
+    return pl.pallas_call(
+        rows_kernel,
+        in_specs=[pl.BlockSpec(memory_space=pltpu.SMEM)] + [vmem] * 5,
+        out_specs=vmem,
+        out_shape=jax.ShapeDtypeStruct((m, n), BF16),
+        cost_estimate=cost(m, k, n),
+        compiler_params=pltpu.CompilerParams(vmem_limit_bytes=16 * 2**20),
+    )(z, directions, *shares)
+
+
 def lay_kernel(in_ref, out_ref):
-    width = in_ref.shape[2]
-    for i in range(in_ref.shape[0]):
-        out_ref[:, i * width : (i + 1) * width] = in_ref[i]
+    n, _, columns = in_ref.shape
+    width = columns // 4
+    for z in range(4):
+        for i in range(n):
+            at = (z * n + i) * width
+            out_ref[:, at : at + width] = in_ref[i, :, z * width : (z + 1) * width]
 
 
 def lay(blocks):
@@ -99,16 +134,23 @@
 
 def local(tokens, tangent, projector, first_moment, second_moment):
     r = projector.shape[1]
+    z = lax.axis_index("zh").reshape(1).astype(jnp.int32)
     tt = turn(tangent)
+    half = projector.shape[0] // 2
+    share = lax.dynamic_slice_in_dim(projector, lax.axis_index("c") * half, half, 0)
+    one, three = back(share, "zh", 4, 1), back(share, "zh", 4, 3)
     part = jnp.dot(tokens, projector, preferred_element_type=F32).astype(BF16)
     part = scattered_sum(part, "x", 4).astype(BF16)
-    tt, part = lax.optimization_barrier((tt, part))
+    z, one, three, tt, share, part = lax.optimization_barrier((z, one, three, tt, share, part))
     part = scattered_sum(part, "zh", 4).astype(BF16)
     part = spread(part, "zh", 4).reshape(-1, r)
     reduced = spread(part, "x", 4).reshape(-1, r)
     grad = product(tt, reduced)
     grad = scattered_sum(grad, "c", 2).astype(BF16)
+    share, grad = lax.optimization_barrier((share, grad))
+    two = back(share, "zh", 4, 2)
     gradient = scattered_sum(grad, ("y", "zl"), 16)
+    two, gradient = lax.optimization_barrier((two, gradient))
 
     new_first = 0.9 * first_moment + 0.1 * gradient
     new_second = 0.999 * second_moment + 0.001 * gradient * gradient
@@ -116,11 +158,9 @@
     second_fix = 1.0 - 0.999**STEP
     direction = (new_first / first_fix / (jnp.sqrt(new_second / second_fix) + 1e-08)).astype(BF16)
     rows = direction.shape[0]
-    directions = spread(direction, ("zh", "x"), 16).reshape(-1, r)
-    out = lax.dot_general(
-        directions, projector, (((1,), (1,)), ((), ())), preferred_element_type=F32
-    ).astype(BF16)
-    out = lay(swap(out.reshape(16, rows, -1), ("zh", "x")))
+    directions = spread(direction, ("x", "c"), 8).reshape(-1, r)
+    out = update_rows(z, directions, (share, one, two, three))
+    out = lay(swap(out.reshape(8, rows, -1), ("x", "c")))
     return (out, new_first, new_second)
 
 

time: 149 us -> 144 us (0.966)
  the two profiles are of different devices: /device:TPU:24 before, /device:TPU:1 now
where the time goes in v13:
time: 144 us; the launch traced here: 142 us
  blocking collectives  74.1 us (51%)
  starting transfers between devices  29.6 us (21%)
  waiting for transfers between devices  23.3 us (16%)
  Pallas kernels  5.79 us (4%)
  other arithmetic  3.05 us (2%)
  local copies, waits for them, and re-layouts  2.94 us (2%)
  matrix products  2.75 us (2%)
    all_to_all x6, blocking collectives, swap(): return lax.all_to_all(parts, axis, 0, 0)  74.1 us
    ppermute x3, starting transfers between devices, back(): return lax.ppermute(block, axis, [(i, (i + k) % n) for i in range(n)])  15.9 us
    all_to_all x2, starting transfers between devices, swap(): return lax.all_to_all(parts, axis, 0, 0)  13.8 us
    all_to_all x2, waiting for transfers between devices, swap(): return lax.all_to_all(parts, axis, 0, 0)  13 us
    ppermute x3, waiting for transfers between devices, back(): return lax.ppermute(block, axis, [(i, (i + k) % n) for i in range(n)])  10.3 us
  transfers between devices with their start and end apart: 5, of which 4 were waited for; matrix products, arithmetic and copies ran while one was open for 1% of the time, Pallas kernels for 1%

profile of v13, /device:TPU:1, one launch (start us, length us, event | category | flops | bytes accessed | tf_op | source)
XLA Modules:
  0.0 142.3 jit_solution(1170023340297943507)
XLA Ops:
  0.7 1.2 copy-done
  1.9 2.7 %convolution_convert_fusion = bf16[1024,512]{1,0:T(8,128)(2,1)} fusion(bf16[1024,512]{1,0:T(8,128)(2,1)S(1)} %copy-done, bf16[512,512]{1,0:T(8,128)(2,1)} %param.7), kind=kOutput, calls=%fused_computation | convolution fusion | flops 537395200 | bytes 2621440 | tf_op jit(solution)/shard_map/dot_general | solution.py:142
  4.6 4.8 %all-to-all-start = ((bf16[4,256,512]{2,1,0:T(8,128)(2,1)}), bf16[4,256,512]{2,1,0:T(8,128)(2,1)}, u32[]{:S(2)}, u32[]{:S(2)}) async-start(bf16[4,256,512]{2,1,0:T(8,128)(2,1)} %bitcast.2), calls=%async_computation | async-start | bytes 2097152 | tf_op jit(solution)/shard_map/all_to_all | solution.py:14
  9.5 10.9 %collective-permute-start.1 = (bf16[256,512]{1,0:T(8,128)(2,1)S(1)}, bf16[256,512]{1,0:T(8,128)(2,1)}, u32[]{:S(2)}, u32[]{:S(2)}) collective-permute-start(bf16[256,512]{1,0:T(8,128)(2,1)S(1)} %constant_dynamic-slice_fusion.refs_0_), channel_id=1, source_target_pairs={{0,384},{128,0},{256,128},{384,256},{1,385},{129,1},{257,129},{385... | collective-permute-start | bytes 786440 | tf_op jit(solution)/shard_map/ppermute | solution.py:33
  20.4 1.9 %collective-permute-start = (bf16[256,512]{1,0:T(8,128)(2,1)S(1)}, bf16[256,512]{1,0:T(8,128)(2,1)}, u32[]{:S(2)}, u32[]{:S(2)}) collective-permute-start(bf16[256,512]{1,0:T(8,128)(2,1)S(1)} %constant_dynamic-slice_fusion.refs_0_), channel_id=1, source_target_pairs={{0,128},{128,256},{256,384},{384,0},{1,129},{129,257},{257,385},{3... | collective-permute-start | bytes 786440 | tf_op jit(solution)/shard_map/ppermute | solution.py:33
  22.4 1.6 %copy-done.1 = bf16[1024,1024]{1,0:T(8,128)(2,1)S(1)} copy-done((bf16[1024,1024]{1,0:T(8,128)(2,1)S(1)}, bf16[1024,1024]{1,0:T(8,128)(2,1)}, u32[]{:S(2)}) %copy-start.1) | copy-done | bytes 2097176
  23.9 1.7 %shard_map.76 = bf16[2,16,32,1024]{3,2,1,0:T(8,128)(2,1)S(1)} custom-call(bf16[1024,1024]{1,0:T(8,128)(2,1)S(1)} %copy-done.1), custom_call_target="tpu_custom_call" | custom-call | bytes 4194304 | tf_op jit(solution)/shard_map/pallas_call | solution.py:49
  25.7 1.3 fusion.1
  27.0 3.9 %collective-permute-done.1.refs_3_ = bf16[256,512]{1,0:T(8,128)(2,1)} collective-permute-done((bf16[256,512]{1,0:T(8,128)(2,1)S(1)}, bf16[256,512]{1,0:T(8,128)(2,1)}, u32[]{:S(2)}, u32[]{:S(2)}) %collective-permute-start.1) | collective-permute-done | bytes 262176 | tf_op jit(solution)/shard_map/ppermute | solution.py:33
  31.4 13.5 %all_to_all.40 = bf16[4,64,512]{2,1,0:T(8,128)(2,1)S(1)} all-to-all(bf16[4,64,512]{2,1,0:T(8,128)(2,1)S(1)} %bitcast.30), channel_id=1, replica_groups=mesh['zh'=4,'x'=4,'y'=8,'zl'=2,'c'=2] {'zh'}, dimensions={0} | all-to-all | bytes 524288 | tf_op jit(solution)/shard_map/all_to_all | solution.py:14
  45.0 10.7 %all_to_all.41 = bf16[4,64,512]{2,1,0:T(8,128)(2,1)S(1)} all-to-all(bf16[4,64,512]{2,1,0:T(8,128)(2,1)S(1)} %broadcast_in_dim.22), channel_id=1, replica_groups=mesh['zh'=4,'x'=4,'y'=8,'zl'=2,'c'=2] {'zh'}, dimensions={0} | all-to-all | bytes 524288 | tf_op jit(solution)/shard_map/all_to_all | solution.py:14
  55.8 13.7 %all_to_all.42 = bf16[4,256,512]{2,1,0:T(8,128)(2,1)S(1)} all-to-all(bf16[4,256,512]{2,1,0:T(8,128)(2,1)S(1)} %broadcast_in_dim.24), channel_id=1, replica_groups=mesh['zh'=4,'x'=4,'y'=8,'zl'=2,'c'=2] {'x'}, dimensions={0} | all-to-all | bytes 2097152 | tf_op jit(solution)/shard_map/all_to_all | solution.py:14
  69.4 1.7 %shard_map.77 = bf16[1024,512]{1,0:T(8,128)(2,1)S(1)} custom-call(bf16[1024,1024]{1,0:T(8,128)(2,1)S(1)} %bitcast.25, bf16[1024,512]{1,0:T(8,128)(2,1)S(1)} %bitcast.26), custom_call_target="tpu_custom_call" | custom-call | flops 1073741824 | bytes 4194304 | tf_op jit(solution)/shard_map/pallas_call | solution.py:79
  71.2 14.0 %all_to_all.43 = bf16[2,512,512]{2,1,0:T(8,128)(2,1)S(1)} all-to-all(bf16[2,512,512]{2,1,0:T(8,128)(2,1)S(1)} %bitcast.27), channel_id=1, replica_groups=mesh['zh'=4,'x'=4,'y'=8,'zl'=2,'c'=2] {'c'}, dimensions={0} | all-to-all | bytes 2097152 | tf_op jit(solution)/shard_map/all_to_all | solution.py:14
  85.2 0.9 fusion
  86.1 8.9 %all-to-all-start.5 = ((bf16[16,32,512]{2,1,0:T(8,128)(2,1)}), bf16[16,32,512]{2,1,0:T(8,128)(2,1)S(1)}, u32[]{:S(2)}, u32[]{:S(2)}) async-start(bf16[16,32,512]{2,1,0:T(8,128)(2,1)} %bitcast.10), calls=%async_computation.5 | async-start | bytes 1048576 | tf_op jit(solution)/shard_map/all_to_all | solution.py:14
  95.0 3.0 %collective-permute-start.2 = (bf16[256,512]{1,0:T(8,128)(2,1)S(1)}, bf16[256,512]{1,0:T(8,128)(2,1)S(1)}, u32[]{:S(2)}, u32[]{:S(2)}) collective-permute-start(bf16[256,512]{1,0:T(8,128)(2,1)S(1)} %constant_dynamic-slice_fusion.refs_0_), channel_id=1, source_target_pairs={{0,256},{128,384},{256,0},{384,128},{1,257},{129,385},{257,1},{385... | collective-permute-start | bytes 786440 | tf_op jit(solution)/shard_map/ppermute | solution.py:33
  98.1 13.0 %all-to-all-done.5 = bf16[16,32,512]{2,1,0:T(8,128)(2,1)S(1)} async-done(((bf16[16,32,512]{2,1,0:T(8,128)(2,1)}), bf16[16,32,512]{2,1,0:T(8,128)(2,1)S(1)}, u32[]{:S(2)}, u32[]{:S(2)}) %all-to-all-start.5) | async-done | bytes 524320 | tf_op jit(solution)/shard_map/all_to_all | solution.py:14
  111.1 5.9 %collective-permute-done.2.refs_2_ = bf16[256,512]{1,0:T(8,128)(2,1)S(1)} collective-permute-done((bf16[256,512]{1,0:T(8,128)(2,1)S(1)}, bf16[256,512]{1,0:T(8,128)(2,1)S(1)}, u32[]{:S(2)}, u32[]{:S(2)}) %collective-permute-start.2) | collective-permute-done | bytes 262176 | tf_op jit(solution)/shard_map/ppermute | solution.py:33
  117.0 0.7 divide_convert_fusion
  117.7 9.4 %all_to_all.44 = bf16[8,32,512]{2,1,0:T(8,128)(2,1)S(1)} all-to-all(bf16[8,32,512]{2,1,0:T(8,128)(2,1)S(1)} %broadcast_in_dim.25), channel_id=1, replica_groups=mesh['zh'=4,'x'=4,'y'=8,'zl'=2,'c'=2] {'x','c'}, dimensions={0} | all-to-all | bytes 524288 | tf_op jit(solution)/shard_map/all_to_all | solution.py:14
  127.1 1.5 %shard_map.78 = bf16[256,1024]{1,0:T(8,128)(2,1)S(1)} custom-call(s32[1]{0:T(128)} %bitcast.z_ref, bf16[256,512]{1,0:T(8,128)(2,1)S(1)} %bitcast.29, bf16[256,512]{1,0:T(8,128)(2,1)S(1)} %constant_dynamic-slice_fusion.refs_0_, bf16[256,512]{1,0:T(8,128)(2,1)} %collective-permute-done.refs_1_, bf16[256,512]{1,0:T(8,128)(2,1)S(1)} %collective-permute-done.2.refs_2_, ...), custom_call_target="tpu_custom_call" | custom-call | flops 268435456 | bytes 1835008 | tf_op jit(solution)/shard_map/pallas_call | solution.py:103
  128.6 12.8 %all_to_all.45.in_ref = bf16[8,32,1024]{2,1,0:T(8,128)(2,1)S(1)} all-to-all(bf16[8,32,1024]{2,1,0:T(8,128)(2,1)S(1)} %bitcast.28), channel_id=1, replica_groups=mesh['zh'=4,'x'=4,'y'=8,'zl'=2,'c'=2] {'x','c'}, dimensions={0} | all-to-all | bytes 1048576 | tf_op jit(solution)/shard_map/all_to_all | solution.py:14
  141.4 0.8 shard_map.79
  (16 shorter events, 0.8 us)
Async XLA Ops:
  0.6 1.2 copy-start
  0.6 8.8 %copy-start.2 = (bf16[512,512]{1,0:T(8,128)(2,1)S(1)}, bf16[512,512]{1,0:T(8,128)(2,1)}, u32[]{:S(2)}) copy-start(bf16[512,512]{1,0:T(8,128)(2,1)} %param.7) | copy-start | bytes 1572868
  4.6 21.1 %all-to-all-start = ((bf16[4,256,512]{2,1,0:T(8,128)(2,1)}), bf16[4,256,512]{2,1,0:T(8,128)(2,1)}, u32[]{:S(2)}, u32[]{:S(2)}) async-start(bf16[4,256,512]{2,1,0:T(8,128)(2,1)} %bitcast.2), calls=%async_computation | async-start | bytes 2097152 | tf_op jit(solution)/shard_map/all_to_all | solution.py:14
  9.5 21.5 %collective-permute-start.1 = (bf16[256,512]{1,0:T(8,128)(2,1)S(1)}, bf16[256,512]{1,0:T(8,128)(2,1)}, u32[]{:S(2)}, u32[]{:S(2)}) collective-permute-start(bf16[256,512]{1,0:T(8,128)(2,1)S(1)} %constant_dynamic-slice_fusion.refs_0_), channel_id=1, source_target_pairs={{0,384},{128,0},{256,128},{384,256},{1,385},{129,1},{257,129},{385... | collective-permute-start | bytes 786440 | tf_op jit(solution)/shard_map/ppermute | solution.py:33
  20.4 11.0 %collective-permute-start = (bf16[256,512]{1,0:T(8,128)(2,1)S(1)}, bf16[256,512]{1,0:T(8,128)(2,1)}, u32[]{:S(2)}, u32[]{:S(2)}) collective-permute-start(bf16[256,512]{1,0:T(8,128)(2,1)S(1)} %constant_dynamic-slice_fusion.refs_0_), channel_id=1, source_target_pairs={{0,128},{128,256},{256,384},{384,0},{1,129},{129,257},{257,385},{3... | collective-permute-start | bytes 786440 | tf_op jit(solution)/shard_map/ppermute | solution.py:33
  22.3 1.6 %copy-start.1 = (bf16[1024,1024]{1,0:T(8,128)(2,1)S(1)}, bf16[1024,1024]{1,0:T(8,128)(2,1)}, u32[]{:S(2)}) copy-start(bf16[1024,1024]{1,0:T(8,128)(2,1)} %in_ref.1) | copy-start | bytes 6291460
  85.2 31.8 %copy-start.3 = (f32[32,512]{1,0:T(8,128)S(1)}, f32[32,512]{1,0:T(8,128)}, u32[]{:S(2)}) copy-start(f32[32,512]{1,0:T(8,128)} %param.8) | copy-start | bytes 196612
  85.2 31.8 %copy-start.4 = (f32[32,512]{1,0:T(8,128)S(1)}, f32[32,512]{1,0:T(8,128)}, u32[]{:S(2)}) copy-start(f32[32,512]{1,0:T(8,128)} %param.9) | copy-start | bytes 196612
  86.1 24.9 %all-to-all-start.5 = ((bf16[16,32,512]{2,1,0:T(8,128)(2,1)}), bf16[16,32,512]{2,1,0:T(8,128)(2,1)S(1)}, u32[]{:S(2)}, u32[]{:S(2)}) async-start(bf16[16,32,512]{2,1,0:T(8,128)(2,1)} %bitcast.10), calls=%async_computation.5 | async-start | bytes 1048576 | tf_op jit(solution)/shard_map/all_to_all | solution.py:14
  95.0 21.9 %collective-permute-start.2 = (bf16[256,512]{1,0:T(8,128)(2,1)S(1)}, bf16[256,512]{1,0:T(8,128)(2,1)S(1)}, u32[]{:S(2)}, u32[]{:S(2)}) collective-permute-start(bf16[256,512]{1,0:T(8,128)(2,1)S(1)} %constant_dynamic-slice_fusion.refs_0_), channel_id=1, source_target_pairs={{0,256},{128,384},{256,0},{384,128},{1,257},{129,385},{257,1},{385... | collective-permute-start | bytes 786440 | tf_op jit(solution)/shard_map/ppermute | solution.py:33

commit v14 on v13

--- a/solution.py
+++ b/solution.py
@@ -147,10 +147,9 @@
     reduced = spread(part, "x", 4).reshape(-1, r)
     grad = product(tt, reduced)
     grad = scattered_sum(grad, "c", 2).astype(BF16)
-    share, grad = lax.optimization_barrier((share, grad))
-    two = back(share, "zh", 4, 2)
+    one, grad = lax.optimization_barrier((one, grad))
+    two = back(one, "zh", 4, 1)
     gradient = scattered_sum(grad, ("y", "zl"), 16)
-    two, gradient = lax.optimization_barrier((two, gradient))
 
     new_first = 0.9 * first_moment + 0.1 * gradient
     new_second = 0.999 * second_moment + 0.001 * gradient * gradient
@@ -159,6 +158,7 @@
     direction = (new_first / first_fix / (jnp.sqrt(new_second / second_fix) + 1e-08)).astype(BF16)
     rows = direction.shape[0]
     directions = spread(direction, ("x", "c"), 8).reshape(-1, r)
+    two, directions = lax.optimization_barrier((two, directions))
     out = update_rows(z, directions, (share, one, two, three))
     out = lay(swap(out.reshape(8, rows, -1), ("x", "c")))
     return (out, new_first, new_second)

time: 144 us -> 141 us (0.979)
  blocking collectives: 74.1 us -> 64.8 us
  starting transfers between devices: 29.6 us -> 35.8 us
    all_to_all x6 -> x5, blocking collectives: 74.1 us -> 64.8 us  [swap(): return lax.all_to_all(parts, axis, 0, 0)]
    all_to_all x2 -> x3, waiting for transfers between devices: 13 us -> 19.2 us  [swap(): return lax.all_to_all(parts, axis, 0, 0)]
    all_to_all x2 -> x3, starting transfers between devices: 13.8 us -> 19.6 us  [swap(): return lax.all_to_all(parts, axis, 0, 0)]
    ppermute x3, waiting for transfers between devices: 10.3 us -> 4.43 us  [back(): return lax.ppermute(block, axis, [(i, (i + k) % n) for i in range(n)])]
  transfers between devices with their start and end apart: 5 -> 6, of which waited for: 4 -> 4; matrix products, arithmetic and copies ran while one was open for 1% -> 2% of each run, Pallas kernels for 1% -> 1%
where the time goes in v14:
time: 141 us; the launch traced here: 140 us
  blocking collectives  64.8 us (46%)
  starting transfers between devices  35.8 us (25%)
  waiting for transfers between devices  23.7 us (17%)
  Pallas kernels  5.79 us (4%)
  local copies, waits for them, and re-layouts  3.65 us (3%)
  other arithmetic  3.04 us (2%)
  matrix products  2.74 us (2%)
    all_to_all x5, blocking collectives, swap(): return lax.all_to_all(parts, axis, 0, 0)  64.8 us
    all_to_all x3, starting transfers between devices, swap(): return lax.all_to_all(parts, axis, 0, 0)  19.6 us
    all_to_all x3, waiting for transfers between devices, swap(): return lax.all_to_all(parts, axis, 0, 0)  19.2 us
    ppermute x3, starting transfers between devices, back(): return lax.ppermute(block, axis, [(i, (i + k) % n) for i in range(n)])  16.1 us
    ppermute x3, waiting for transfers between devices, back(): return lax.ppermute(block, axis, [(i, (i + k) % n) for i in range(n)])  4.43 us
  transfers between devices with their start and end apart: 6, of which 4 were waited for; matrix products, arithmetic and copies ran while one was open for 2% of the time, Pallas kernels for 1%

profile of v14, /device:TPU:1, one launch (start us, length us, event | category | flops | bytes accessed | tf_op | source)
XLA Modules:
  0.0 140.2 jit_solution(7041832848709145378)
XLA Ops:
  0.7 1.2 copy-done
  1.9 2.7 %convolution_convert_fusion = bf16[1024,512]{1,0:T(8,128)(2,1)} fusion(bf16[1024,512]{1,0:T(8,128)(2,1)S(1)} %copy-done, bf16[512,512]{1,0:T(8,128)(2,1)} %param.7), kind=kOutput, calls=%fused_computation | convolution fusion | flops 537395200 | bytes 2621440 | tf_op jit(solution)/shard_map/dot_general | solution.py:142
  4.6 4.8 %all-to-all-start = ((bf16[4,256,512]{2,1,0:T(8,128)(2,1)}), bf16[4,256,512]{2,1,0:T(8,128)(2,1)}, u32[]{:S(2)}, u32[]{:S(2)}) async-start(bf16[4,256,512]{2,1,0:T(8,128)(2,1)} %bitcast.2), calls=%async_computation | async-start | bytes 2097152 | tf_op jit(solution)/shard_map/all_to_all | solution.py:14
  9.5 10.9 %collective-permute-start.1 = (bf16[256,512]{1,0:T(8,128)(2,1)S(1)}, bf16[256,512]{1,0:T(8,128)(2,1)}, u32[]{:S(2)}, u32[]{:S(2)}) collective-permute-start(bf16[256,512]{1,0:T(8,128)(2,1)S(1)} %constant_dynamic-slice_fusion.refs_0_), channel_id=1, source_target_pairs={{0,384},{128,0},{256,128},{384,256},{1,385},{129,1},{257,129},{385... | collective-permute-start | bytes 786440 | tf_op jit(solution)/shard_map/ppermute | solution.py:33
  20.4 1.9 %collective-permute-start = (bf16[256,512]{1,0:T(8,128)(2,1)S(1)}, bf16[256,512]{1,0:T(8,128)(2,1)}, u32[]{:S(2)}, u32[]{:S(2)}) collective-permute-start(bf16[256,512]{1,0:T(8,128)(2,1)S(1)} %constant_dynamic-slice_fusion.refs_0_), channel_id=1, source_target_pairs={{0,128},{128,256},{256,384},{384,0},{1,129},{129,257},{257,385},{3... | collective-permute-start | bytes 786440 | tf_op jit(solution)/shard_map/ppermute | solution.py:33
  22.3 1.6 %copy-done.1 = bf16[1024,1024]{1,0:T(8,128)(2,1)S(1)} copy-done((bf16[1024,1024]{1,0:T(8,128)(2,1)S(1)}, bf16[1024,1024]{1,0:T(8,128)(2,1)}, u32[]{:S(2)}) %copy-start.1) | copy-done | bytes 2097176
  23.9 1.7 %shard_map.76 = bf16[2,16,32,1024]{3,2,1,0:T(8,128)(2,1)S(1)} custom-call(bf16[1024,1024]{1,0:T(8,128)(2,1)S(1)} %copy-done.1), custom_call_target="tpu_custom_call" | custom-call | bytes 4194304 | tf_op jit(solution)/shard_map/pallas_call | solution.py:49
  25.7 1.3 fusion.1
  27.0 3.9 %collective-permute-done.1.refs_3_ = bf16[256,512]{1,0:T(8,128)(2,1)} collective-permute-done((bf16[256,512]{1,0:T(8,128)(2,1)S(1)}, bf16[256,512]{1,0:T(8,128)(2,1)}, u32[]{:S(2)}, u32[]{:S(2)}) %collective-permute-start.1) | collective-permute-done | bytes 262176 | tf_op jit(solution)/shard_map/ppermute | solution.py:33
  31.4 13.5 %all_to_all.40 = bf16[4,64,512]{2,1,0:T(8,128)(2,1)S(1)} all-to-all(bf16[4,64,512]{2,1,0:T(8,128)(2,1)S(1)} %bitcast.30), channel_id=1, replica_groups=mesh['zh'=4,'x'=4,'y'=8,'zl'=2,'c'=2] {'zh'}, dimensions={0} | all-to-all | bytes 524288 | tf_op jit(solution)/shard_map/all_to_all | solution.py:14
  45.0 10.7 %all_to_all.41 = bf16[4,64,512]{2,1,0:T(8,128)(2,1)S(1)} all-to-all(bf16[4,64,512]{2,1,0:T(8,128)(2,1)S(1)} %broadcast_in_dim.22), channel_id=1, replica_groups=mesh['zh'=4,'x'=4,'y'=8,'zl'=2,'c'=2] {'zh'}, dimensions={0} | all-to-all | bytes 524288 | tf_op jit(solution)/shard_map/all_to_all | solution.py:14
  55.8 13.7 %all_to_all.42 = bf16[4,256,512]{2,1,0:T(8,128)(2,1)S(1)} all-to-all(bf16[4,256,512]{2,1,0:T(8,128)(2,1)S(1)} %broadcast_in_dim.24), channel_id=1, replica_groups=mesh['zh'=4,'x'=4,'y'=8,'zl'=2,'c'=2] {'x'}, dimensions={0} | all-to-all | bytes 2097152 | tf_op jit(solution)/shard_map/all_to_all | solution.py:14
  69.4 1.7 %shard_map.77 = bf16[1024,512]{1,0:T(8,128)(2,1)S(1)} custom-call(bf16[1024,1024]{1,0:T(8,128)(2,1)S(1)} %bitcast.25, bf16[1024,512]{1,0:T(8,128)(2,1)S(1)} %bitcast.26), custom_call_target="tpu_custom_call" | custom-call | flops 1073741824 | bytes 4194304 | tf_op jit(solution)/shard_map/pallas_call | solution.py:79
  71.2 14.1 %all_to_all.43 = bf16[2,512,512]{2,1,0:T(8,128)(2,1)S(1)} all-to-all(bf16[2,512,512]{2,1,0:T(8,128)(2,1)S(1)} %bitcast.27), channel_id=1, replica_groups=mesh['zh'=4,'x'=4,'y'=8,'zl'=2,'c'=2] {'c'}, dimensions={0} | all-to-all | bytes 2097152 | tf_op jit(solution)/shard_map/all_to_all | solution.py:14
  85.3 0.9 fusion
  86.3 8.9 %all-to-all-start.5 = ((bf16[16,32,512]{2,1,0:T(8,128)(2,1)}), bf16[16,32,512]{2,1,0:T(8,128)(2,1)S(1)}, u32[]{:S(2)}, u32[]{:S(2)}) async-start(bf16[16,32,512]{2,1,0:T(8,128)(2,1)} %bitcast.10), calls=%async_computation.5 | async-start | bytes 1048576 | tf_op jit(solution)/shard_map/all_to_all | solution.py:14
  95.2 3.3 %collective-permute-start.2 = (bf16[256,512]{1,0:T(8,128)(2,1)}, bf16[256,512]{1,0:T(8,128)(2,1)S(1)}, u32[]{:S(2)}, u32[]{:S(2)}) collective-permute-start(bf16[256,512]{1,0:T(8,128)(2,1)} %collective-permute-done.refs_1_), channel_id=1, source_target_pairs={{0,128},{128,256},{256,384},{384,0},{1,129},{129,257},{257,385},{3... | collective-permute-start | bytes 786440 | tf_op jit(solution)/shard_map/ppermute | solution.py:33
  98.5 12.7 %all-to-all-done.5 = bf16[16,32,512]{2,1,0:T(8,128)(2,1)S(1)} async-done(((bf16[16,32,512]{2,1,0:T(8,128)(2,1)}), bf16[16,32,512]{2,1,0:T(8,128)(2,1)S(1)}, u32[]{:S(2)}, u32[]{:S(2)}) %all-to-all-start.5) | async-done | bytes 524320 | tf_op jit(solution)/shard_map/all_to_all | solution.py:14
  111.2 0.8 divide_convert_fusion
  112.7 5.9 %all-to-all-start.6 = ((bf16[8,32,512]{2,1,0:T(8,128)(2,1)}), bf16[8,32,512]{2,1,0:T(8,128)(2,1)S(1)}, u32[]{:S(2)}, u32[]{:S(2)}) async-start(bf16[8,32,512]{2,1,0:T(8,128)(2,1)} %broadcast_in_dim.25), calls=%async_computation.6 | async-start | bytes 524288 | tf_op jit(solution)/shard_map/all_to_all | solution.py:14
  118.6 6.5 %all-to-all-done.6 = bf16[8,32,512]{2,1,0:T(8,128)(2,1)S(1)} async-done(((bf16[8,32,512]{2,1,0:T(8,128)(2,1)}), bf16[8,32,512]{2,1,0:T(8,128)(2,1)S(1)}, u32[]{:S(2)}, u32[]{:S(2)}) %all-to-all-start.6) | async-done | bytes 262176 | tf_op jit(solution)/shard_map/all_to_all | solution.py:14
  125.1 1.5 %shard_map.78 = bf16[256,1024]{1,0:T(8,128)(2,1)S(1)} custom-call(s32[1]{0:T(128)} %bitcast.z_ref, bf16[256,512]{1,0:T(8,128)(2,1)S(1)} %bitcast.29, bf16[256,512]{1,0:T(8,128)(2,1)S(1)} %constant_dynamic-slice_fusion.refs_0_, bf16[256,512]{1,0:T(8,128)(2,1)} %collective-permute-done.refs_1_, bf16[256,512]{1,0:T(8,128)(2,1)S(1)} %collective-permute-done.2.refs_2_, ...), custom_call_target="tpu_custom_call" | custom-call | flops 268435456 | bytes 1835008 | tf_op jit(solution)/shard_map/pallas_call | solution.py:103
  126.6 12.8 %all_to_all.44.in_ref = bf16[8,32,1024]{2,1,0:T(8,128)(2,1)S(1)} all-to-all(bf16[8,32,1024]{2,1,0:T(8,128)(2,1)S(1)} %bitcast.28), channel_id=1, replica_groups=mesh['zh'=4,'x'=4,'y'=8,'zl'=2,'c'=2] {'x','c'}, dimensions={0} | all-to-all | bytes 1048576 | tf_op jit(solution)/shard_map/all_to_all | solution.py:14
  139.4 0.8 shard_map.79
  (16 shorter events, 1.4 us)
Async XLA Ops:
  0.6 1.2 copy-start
  0.6 8.8 %copy-start.2 = (bf16[512,512]{1,0:T(8,128)(2,1)S(1)}, bf16[512,512]{1,0:T(8,128)(2,1)}, u32[]{:S(2)}) copy-start(bf16[512,512]{1,0:T(8,128)(2,1)} %param.7) | copy-start | bytes 1572868
  4.6 21.1 %all-to-all-start = ((bf16[4,256,512]{2,1,0:T(8,128)(2,1)}), bf16[4,256,512]{2,1,0:T(8,128)(2,1)}, u32[]{:S(2)}, u32[]{:S(2)}) async-start(bf16[4,256,512]{2,1,0:T(8,128)(2,1)} %bitcast.2), calls=%async_computation | async-start | bytes 2097152 | tf_op jit(solution)/shard_map/all_to_all | solution.py:14
  9.5 21.5 %collective-permute-start.1 = (bf16[256,512]{1,0:T(8,128)(2,1)S(1)}, bf16[256,512]{1,0:T(8,128)(2,1)}, u32[]{:S(2)}, u32[]{:S(2)}) collective-permute-start(bf16[256,512]{1,0:T(8,128)(2,1)S(1)} %constant_dynamic-slice_fusion.refs_0_), channel_id=1, source_target_pairs={{0,384},{128,0},{256,128},{384,256},{1,385},{129,1},{257,129},{385... | collective-permute-start | bytes 786440 | tf_op jit(solution)/shard_map/ppermute | solution.py:33
  20.4 11.0 %collective-permute-start = (bf16[256,512]{1,0:T(8,128)(2,1)S(1)}, bf16[256,512]{1,0:T(8,128)(2,1)}, u32[]{:S(2)}, u32[]{:S(2)}) collective-permute-start(bf16[256,512]{1,0:T(8,128)(2,1)S(1)} %constant_dynamic-slice_fusion.refs_0_), channel_id=1, source_target_pairs={{0,128},{128,256},{256,384},{384,0},{1,129},{129,257},{257,385},{3... | collective-permute-start | bytes 786440 | tf_op jit(solution)/shard_map/ppermute | solution.py:33
  22.3 1.6 %copy-start.1 = (bf16[1024,1024]{1,0:T(8,128)(2,1)S(1)}, bf16[1024,1024]{1,0:T(8,128)(2,1)}, u32[]{:S(2)}) copy-start(bf16[1024,1024]{1,0:T(8,128)(2,1)} %in_ref.1) | copy-start | bytes 6291460
  71.2 40.0 %copy-start.3 = (f32[32,512]{1,0:T(8,128)S(1)}, f32[32,512]{1,0:T(8,128)}, u32[]{:S(2)}) copy-start(f32[32,512]{1,0:T(8,128)} %param.8) | copy-start | bytes 196612
  71.2 40.0 %copy-start.4 = (f32[32,512]{1,0:T(8,128)S(1)}, f32[32,512]{1,0:T(8,128)}, u32[]{:S(2)}) copy-start(f32[32,512]{1,0:T(8,128)} %param.9) | copy-start | bytes 196612
  86.3 24.9 %all-to-all-start.5 = ((bf16[16,32,512]{2,1,0:T(8,128)(2,1)}), bf16[16,32,512]{2,1,0:T(8,128)(2,1)S(1)}, u32[]{:S(2)}, u32[]{:S(2)}) async-start(bf16[16,32,512]{2,1,0:T(8,128)(2,1)} %bitcast.10), calls=%async_computation.5 | async-start | bytes 1048576 | tf_op jit(solution)/shard_map/all_to_all | solution.py:14
  95.2 23.4 %collective-permute-start.2 = (bf16[256,512]{1,0:T(8,128)(2,1)}, bf16[256,512]{1,0:T(8,128)(2,1)S(1)}, u32[]{:S(2)}, u32[]{:S(2)}) collective-permute-start(bf16[256,512]{1,0:T(8,128)(2,1)} %collective-permute-done.refs_1_), channel_id=1, source_target_pairs={{0,128},{128,256},{256,384},{384,0},{1,129},{129,257},{257,385},{3... | collective-permute-start | bytes 786440 | tf_op jit(solution)/shard_map/ppermute | solution.py:33
  112.7 12.4 %all-to-all-start.6 = ((bf16[8,32,512]{2,1,0:T(8,128)(2,1)}), bf16[8,32,512]{2,1,0:T(8,128)(2,1)S(1)}, u32[]{:S(2)}, u32[]{:S(2)}) async-start(bf16[8,32,512]{2,1,0:T(8,128)(2,1)} %broadcast_in_dim.25), calls=%async_computation.6 | async-start | bytes 524288 | tf_op jit(solution)/shard_map/all_to_all | solution.py:14

commit v15 on v14

--- a/solution.py
+++ b/solution.py
@@ -1,3 +1,5 @@
+import functools
+
 import jax
 import jax.numpy as jnp
 from jax import lax
@@ -33,38 +35,42 @@
     return lax.ppermute(block, axis, [(i, (i + k) % n) for i in range(n)])
 
 
-def turn_kernel(in_ref, out_ref):
+def turn_kernel(core_ref, in_ref, out_ref):
     turned = in_ref[...].T
     rows = out_ref.shape[2]
     for i in range(out_ref.shape[1]):
         for c in range(2):
             at = (2 * i + c) * rows
-            out_ref[c, i] = turned[at : at + rows]
+            out_ref[lax.rem(c + core_ref[0], 2), i] = turned[at : at + rows]
 
 
-def turn(tangent):
+def turn(core, tangent):
     tokens, hidden = tangent.shape
     rows = hidden // 32
     step = 128 // (2 * rows)
     out = pl.pallas_call(
         turn_kernel,
         grid=(hidden // 128,),
-        in_specs=[pl.BlockSpec((tokens, 128), lambda i: (0, i))],
+        in_specs=[
+            pl.BlockSpec(memory_space=pltpu.SMEM),
+            pl.BlockSpec((tokens, 128), lambda i: (0, i)),
+        ],
         out_specs=pl.BlockSpec((2, step, rows, tokens), lambda i: (0, i, 0, 0)),
         out_shape=jax.ShapeDtypeStruct((2, 16, rows, tokens), tangent.dtype),
         cost_estimate=pl.CostEstimate(flops=0, bytes_accessed=4 * tokens * hidden, transcendentals=0),
         compiler_params=pltpu.CompilerParams(vmem_limit_bytes=16 * 2**20),
-    )(tangent)
-    return out.reshape(hidden, tokens)
+    )(core, tangent)
+    return out.reshape(2, hidden // 2, tokens)
 
 
-def product_kernel(a_ref, b_ref, out_ref):
+def product_kernel(part, a_ref, b_ref, out_ref):
     step = 256
 
-    @pl.loop(0, a_ref.shape[0] // step)
+    @pl.loop(0, a_ref.shape[1] // step)
     def _(i):
         at = pl.ds(pl.multiple_of(i * step, step), step)
-        out_ref[at] = jnp.dot(a_ref[at], b_ref[...], preferred_element_type=F32).astype(BF16)
+        total = jnp.dot(a_ref[part, at], b_ref[...], preferred_element_type=F32)
+        out_ref[at] = total.astype(out_ref.dtype)
 
 
 def cost(m, k, n):
@@ -73,14 +79,14 @@
     )
 
 
-def product(a, b):
+def product(a, part, b, dtype):
     vmem = pl.BlockSpec(memory_space=pltpu.VMEM)
-    m, k, n = a.shape[0], a.shape[1], b.shape[1]
+    m, k, n = a.shape[1], a.shape[2], b.shape[1]
     return pl.pallas_call(
-        product_kernel,
+        functools.partial(product_kernel, part),
         in_specs=[vmem, vmem],
         out_specs=vmem,
-        out_shape=jax.ShapeDtypeStruct((m, n), BF16),
+        out_shape=jax.ShapeDtypeStruct((m, n), dtype),
         cost_estimate=cost(m, k, n),
         compiler_params=pltpu.CompilerParams(vmem_limit_bytes=16 * 2**20),
     )(a, b)
@@ -135,7 +141,8 @@
 def local(tokens, tangent, projector, first_moment, second_moment):
     r = projector.shape[1]
     z = lax.axis_index("zh").reshape(1).astype(jnp.int32)
-    tt = turn(tangent)
+    core = lax.axis_index("c").reshape(1).astype(jnp.int32)
+    tt = turn(core, tangent)
     half = projector.shape[0] // 2
     share = lax.dynamic_slice_in_dim(projector, lax.axis_index("c") * half, half, 0)
     one, three = back(share, "zh", 4, 1), back(share, "zh", 4, 3)
@@ -143,10 +150,9 @@
     part = scattered_sum(part, "x", 4).astype(BF16)
     z, one, three, tt, share, part = lax.optimization_barrier((z, one, three, tt, share, part))
     part = scattered_sum(part, "zh", 4).astype(BF16)
-    part = spread(part, "zh", 4).reshape(-1, r)
-    reduced = spread(part, "x", 4).reshape(-1, r)
-    grad = product(tt, reduced)
-    grad = scattered_sum(grad, "c", 2).astype(BF16)
+    reduced = spread(part, ("x", "zh"), 16).reshape(-1, r)
+    others = lax.ppermute(product(tt, 1, reduced, BF16), "c", [(0, 1), (1, 0)])
+    grad = (product(tt, 0, reduced, F32) + others.astype(F32)).astype(BF16)
     one, grad = lax.optimization_barrier((one, grad))
     two = back(one, "zh", 4, 1)
     gradient = scattered_sum(grad, ("y", "zl"), 16)

time: 141 us -> 140 us (level)
  blocking collectives: 64.8 us -> 47.4 us
  starting transfers between devices: 35.8 us -> 52.7 us
    all_to_all x5 -> x3, blocking collectives: 64.8 us -> 47.4 us  [swap(): return lax.all_to_all(parts, axis, 0, 0)]
    ppermute x0 -> x1, starting transfers between devices: none -> 16.5 us  [local(): others = lax.ppermute(product(tt, 1, reduced, BF16), 'c', [(0, 1), (1, 0)])]
    all_to_all x3, waiting for transfers between devices: 19.2 us -> 17.8 us  [swap(): return lax.all_to_all(parts, axis, 0, 0)]
  transfers between devices with their start and end apart: 6 -> 7, of which waited for: 4 -> 5; matrix products, arithmetic and copies ran while one was open for 2% -> 2% of each run, Pallas kernels for 1% -> 2%
where the time goes in v15:
time: 140 us; the launch traced here: 139 us
  starting transfers between devices  52.7 us (38%)
  blocking collectives  47.4 us (34%)
  waiting for transfers between devices  22.8 us (16%)
  Pallas kernels  5.84 us (4%)
  local copies, waits for them, and re-layouts  3.65 us (3%)
  other arithmetic  3.07 us (2%)
  matrix products  2.74 us (2%)
    all_to_all x3, blocking collectives, swap(): return lax.all_to_all(parts, axis, 0, 0)  47.4 us
    all_to_all x3, starting transfers between devices, swap(): return lax.all_to_all(parts, axis, 0, 0)  18.7 us
    all_to_all x3, waiting for transfers between devices, swap(): return lax.all_to_all(parts, axis, 0, 0)  17.8 us
    ppermute x3, starting transfers between devices, back(): return lax.ppermute(block, axis, [(i, (i + k) % n) for i in range(n)])  17.5 us
    ppermute x1, starting transfers between devices, local(): others = lax.ppermute(product(tt, 1, reduced, BF16), 'c', [(0, 1), (1, 0)])  16.5 us
    ppermute x3, waiting for transfers between devices, back(): return lax.ppermute(block, axis, [(i, (i + k) % n) for i in range(n)])  4.37 us
    unnamed x10, local copies, waits for them, and re-layouts  2.82 us
  transfers between devices with their start and end apart: 7, of which 5 were waited for; matrix products, arithmetic and copies ran while one was open for 2% of the time, Pallas kernels for 2%

profile of v15, /device:TPU:1, one launch (start us, length us, event | category | flops | bytes accessed | tf_op | source)
XLA Modules:
  0.0 139.0 jit_solution(10651866165875836217)
XLA Ops:
  0.7 1.2 copy-done
  1.9 2.7 %convolution_convert_fusion = bf16[1024,512]{1,0:T(8,128)(2,1)} fusion(bf16[1024,512]{1,0:T(8,128)(2,1)S(1)} %copy-done, bf16[512,512]{1,0:T(8,128)(2,1)} %param.7), kind=kOutput, calls=%fused_computation | convolution fusion | flops 537395200 | bytes 2621440 | tf_op jit(solution)/shard_map/dot_general | solution.py:149
  4.6 4.8 %all-to-all-start = ((bf16[4,256,512]{2,1,0:T(8,128)(2,1)}), bf16[4,256,512]{2,1,0:T(8,128)(2,1)}, u32[]{:S(2)}, u32[]{:S(2)}) async-start(bf16[4,256,512]{2,1,0:T(8,128)(2,1)} %bitcast.3), calls=%async_computation | async-start | bytes 2097152 | tf_op jit(solution)/shard_map/all_to_all | solution.py:16
  9.5 10.9 %collective-permute-start.1 = (bf16[256,512]{1,0:T(8,128)(2,1)S(1)}, bf16[256,512]{1,0:T(8,128)(2,1)}, u32[]{:S(2)}, u32[]{:S(2)}) collective-permute-start(bf16[256,512]{1,0:T(8,128)(2,1)S(1)} %constant_dynamic-slice_fusion.refs_0_), channel_id=1, source_target_pairs={{0,384},{128,0},{256,128},{384,256},{1,385},{129,1},{257,129},{385... | collective-permute-start | bytes 786440 | tf_op jit(solution)/shard_map/ppermute | solution.py:35
  20.4 1.9 %collective-permute-start = (bf16[256,512]{1,0:T(8,128)(2,1)S(1)}, bf16[256,512]{1,0:T(8,128)(2,1)}, u32[]{:S(2)}, u32[]{:S(2)}) collective-permute-start(bf16[256,512]{1,0:T(8,128)(2,1)S(1)} %constant_dynamic-slice_fusion.refs_0_), channel_id=1, source_target_pairs={{0,128},{128,256},{256,384},{384,0},{1,129},{129,257},{257,385},{3... | collective-permute-start | bytes 786440 | tf_op jit(solution)/shard_map/ppermute | solution.py:35
  22.3 1.6 %copy-done.1 = bf16[1024,1024]{1,0:T(8,128)(2,1)S(1)} copy-done((bf16[1024,1024]{1,0:T(8,128)(2,1)S(1)}, bf16[1024,1024]{1,0:T(8,128)(2,1)}, u32[]{:S(2)}) %copy-start.1) | copy-done | bytes 2097176
  23.9 1.8 %shard_map.76 = bf16[2,16,32,1024]{3,2,1,0:T(8,128)(2,1)S(1)} custom-call(s32[1]{0:T(128)} %bitcast.1.core_ref, bf16[1024,1024]{1,0:T(8,128)(2,1)S(1)} %copy-done.1), custom_call_target="tpu_custom_call" | custom-call | bytes 4194304 | tf_op jit(solution)/shard_map/pallas_call | solution.py:51
  25.7 1.3 fusion
  27.0 3.9 %collective-permute-done.1.refs_3_ = bf16[256,512]{1,0:T(8,128)(2,1)} collective-permute-done((bf16[256,512]{1,0:T(8,128)(2,1)S(1)}, bf16[256,512]{1,0:T(8,128)(2,1)}, u32[]{:S(2)}, u32[]{:S(2)}) %collective-permute-start.1) | collective-permute-done | bytes 262176 | tf_op jit(solution)/shard_map/ppermute | solution.py:35
  31.4 13.5 %all_to_all.30 = bf16[4,64,512]{2,1,0:T(8,128)(2,1)S(1)} all-to-all(bf16[4,64,512]{2,1,0:T(8,128)(2,1)S(1)} %bitcast.28), channel_id=1, replica_groups=mesh['zh'=4,'x'=4,'y'=8,'zl'=2,'c'=2] {'zh'}, dimensions={0} | all-to-all | bytes 524288 | tf_op jit(solution)/shard_map/all_to_all | solution.py:16
  45.1 21.1 %all_to_all.31 = bf16[16,64,512]{2,1,0:T(8,128)(2,1)S(1)} all-to-all(bf16[16,64,512]{2,1,0:T(8,128)(2,1)S(1)} %broadcast_in_dim.7), channel_id=1, replica_groups=mesh['zh'=4,'x'=4,'y'=8,'zl'=2,'c'=2] {'x','zh'}, dimensions={0} | all-to-all | bytes 2097152 | tf_op jit(solution)/shard_map/all_to_all | solution.py:16
  66.2 0.9 shard_map.78
  67.0 16.5 %collective-permute-start.2 = (bf16[512,512]{1,0:T(8,128)(2,1)S(1)}, bf16[512,512]{1,0:T(8,128)(2,1)S(1)}, u32[]{:S(2)}, u32[]{:S(2)}) collective-permute-start(bf16[512,512]{1,0:T(8,128)(2,1)S(1)} %shard_map.78), channel_id=1, source_target_pairs={{0,1},{1,0},{2,3},{3,2},{4,5},{5,4},{6,7},{7,6},{8,9},{9,8},{10,11... | collective-permute-start | bytes 1572872 | tf_op jit(solution)/shard_map/ppermute | solution.py:154
  83.6 0.9 shard_map.77
  85.1 1.0 add_convert_fusion
  86.1 7.7 %all-to-all-start.3 = ((bf16[16,32,512]{2,1,0:T(8,128)(2,1)}), bf16[16,32,512]{2,1,0:T(8,128)(2,1)S(1)}, u32[]{:S(2)}, u32[]{:S(2)}) async-start(bf16[16,32,512]{2,1,0:T(8,128)(2,1)} %bitcast.8), calls=%async_computation.3 | async-start | bytes 1048576 | tf_op jit(solution)/shard_map/all_to_all | solution.py:16
  93.8 4.7 %collective-permute-start.3 = (bf16[256,512]{1,0:T(8,128)(2,1)}, bf16[256,512]{1,0:T(8,128)(2,1)S(1)}, u32[]{:S(2)}, u32[]{:S(2)}) collective-permute-start(bf16[256,512]{1,0:T(8,128)(2,1)} %collective-permute-done.refs_1_), channel_id=1, source_target_pairs={{0,128},{128,256},{256,384},{384,0},{1,129},{129,257},{257,385},{3... | collective-permute-start | bytes 786440 | tf_op jit(solution)/shard_map/ppermute | solution.py:35
  98.5 11.3 %all-to-all-done.3 = bf16[16,32,512]{2,1,0:T(8,128)(2,1)S(1)} async-done(((bf16[16,32,512]{2,1,0:T(8,128)(2,1)}), bf16[16,32,512]{2,1,0:T(8,128)(2,1)S(1)}, u32[]{:S(2)}, u32[]{:S(2)}) %all-to-all-start.3) | async-done | bytes 524320 | tf_op jit(solution)/shard_map/all_to_all | solution.py:16
  109.8 0.8 divide_convert_fusion
  111.3 6.1 %all-to-all-start.4 = ((bf16[8,32,512]{2,1,0:T(8,128)(2,1)}), bf16[8,32,512]{2,1,0:T(8,128)(2,1)S(1)}, u32[]{:S(2)}, u32[]{:S(2)}) async-start(bf16[8,32,512]{2,1,0:T(8,128)(2,1)} %broadcast_in_dim.16), calls=%async_computation.4 | async-start | bytes 524288 | tf_op jit(solution)/shard_map/all_to_all | solution.py:16
  117.4 6.5 %all-to-all-done.4 = bf16[8,32,512]{2,1,0:T(8,128)(2,1)S(1)} async-done(((bf16[8,32,512]{2,1,0:T(8,128)(2,1)}), bf16[8,32,512]{2,1,0:T(8,128)(2,1)S(1)}, u32[]{:S(2)}, u32[]{:S(2)}) %all-to-all-start.4) | async-done | bytes 262176 | tf_op jit(solution)/shard_map/all_to_all | solution.py:16
  123.9 1.5 %shard_map.79 = bf16[256,1024]{1,0:T(8,128)(2,1)S(1)} custom-call(s32[1]{0:T(128)} %bitcast.z_ref, bf16[256,512]{1,0:T(8,128)(2,1)S(1)} %bitcast.27, bf16[256,512]{1,0:T(8,128)(2,1)S(1)} %constant_dynamic-slice_fusion.refs_0_, bf16[256,512]{1,0:T(8,128)(2,1)} %collective-permute-done.refs_1_, bf16[256,512]{1,0:T(8,128)(2,1)S(1)} %collective-permute-done.3.refs_2_, ...), custom_call_target="tpu_custom_call" | custom-call | flops 268435456 | bytes 1835008 | tf_op jit(solution)/shard_map/pallas_call | solution.py:109
  125.4 12.8 %all_to_all.32.in_ref = bf16[8,32,1024]{2,1,0:T(8,128)(2,1)S(1)} all-to-all(bf16[8,32,1024]{2,1,0:T(8,128)(2,1)S(1)} %bitcast.26), channel_id=1, replica_groups=mesh['zh'=4,'x'=4,'y'=8,'zl'=2,'c'=2] {'x','c'}, dimensions={0} | all-to-all | bytes 1048576 | tf_op jit(solution)/shard_map/all_to_all | solution.py:16
  138.2 0.8 shard_map.80
  (16 shorter events, 2.0 us)
Async XLA Ops:
  0.6 1.2 copy-start
  0.6 8.8 %copy-start.2 = (bf16[512,512]{1,0:T(8,128)(2,1)S(1)}, bf16[512,512]{1,0:T(8,128)(2,1)}, u32[]{:S(2)}) copy-start(bf16[512,512]{1,0:T(8,128)(2,1)} %param.7) | copy-start | bytes 1572868
  4.6 21.1 %all-to-all-start = ((bf16[4,256,512]{2,1,0:T(8,128)(2,1)}), bf16[4,256,512]{2,1,0:T(8,128)(2,1)}, u32[]{:S(2)}, u32[]{:S(2)}) async-start(bf16[4,256,512]{2,1,0:T(8,128)(2,1)} %bitcast.3), calls=%async_computation | async-start | bytes 2097152 | tf_op jit(solution)/shard_map/all_to_all | solution.py:16
  9.5 21.4 %collective-permute-start.1 = (bf16[256,512]{1,0:T(8,128)(2,1)S(1)}, bf16[256,512]{1,0:T(8,128)(2,1)}, u32[]{:S(2)}, u32[]{:S(2)}) collective-permute-start(bf16[256,512]{1,0:T(8,128)(2,1)S(1)} %constant_dynamic-slice_fusion.refs_0_), channel_id=1, source_target_pairs={{0,384},{128,0},{256,128},{384,256},{1,385},{129,1},{257,129},{385... | collective-permute-start | bytes 786440 | tf_op jit(solution)/shard_map/ppermute | solution.py:35
  20.4 11.0 %collective-permute-start = (bf16[256,512]{1,0:T(8,128)(2,1)S(1)}, bf16[256,512]{1,0:T(8,128)(2,1)}, u32[]{:S(2)}, u32[]{:S(2)}) collective-permute-start(bf16[256,512]{1,0:T(8,128)(2,1)S(1)} %constant_dynamic-slice_fusion.refs_0_), channel_id=1, source_target_pairs={{0,128},{128,256},{256,384},{384,0},{1,129},{129,257},{257,385},{3... | collective-permute-start | bytes 786440 | tf_op jit(solution)/shard_map/ppermute | solution.py:35
  22.3 1.6 %copy-start.1 = (bf16[1024,1024]{1,0:T(8,128)(2,1)S(1)}, bf16[1024,1024]{1,0:T(8,128)(2,1)}, u32[]{:S(2)}) copy-start(bf16[1024,1024]{1,0:T(8,128)(2,1)} %in_ref.1) | copy-start | bytes 6291460
  67.0 18.1 %collective-permute-start.2 = (bf16[512,512]{1,0:T(8,128)(2,1)S(1)}, bf16[512,512]{1,0:T(8,128)(2,1)S(1)}, u32[]{:S(2)}, u32[]{:S(2)}) collective-permute-start(bf16[512,512]{1,0:T(8,128)(2,1)S(1)} %shard_map.78), channel_id=1, source_target_pairs={{0,1},{1,0},{2,3},{3,2},{4,5},{5,4},{6,7},{7,6},{8,9},{9,8},{10,11... | collective-permute-start | bytes 1572872 | tf_op jit(solution)/shard_map/ppermute | solution.py:154
  84.5 25.3 %copy-start.3 = (f32[32,512]{1,0:T(8,128)S(1)}, f32[32,512]{1,0:T(8,128)}, u32[]{:S(2)}) copy-start(f32[32,512]{1,0:T(8,128)} %param.8) | copy-start | bytes 196612
  84.5 25.3 %copy-start.4 = (f32[32,512]{1,0:T(8,128)S(1)}, f32[32,512]{1,0:T(8,128)}, u32[]{:S(2)}) copy-start(f32[32,512]{1,0:T(8,128)} %param.9) | copy-start | bytes 196612
  86.1 23.7 %all-to-all-start.3 = ((bf16[16,32,512]{2,1,0:T(8,128)(2,1)}), bf16[16,32,512]{2,1,0:T(8,128)(2,1)S(1)}, u32[]{:S(2)}, u32[]{:S(2)}) async-start(bf16[16,32,512]{2,1,0:T(8,128)(2,1)} %bitcast.8), calls=%async_computation.3 | async-start | bytes 1048576 | tf_op jit(solution)/shard_map/all_to_all | solution.py:16
  93.8 23.6 %collective-permute-start.3 = (bf16[256,512]{1,0:T(8,128)(2,1)}, bf16[256,512]{1,0:T(8,128)(2,1)S(1)}, u32[]{:S(2)}, u32[]{:S(2)}) collective-permute-start(bf16[256,512]{1,0:T(8,128)(2,1)} %collective-permute-done.refs_1_), channel_id=1, source_target_pairs={{0,128},{128,256},{256,384},{384,0},{1,129},{129,257},{257,385},{3... | collective-permute-start | bytes 786440 | tf_op jit(solution)/shard_map/ppermute | solution.py:35
  111.3 12.6 %all-to-all-start.4 = ((bf16[8,32,512]{2,1,0:T(8,128)(2,1)}), bf16[8,32,512]{2,1,0:T(8,128)(2,1)S(1)}, u32[]{:S(2)}, u32[]{:S(2)}) async-start(bf16[8,32,512]{2,1,0:T(8,128)(2,1)} %broadcast_in_dim.16), calls=%async_computation.4 | async-start | bytes 524288 | tf_op jit(solution)/shard_map/all_to_all | solution.py:16

commit v16 on v15

--- a/solution.py
+++ b/solution.py
@@ -145,16 +145,17 @@
     tt = turn(core, tangent)
     half = projector.shape[0] // 2
     share = lax.dynamic_slice_in_dim(projector, lax.axis_index("c") * half, half, 0)
-    one, three = back(share, "zh", 4, 1), back(share, "zh", 4, 3)
+    one = back(share, "zh", 4, 1)
     part = jnp.dot(tokens, projector, preferred_element_type=F32).astype(BF16)
     part = scattered_sum(part, "x", 4).astype(BF16)
-    z, one, three, tt, share, part = lax.optimization_barrier((z, one, three, tt, share, part))
+    z, one, tt, share, part = lax.optimization_barrier((z, one, tt, share, part))
     part = scattered_sum(part, "zh", 4).astype(BF16)
-    reduced = spread(part, ("x", "zh"), 16).reshape(-1, r)
+    part = spread(part, "zh", 4).reshape(-1, r)
+    reduced = spread(part, "x", 4).reshape(-1, r)
     others = lax.ppermute(product(tt, 1, reduced, BF16), "c", [(0, 1), (1, 0)])
     grad = (product(tt, 0, reduced, F32) + others.astype(F32)).astype(BF16)
-    one, grad = lax.optimization_barrier((one, grad))
-    two = back(one, "zh", 4, 1)
+    one, share, grad = lax.optimization_barrier((one, share, grad))
+    two, three = back(one, "zh", 4, 1), back(share, "zh", 4, 3)
     gradient = scattered_sum(grad, ("y", "zl"), 16)
 
     new_first = 0.9 * first_moment + 0.1 * gradient
@@ -164,7 +165,7 @@
     direction = (new_first / first_fix / (jnp.sqrt(new_second / second_fix) + 1e-08)).astype(BF16)
     rows = direction.shape[0]
     directions = spread(direction, ("x", "c"), 8).reshape(-1, r)
-    two, directions = lax.optimization_barrier((two, directions))
+    two, three, directions = lax.optimization_barrier((two, three, directions))
     out = update_rows(z, directions, (share, one, two, three))
     out = lay(swap(out.reshape(8, rows, -1), ("x", "c")))
     return (out, new_first, new_second)

time: 140 us -> 136 us (0.971)
  starting transfers between devices: 52.7 us -> 35.9 us
  blocking collectives: 47.4 us -> 61 us
    all_to_all x3 -> x4, blocking collectives: 47.4 us -> 61 us  [swap(): return lax.all_to_all(parts, axis, 0, 0)]
    ppermute x1, starting transfers between devices: 16.5 us -> 5.96 us  [local(): others = lax.ppermute(product(tt, 1, reduced, BF16), 'c', [(0, 1), (1, 0)])]
    ppermute x3, starting transfers between devices: 17.5 us -> 13.5 us  [back(): return lax.ppermute(block, axis, [(i, (i + k) % n) for i in range(n)])]
    all_to_all x3, starting transfers between devices: 18.7 us -> 16.5 us  [swap(): return lax.all_to_all(parts, axis, 0, 0)]
where the time goes in v16:
time: 136 us
  blocking collectives  61 us (45%)
  starting transfers between devices  35.9 us (26%)
  waiting for transfers between devices  22.7 us (17%)
  Pallas kernels  5.76 us (4%)
  local copies, waits for them, and re-layouts  3.65 us (3%)
  other arithmetic  3.07 us (2%)
  matrix products  2.74 us (2%)
    all_to_all x4, blocking collectives, swap(): return lax.all_to_all(parts, axis, 0, 0)  61 us
    all_to_all x3, waiting for transfers between devices, swap(): return lax.all_to_all(parts, axis, 0, 0)  16.6 us
    all_to_all x3, starting transfers between devices, swap(): return lax.all_to_all(parts, axis, 0, 0)  16.5 us
    ppermute x3, starting transfers between devices, back(): return lax.ppermute(block, axis, [(i, (i + k) % n) for i in range(n)])  13.5 us
    ppermute x1, starting transfers between devices, local(): others = lax.ppermute(product(tt, 1, reduced, BF16), 'c', [(0, 1), (1, 0)])  5.96 us
    ppermute x3, waiting for transfers between devices, back(): return lax.ppermute(block, axis, [(i, (i + k) % n) for i in range(n)])  5.5 us
    unnamed x10, local copies, waits for them, and re-layouts  2.82 us
    dot_general x1, matrix products, local(): part = jnp.dot(tokens, projector, preferred_element_type=F32).astype(BF16)  2.74 us
  transfers between devices with their start and end apart: 7, of which 5 were waited for; matrix products, arithmetic and copies ran while one was open for 2% of the time, Pallas kernels for 2%

profile of v16, /device:TPU:1, one launch (start us, length us, event | category | flops | bytes accessed | tf_op | source)
XLA Modules:
  0.0 135.6 jit_solution(2871633433976459917)
XLA Ops:
  0.7 1.2 copy-done
  1.9 2.7 %convolution_convert_fusion = bf16[1024,512]{1,0:T(8,128)(2,1)} fusion(bf16[1024,512]{1,0:T(8,128)(2,1)S(1)} %copy-done, bf16[512,512]{1,0:T(8,128)(2,1)} %param.7), kind=kOutput, calls=%fused_computation | convolution fusion | flops 537395200 | bytes 2621440 | tf_op jit(solution)/shard_map/dot_general | solution.py:149
  4.6 4.8 %all-to-all-start = ((bf16[4,256,512]{2,1,0:T(8,128)(2,1)}), bf16[4,256,512]{2,1,0:T(8,128)(2,1)}, u32[]{:S(2)}, u32[]{:S(2)}) async-start(bf16[4,256,512]{2,1,0:T(8,128)(2,1)} %bitcast.3), calls=%async_computation | async-start | bytes 2097152 | tf_op jit(solution)/shard_map/all_to_all | solution.py:16
  9.5 6.1 %collective-permute-start = (bf16[256,512]{1,0:T(8,128)(2,1)S(1)}, bf16[256,512]{1,0:T(8,128)(2,1)}, u32[]{:S(2)}, u32[]{:S(2)}) collective-permute-start(bf16[256,512]{1,0:T(8,128)(2,1)S(1)} %constant_dynamic-slice_fusion.refs_0_), channel_id=1, source_target_pairs={{0,128},{128,256},{256,384},{384,0},{1,129},{129,257},{257,385},{3... | collective-permute-start | bytes 786440 | tf_op jit(solution)/shard_map/ppermute | solution.py:35
  15.6 1.6 %copy-done.1 = bf16[1024,1024]{1,0:T(8,128)(2,1)S(1)} copy-done((bf16[1024,1024]{1,0:T(8,128)(2,1)S(1)}, bf16[1024,1024]{1,0:T(8,128)(2,1)}, u32[]{:S(2)}) %copy-start.1) | copy-done | bytes 2097176
  17.1 1.8 %shard_map.76 = bf16[2,16,32,1024]{3,2,1,0:T(8,128)(2,1)S(1)} custom-call(s32[1]{0:T(128)} %bitcast.1.core_ref, bf16[1024,1024]{1,0:T(8,128)(2,1)S(1)} %copy-done.1), custom_call_target="tpu_custom_call" | custom-call | bytes 4194304 | tf_op jit(solution)/shard_map/pallas_call | solution.py:51
  19.3 1.3 fusion
  20.6 5.5 %collective-permute-done.refs_1_ = bf16[256,512]{1,0:T(8,128)(2,1)} collective-permute-done((bf16[256,512]{1,0:T(8,128)(2,1)S(1)}, bf16[256,512]{1,0:T(8,128)(2,1)}, u32[]{:S(2)}, u32[]{:S(2)}) %collective-permute-start) | collective-permute-done | bytes 262176 | tf_op jit(solution)/shard_map/ppermute | solution.py:35
  26.1 19.2 %all_to_all.35 = bf16[4,64,512]{2,1,0:T(8,128)(2,1)S(1)} all-to-all(bf16[4,64,512]{2,1,0:T(8,128)(2,1)S(1)} %bitcast.29), channel_id=1, replica_groups=mesh['zh'=4,'x'=4,'y'=8,'zl'=2,'c'=2] {'zh'}, dimensions={0} | all-to-all | bytes 524288 | tf_op jit(solution)/shard_map/all_to_all | solution.py:16
  45.3 11.8 %all_to_all.36 = bf16[4,64,512]{2,1,0:T(8,128)(2,1)S(1)} all-to-all(bf16[4,64,512]{2,1,0:T(8,128)(2,1)S(1)} %broadcast_in_dim.22), channel_id=1, replica_groups=mesh['zh'=4,'x'=4,'y'=8,'zl'=2,'c'=2] {'zh'}, dimensions={0} | all-to-all | bytes 524288 | tf_op jit(solution)/shard_map/all_to_all | solution.py:16
  57.2 17.3 %all_to_all.37 = bf16[4,256,512]{2,1,0:T(8,128)(2,1)S(1)} all-to-all(bf16[4,256,512]{2,1,0:T(8,128)(2,1)S(1)} %broadcast_in_dim.24), channel_id=1, replica_groups=mesh['zh'=4,'x'=4,'y'=8,'zl'=2,'c'=2] {'x'}, dimensions={0} | all-to-all | bytes 2097152 | tf_op jit(solution)/shard_map/all_to_all | solution.py:16
  74.5 0.9 shard_map.78
  75.3 6.0 %collective-permute-start.1 = (bf16[512,512]{1,0:T(8,128)(2,1)S(1)}, bf16[512,512]{1,0:T(8,128)(2,1)S(1)}, u32[]{:S(2)}, u32[]{:S(2)}) collective-permute-start(bf16[512,512]{1,0:T(8,128)(2,1)S(1)} %shard_map.78), channel_id=1, source_target_pairs={{0,1},{1,0},{2,3},{3,2},{4,5},{5,4},{6,7},{7,6},{8,9},{9,8},{10,11... | collective-permute-start | bytes 1572872 | tf_op jit(solution)/shard_map/ppermute | solution.py:155
  81.3 0.9 shard_map.77
  82.8 1.0 add_convert_fusion
  83.8 6.9 %all-to-all-start.4 = ((bf16[16,32,512]{2,1,0:T(8,128)(2,1)}), bf16[16,32,512]{2,1,0:T(8,128)(2,1)S(1)}, u32[]{:S(2)}, u32[]{:S(2)}) async-start(bf16[16,32,512]{2,1,0:T(8,128)(2,1)} %bitcast.9), calls=%async_computation.4 | async-start | bytes 1048576 | tf_op jit(solution)/shard_map/all_to_all | solution.py:16
  90.6 1.9 %collective-permute-start.2 = (bf16[256,512]{1,0:T(8,128)(2,1)}, bf16[256,512]{1,0:T(8,128)(2,1)S(1)}, u32[]{:S(2)}, u32[]{:S(2)}) collective-permute-start(bf16[256,512]{1,0:T(8,128)(2,1)} %collective-permute-done.refs_1_), channel_id=1, source_target_pairs={{0,128},{128,256},{256,384},{384,0},{1,129},{129,257},{257,385},{3... | collective-permute-start | bytes 786440 | tf_op jit(solution)/shard_map/ppermute | solution.py:35
  92.6 5.5 %collective-permute-start.3 = (bf16[256,512]{1,0:T(8,128)(2,1)S(1)}, bf16[256,512]{1,0:T(8,128)(2,1)S(1)}, u32[]{:S(2)}, u32[]{:S(2)}) collective-permute-start(bf16[256,512]{1,0:T(8,128)(2,1)S(1)} %constant_dynamic-slice_fusion.refs_0_), channel_id=1, source_target_pairs={{0,384},{128,0},{256,128},{384,256},{1,385},{129,1},{257,129},{385... | collective-permute-start | bytes 786440 | tf_op jit(solution)/shard_map/ppermute | solution.py:35
  98.0 9.7 %all-to-all-done.4 = bf16[16,32,512]{2,1,0:T(8,128)(2,1)S(1)} async-done(((bf16[16,32,512]{2,1,0:T(8,128)(2,1)}), bf16[16,32,512]{2,1,0:T(8,128)(2,1)S(1)}, u32[]{:S(2)}, u32[]{:S(2)}) %all-to-all-start.4) | async-done | bytes 524320 | tf_op jit(solution)/shard_map/all_to_all | solution.py:16
  109.2 4.8 %all-to-all-start.5 = ((bf16[8,32,512]{2,1,0:T(8,128)(2,1)}), bf16[8,32,512]{2,1,0:T(8,128)(2,1)S(1)}, u32[]{:S(2)}, u32[]{:S(2)}) async-start(bf16[8,32,512]{2,1,0:T(8,128)(2,1)} %broadcast_in_dim.25), calls=%async_computation.5 | async-start | bytes 524288 | tf_op jit(solution)/shard_map/all_to_all | solution.py:16
  114.0 6.5 %all-to-all-done.5 = bf16[8,32,512]{2,1,0:T(8,128)(2,1)S(1)} async-done(((bf16[8,32,512]{2,1,0:T(8,128)(2,1)}), bf16[8,32,512]{2,1,0:T(8,128)(2,1)S(1)}, u32[]{:S(2)}, u32[]{:S(2)}) %all-to-all-start.5) | async-done | bytes 262176 | tf_op jit(solution)/shard_map/all_to_all | solution.py:16
  120.5 1.4 %shard_map.79 = bf16[256,1024]{1,0:T(8,128)(2,1)S(1)} custom-call(s32[1]{0:T(128)} %bitcast.z_ref, bf16[256,512]{1,0:T(8,128)(2,1)S(1)} %bitcast.28, bf16[256,512]{1,0:T(8,128)(2,1)S(1)} %constant_dynamic-slice_fusion.refs_0_, bf16[256,512]{1,0:T(8,128)(2,1)} %collective-permute-done.refs_1_, bf16[256,512]{1,0:T(8,128)(2,1)S(1)} %collective-permute-done.2.refs_2_, ...), custom_call_target="tpu_custom_call" | custom-call | flops 268435456 | bytes 1835008 | tf_op jit(solution)/shard_map/pallas_call | solution.py:109
  122.0 12.8 %all_to_all.38.in_ref = bf16[8,32,1024]{2,1,0:T(8,128)(2,1)S(1)} all-to-all(bf16[8,32,1024]{2,1,0:T(8,128)(2,1)S(1)} %bitcast.27), channel_id=1, replica_groups=mesh['zh'=4,'x'=4,'y'=8,'zl'=2,'c'=2] {'x','c'}, dimensions={0} | all-to-all | bytes 1048576 | tf_op jit(solution)/shard_map/all_to_all | solution.py:16
  134.8 0.8 shard_map.80
  (18 shorter events, 2.6 us)
Async XLA Ops:
  0.6 1.2 copy-start
  0.6 8.8 %copy-start.2 = (bf16[512,512]{1,0:T(8,128)(2,1)S(1)}, bf16[512,512]{1,0:T(8,128)(2,1)}, u32[]{:S(2)}) copy-start(bf16[512,512]{1,0:T(8,128)(2,1)} %param.7) | copy-start | bytes 1572868
  4.6 14.7 %all-to-all-start = ((bf16[4,256,512]{2,1,0:T(8,128)(2,1)}), bf16[4,256,512]{2,1,0:T(8,128)(2,1)}, u32[]{:S(2)}, u32[]{:S(2)}) async-start(bf16[4,256,512]{2,1,0:T(8,128)(2,1)} %bitcast.3), calls=%async_computation | async-start | bytes 2097152 | tf_op jit(solution)/shard_map/all_to_all | solution.py:16
  9.5 16.6 %collective-permute-start = (bf16[256,512]{1,0:T(8,128)(2,1)S(1)}, bf16[256,512]{1,0:T(8,128)(2,1)}, u32[]{:S(2)}, u32[]{:S(2)}) collective-permute-start(bf16[256,512]{1,0:T(8,128)(2,1)S(1)} %constant_dynamic-slice_fusion.refs_0_), channel_id=1, source_target_pairs={{0,128},{128,256},{256,384},{384,0},{1,129},{129,257},{257,385},{3... | collective-permute-start | bytes 786440 | tf_op jit(solution)/shard_map/ppermute | solution.py:35
  15.5 1.6 %copy-start.1 = (bf16[1024,1024]{1,0:T(8,128)(2,1)S(1)}, bf16[1024,1024]{1,0:T(8,128)(2,1)}, u32[]{:S(2)}) copy-start(bf16[1024,1024]{1,0:T(8,128)(2,1)} %in_ref.1) | copy-start | bytes 6291460
  75.3 7.5 %collective-permute-start.1 = (bf16[512,512]{1,0:T(8,128)(2,1)S(1)}, bf16[512,512]{1,0:T(8,128)(2,1)S(1)}, u32[]{:S(2)}, u32[]{:S(2)}) collective-permute-start(bf16[512,512]{1,0:T(8,128)(2,1)S(1)} %shard_map.78), channel_id=1, source_target_pairs={{0,1},{1,0},{2,3},{3,2},{4,5},{5,4},{6,7},{7,6},{8,9},{9,8},{10,11... | collective-permute-start | bytes 1572872 | tf_op jit(solution)/shard_map/ppermute | solution.py:155
  82.2 25.5 %copy-start.3 = (f32[32,512]{1,0:T(8,128)S(1)}, f32[32,512]{1,0:T(8,128)}, u32[]{:S(2)}) copy-start(f32[32,512]{1,0:T(8,128)} %param.8) | copy-start | bytes 196612
  82.2 25.5 %copy-start.4 = (f32[32,512]{1,0:T(8,128)S(1)}, f32[32,512]{1,0:T(8,128)}, u32[]{:S(2)}) copy-start(f32[32,512]{1,0:T(8,128)} %param.9) | copy-start | bytes 196612
  83.8 23.9 %all-to-all-start.4 = ((bf16[16,32,512]{2,1,0:T(8,128)(2,1)}), bf16[16,32,512]{2,1,0:T(8,128)(2,1)S(1)}, u32[]{:S(2)}, u32[]{:S(2)}) async-start(bf16[16,32,512]{2,1,0:T(8,128)(2,1)} %bitcast.9), calls=%async_computation.4 | async-start | bytes 1048576 | tf_op jit(solution)/shard_map/all_to_all | solution.py:16
  90.6 23.4 %collective-permute-start.2 = (bf16[256,512]{1,0:T(8,128)(2,1)}, bf16[256,512]{1,0:T(8,128)(2,1)S(1)}, u32[]{:S(2)}, u32[]{:S(2)}) collective-permute-start(bf16[256,512]{1,0:T(8,128)(2,1)} %collective-permute-done.refs_1_), channel_id=1, source_target_pairs={{0,128},{128,256},{256,384},{384,0},{1,129},{129,257},{257,385},{3... | collective-permute-start | bytes 786440 | tf_op jit(solution)/shard_map/ppermute | solution.py:35
  92.6 21.5 %collective-permute-start.3 = (bf16[256,512]{1,0:T(8,128)(2,1)S(1)}, bf16[256,512]{1,0:T(8,128)(2,1)S(1)}, u32[]{:S(2)}, u32[]{:S(2)}) collective-permute-start(bf16[256,512]{1,0:T(8,128)(2,1)S(1)} %constant_dynamic-slice_fusion.refs_0_), channel_id=1, source_target_pairs={{0,384},{128,0},{256,128},{384,256},{1,385},{129,1},{257,129},{385... | collective-permute-start | bytes 786440 | tf_op jit(solution)/shard_map/ppermute | solution.py:35
  109.2 11.3 %all-to-all-start.5 = ((bf16[8,32,512]{2,1,0:T(8,128)(2,1)}), bf16[8,32,512]{2,1,0:T(8,128)(2,1)S(1)}, u32[]{:S(2)}, u32[]{:S(2)}) async-start(bf16[8,32,512]{2,1,0:T(8,128)(2,1)} %broadcast_in_dim.25), calls=%async_computation.5 | async-start | bytes 524288 | tf_op jit(solution)/shard_map/all_to_all | solution.py:16

commit v17 on v16

--- a/solution.py
+++ b/solution.py
@@ -149,8 +149,8 @@
     part = jnp.dot(tokens, projector, preferred_element_type=F32).astype(BF16)
     part = scattered_sum(part, "x", 4).astype(BF16)
     z, one, tt, share, part = lax.optimization_barrier((z, one, tt, share, part))
-    part = scattered_sum(part, "zh", 4).astype(BF16)
-    part = spread(part, "zh", 4).reshape(-1, r)
+    others = [back(part, "zh", 4, k) for k in (1, 3, 2)]
+    part = sum((o.astype(F32) for o in others), part.astype(F32)).astype(BF16)
     reduced = spread(part, "x", 4).reshape(-1, r)
     others = lax.ppermute(product(tt, 1, reduced, BF16), "c", [(0, 1), (1, 0)])
     grad = (product(tt, 0, reduced, F32) + others.astype(F32)).astype(BF16)

time: 136 us -> 141 us (1.037)
  blocking collectives: 61 us -> 30.3 us
  waiting for transfers between devices: 22.7 us -> 42.1 us
  starting transfers between devices: 35.9 us -> 51.5 us
    all_to_all x4 -> x2, blocking collectives: 61 us -> 30.3 us  [swap(): return lax.all_to_all(parts, axis, 0, 0)]
    ppermute x3 -> x6, waiting for transfers between devices: 5.5 us -> 24.8 us  [back(): return lax.ppermute(block, axis, [(i, (i + k) % n) for i in range(n)])]
    ppermute x3 -> x6, starting transfers between devices: 13.5 us -> 30.8 us  [back(): return lax.ppermute(block, axis, [(i, (i + k) % n) for i in range(n)])]
    ppermute x1, starting transfers between devices: 5.96 us -> 3.84 us  [local(): others = lax.ppermute(product(tt, 1, reduced, BF16), 'c', [(0, 1), (1, 0)])]
  transfers between devices with their start and end apart: 7 -> 10, of which waited for: 5 -> 6; matrix products, arithmetic and copies ran while one was open for 2% -> 2% of each run, Pallas kernels for 2% -> 2%
where the time goes in v17:
time: 141 us; the launch traced here: 140 us
  starting transfers between devices  51.5 us (37%)
  waiting for transfers between devices  42.1 us (30%)
  blocking collectives  30.3 us (21%)
  Pallas kernels  5.76 us (4%)
  local copies, waits for them, and re-layouts  3.63 us (3%)
  other arithmetic  3.17 us (2%)
  matrix products  2.74 us (2%)
    ppermute x6, starting transfers between devices, back(): return lax.ppermute(block, axis, [(i, (i + k) % n) for i in range(n)])  30.8 us
    all_to_all x2, blocking collectives, swap(): return lax.all_to_all(parts, axis, 0, 0)  30.3 us
    ppermute x6, waiting for transfers between devices, back(): return lax.ppermute(block, axis, [(i, (i + k) % n) for i in range(n)])  24.8 us
    all_to_all x3, starting transfers between devices, swap(): return lax.all_to_all(parts, axis, 0, 0)  16.9 us
    all_to_all x3, waiting for transfers between devices, swap(): return lax.all_to_all(parts, axis, 0, 0)  16.7 us
    ppermute x1, starting transfers between devices, local(): others = lax.ppermute(product(tt, 1, reduced, BF16), 'c', [(0, 1), (1, 0)])  3.84 us
  transfers between devices with their start and end apart: 10, of which 6 were waited for; matrix products, arithmetic and copies ran while one was open for 2% of the time, Pallas kernels for 2%

profile of v17, /device:TPU:1, one launch (start us, length us, event | category | flops | bytes accessed | tf_op | source)
XLA Modules:
  0.0 140.1 jit_solution(6347025431105988854)
XLA Ops:
  0.7 1.2 copy-done
  1.9 2.7 %convolution_convert_fusion = bf16[1024,512]{1,0:T(8,128)(2,1)} fusion(bf16[1024,512]{1,0:T(8,128)(2,1)S(1)} %copy-done, bf16[512,512]{1,0:T(8,128)(2,1)} %param.7), kind=kOutput, calls=%fused_computation | convolution fusion | flops 537395200 | bytes 2621440 | tf_op jit(solution)/shard_map/dot_general | solution.py:149
  4.6 4.8 %all-to-all-start = ((bf16[4,256,512]{2,1,0:T(8,128)(2,1)}), bf16[4,256,512]{2,1,0:T(8,128)(2,1)}, u32[]{:S(2)}, u32[]{:S(2)}) async-start(bf16[4,256,512]{2,1,0:T(8,128)(2,1)} %bitcast.3), calls=%async_computation | async-start | bytes 2097152 | tf_op jit(solution)/shard_map/all_to_all | solution.py:16
  9.5 6.1 %collective-permute-start = (bf16[256,512]{1,0:T(8,128)(2,1)S(1)}, bf16[256,512]{1,0:T(8,128)(2,1)}, u32[]{:S(2)}, u32[]{:S(2)}) collective-permute-start(bf16[256,512]{1,0:T(8,128)(2,1)S(1)} %constant_dynamic-slice_fusion.refs_0_), channel_id=1, source_target_pairs={{0,128},{128,256},{256,384},{384,0},{1,129},{129,257},{257,385},{3... | collective-permute-start | bytes 786440 | tf_op jit(solution)/shard_map/ppermute | solution.py:35
  15.6 1.6 %copy-done.1 = bf16[1024,1024]{1,0:T(8,128)(2,1)S(1)} copy-done((bf16[1024,1024]{1,0:T(8,128)(2,1)S(1)}, bf16[1024,1024]{1,0:T(8,128)(2,1)}, u32[]{:S(2)}) %copy-start.1) | copy-done | bytes 2097176
  17.2 1.8 %shard_map.76 = bf16[2,16,32,1024]{3,2,1,0:T(8,128)(2,1)S(1)} custom-call(s32[1]{0:T(128)} %bitcast.1.core_ref, bf16[1024,1024]{1,0:T(8,128)(2,1)S(1)} %copy-done.1), custom_call_target="tpu_custom_call" | custom-call | bytes 4194304 | tf_op jit(solution)/shard_map/pallas_call | solution.py:51
  19.3 1.3 fusion
  20.6 5.5 %collective-permute-done.refs_1_ = bf16[256,512]{1,0:T(8,128)(2,1)} collective-permute-done((bf16[256,512]{1,0:T(8,128)(2,1)S(1)}, bf16[256,512]{1,0:T(8,128)(2,1)}, u32[]{:S(2)}, u32[]{:S(2)}) %collective-permute-start) | collective-permute-done | bytes 262176 | tf_op jit(solution)/shard_map/ppermute | solution.py:35
  26.1 11.1 %collective-permute-start.3 = (bf16[256,512]{1,0:T(8,128)(2,1)S(1)}, bf16[256,512]{1,0:T(8,128)(2,1)S(1)}, u32[]{:S(2)}, u32[]{:S(2)}) collective-permute-start(bf16[256,512]{1,0:T(8,128)(2,1)S(1)} %fusion), channel_id=1, source_target_pairs={{0,256},{128,384},{256,0},{384,128},{1,257},{129,385},{257,1},{385... | collective-permute-start | bytes 786440 | tf_op jit(solution)/shard_map/ppermute | solution.py:35
  37.3 1.9 %collective-permute-start.2 = (bf16[256,512]{1,0:T(8,128)(2,1)S(1)}, bf16[256,512]{1,0:T(8,128)(2,1)S(1)}, u32[]{:S(2)}, u32[]{:S(2)}) collective-permute-start(bf16[256,512]{1,0:T(8,128)(2,1)S(1)} %fusion), channel_id=1, source_target_pairs={{0,384},{128,0},{256,128},{384,256},{1,385},{129,1},{257,129},{385... | collective-permute-start | bytes 786440 | tf_op jit(solution)/shard_map/ppermute | solution.py:35
  39.2 4.3 %collective-permute-start.1 = (bf16[256,512]{1,0:T(8,128)(2,1)S(1)}, bf16[256,512]{1,0:T(8,128)(2,1)S(1)}, u32[]{:S(2)}, u32[]{:S(2)}) collective-permute-start(bf16[256,512]{1,0:T(8,128)(2,1)S(1)} %fusion), channel_id=1, source_target_pairs={{0,128},{128,256},{256,384},{384,0},{1,129},{129,257},{257,385},{3... | collective-permute-start | bytes 786440 | tf_op jit(solution)/shard_map/ppermute | solution.py:35
  43.5 19.3 %collective-permute-done.2 = bf16[256,512]{1,0:T(8,128)(2,1)S(1)} collective-permute-done((bf16[256,512]{1,0:T(8,128)(2,1)S(1)}, bf16[256,512]{1,0:T(8,128)(2,1)S(1)}, u32[]{:S(2)}, u32[]{:S(2)}) %collective-permute-start.2) | collective-permute-done | bytes 262176 | tf_op jit(solution)/shard_map/ppermute | solution.py:35
  63.0 17.5 %all_to_all.25 = bf16[4,256,512]{2,1,0:T(8,128)(2,1)S(1)} all-to-all(bf16[4,256,512]{2,1,0:T(8,128)(2,1)S(1)} %broadcast_in_dim.4), channel_id=1, replica_groups=mesh['zh'=4,'x'=4,'y'=8,'zl'=2,'c'=2] {'x'}, dimensions={0} | all-to-all | bytes 2097152 | tf_op jit(solution)/shard_map/all_to_all | solution.py:16
  80.5 0.9 shard_map.78
  81.4 3.8 %collective-permute-start.4 = (bf16[512,512]{1,0:T(8,128)(2,1)S(1)}, bf16[512,512]{1,0:T(8,128)(2,1)S(1)}, u32[]{:S(2)}, u32[]{:S(2)}) collective-permute-start(bf16[512,512]{1,0:T(8,128)(2,1)S(1)} %shard_map.78), channel_id=1, source_target_pairs={{0,1},{1,0},{2,3},{3,2},{4,5},{5,4},{6,7},{7,6},{8,9},{9,8},{10,11... | collective-permute-start | bytes 1572872 | tf_op jit(solution)/shard_map/ppermute | solution.py:155
  86.7 1.0 add_convert_fusion
  87.7 6.9 %all-to-all-start.2 = ((bf16[16,32,512]{2,1,0:T(8,128)(2,1)}), bf16[16,32,512]{2,1,0:T(8,128)(2,1)S(1)}, u32[]{:S(2)}, u32[]{:S(2)}) async-start(bf16[16,32,512]{2,1,0:T(8,128)(2,1)} %bitcast.6), calls=%async_computation.2 | async-start | bytes 1048576 | tf_op jit(solution)/shard_map/all_to_all | solution.py:16
  94.6 2.4 %collective-permute-start.5 = (bf16[256,512]{1,0:T(8,128)(2,1)}, bf16[256,512]{1,0:T(8,128)(2,1)S(1)}, u32[]{:S(2)}, u32[]{:S(2)}) collective-permute-start(bf16[256,512]{1,0:T(8,128)(2,1)} %collective-permute-done.refs_1_), channel_id=1, source_target_pairs={{0,128},{128,256},{256,384},{384,0},{1,129},{129,257},{257,385},{3... | collective-permute-start | bytes 786440 | tf_op jit(solution)/shard_map/ppermute | solution.py:35
  97.0 5.0 %collective-permute-start.6 = (bf16[256,512]{1,0:T(8,128)(2,1)S(1)}, bf16[256,512]{1,0:T(8,128)(2,1)S(1)}, u32[]{:S(2)}, u32[]{:S(2)}) collective-permute-start(bf16[256,512]{1,0:T(8,128)(2,1)S(1)} %constant_dynamic-slice_fusion.refs_0_), channel_id=1, source_target_pairs={{0,384},{128,0},{256,128},{384,256},{1,385},{129,1},{257,129},{385... | collective-permute-start | bytes 786440 | tf_op jit(solution)/shard_map/ppermute | solution.py:35
  102.0 9.9 %all-to-all-done.2 = bf16[16,32,512]{2,1,0:T(8,128)(2,1)S(1)} async-done(((bf16[16,32,512]{2,1,0:T(8,128)(2,1)}), bf16[16,32,512]{2,1,0:T(8,128)(2,1)S(1)}, u32[]{:S(2)}, u32[]{:S(2)}) %all-to-all-start.2) | async-done | bytes 524320 | tf_op jit(solution)/shard_map/all_to_all | solution.py:16
  113.4 5.1 %all-to-all-start.3 = ((bf16[8,32,512]{2,1,0:T(8,128)(2,1)}), bf16[8,32,512]{2,1,0:T(8,128)(2,1)S(1)}, u32[]{:S(2)}, u32[]{:S(2)}) async-start(bf16[8,32,512]{2,1,0:T(8,128)(2,1)} %broadcast_in_dim.5), calls=%async_computation.3 | async-start | bytes 524288 | tf_op jit(solution)/shard_map/all_to_all | solution.py:16
  118.5 6.5 %all-to-all-done.3 = bf16[8,32,512]{2,1,0:T(8,128)(2,1)S(1)} async-done(((bf16[8,32,512]{2,1,0:T(8,128)(2,1)}), bf16[8,32,512]{2,1,0:T(8,128)(2,1)S(1)}, u32[]{:S(2)}, u32[]{:S(2)}) %all-to-all-start.3) | async-done | bytes 262176 | tf_op jit(solution)/shard_map/all_to_all | solution.py:16
  125.0 1.4 %shard_map.79 = bf16[256,1024]{1,0:T(8,128)(2,1)S(1)} custom-call(s32[1]{0:T(128)} %bitcast.z_ref, bf16[256,512]{1,0:T(8,128)(2,1)S(1)} %bitcast.24, bf16[256,512]{1,0:T(8,128)(2,1)S(1)} %constant_dynamic-slice_fusion.refs_0_, bf16[256,512]{1,0:T(8,128)(2,1)} %collective-permute-done.refs_1_, bf16[256,512]{1,0:T(8,128)(2,1)S(1)} %collective-permute-done.5.refs_2_, ...), custom_call_target="tpu_custom_call" | custom-call | flops 268435456 | bytes 1835008 | tf_op jit(solution)/shard_map/pallas_call | solution.py:109
  126.5 12.8 %all_to_all.26.in_ref = bf16[8,32,1024]{2,1,0:T(8,128)(2,1)S(1)} all-to-all(bf16[8,32,1024]{2,1,0:T(8,128)(2,1)S(1)} %bitcast.23), channel_id=1, replica_groups=mesh['zh'=4,'x'=4,'y'=8,'zl'=2,'c'=2] {'x','c'}, dimensions={0} | all-to-all | bytes 1048576 | tf_op jit(solution)/shard_map/all_to_all | solution.py:16
  (21 shorter events, 4.4 us)
Async XLA Ops:
  0.6 1.2 copy-start
  0.6 8.8 %copy-start.2 = (bf16[512,512]{1,0:T(8,128)(2,1)S(1)}, bf16[512,512]{1,0:T(8,128)(2,1)}, u32[]{:S(2)}) copy-start(bf16[512,512]{1,0:T(8,128)(2,1)} %param.7) | copy-start | bytes 1572868
  4.6 14.7 %all-to-all-start = ((bf16[4,256,512]{2,1,0:T(8,128)(2,1)}), bf16[4,256,512]{2,1,0:T(8,128)(2,1)}, u32[]{:S(2)}, u32[]{:S(2)}) async-start(bf16[4,256,512]{2,1,0:T(8,128)(2,1)} %bitcast.3), calls=%async_computation | async-start | bytes 2097152 | tf_op jit(solution)/shard_map/all_to_all | solution.py:16
  9.5 16.7 %collective-permute-start = (bf16[256,512]{1,0:T(8,128)(2,1)S(1)}, bf16[256,512]{1,0:T(8,128)(2,1)}, u32[]{:S(2)}, u32[]{:S(2)}) collective-permute-start(bf16[256,512]{1,0:T(8,128)(2,1)S(1)} %constant_dynamic-slice_fusion.refs_0_), channel_id=1, source_target_pairs={{0,128},{128,256},{256,384},{384,0},{1,129},{129,257},{257,385},{3... | collective-permute-start | bytes 786440 | tf_op jit(solution)/shard_map/ppermute | solution.py:35
  15.6 1.6 %copy-start.1 = (bf16[1024,1024]{1,0:T(8,128)(2,1)S(1)}, bf16[1024,1024]{1,0:T(8,128)(2,1)}, u32[]{:S(2)}) copy-start(bf16[1024,1024]{1,0:T(8,128)(2,1)} %in_ref.1) | copy-start | bytes 6291460
  26.1 17.3 %collective-permute-start.3 = (bf16[256,512]{1,0:T(8,128)(2,1)S(1)}, bf16[256,512]{1,0:T(8,128)(2,1)S(1)}, u32[]{:S(2)}, u32[]{:S(2)}) collective-permute-start(bf16[256,512]{1,0:T(8,128)(2,1)S(1)} %fusion), channel_id=1, source_target_pairs={{0,256},{128,384},{256,0},{384,128},{1,257},{129,385},{257,1},{385... | collective-permute-start | bytes 786440 | tf_op jit(solution)/shard_map/ppermute | solution.py:35
  37.3 25.5 %collective-permute-start.2 = (bf16[256,512]{1,0:T(8,128)(2,1)S(1)}, bf16[256,512]{1,0:T(8,128)(2,1)S(1)}, u32[]{:S(2)}, u32[]{:S(2)}) collective-permute-start(bf16[256,512]{1,0:T(8,128)(2,1)S(1)} %fusion), channel_id=1, source_target_pairs={{0,384},{128,0},{256,128},{384,256},{1,385},{129,1},{257,129},{385... | collective-permute-start | bytes 786440 | tf_op jit(solution)/shard_map/ppermute | solution.py:35
  39.2 23.5 %collective-permute-start.1 = (bf16[256,512]{1,0:T(8,128)(2,1)S(1)}, bf16[256,512]{1,0:T(8,128)(2,1)S(1)}, u32[]{:S(2)}, u32[]{:S(2)}) collective-permute-start(bf16[256,512]{1,0:T(8,128)(2,1)S(1)} %fusion), channel_id=1, source_target_pairs={{0,128},{128,256},{256,384},{384,0},{1,129},{129,257},{257,385},{3... | collective-permute-start | bytes 786440 | tf_op jit(solution)/shard_map/ppermute | solution.py:35
  81.4 5.4 %collective-permute-start.4 = (bf16[512,512]{1,0:T(8,128)(2,1)S(1)}, bf16[512,512]{1,0:T(8,128)(2,1)S(1)}, u32[]{:S(2)}, u32[]{:S(2)}) collective-permute-start(bf16[512,512]{1,0:T(8,128)(2,1)S(1)} %shard_map.78), channel_id=1, source_target_pairs={{0,1},{1,0},{2,3},{3,2},{4,5},{5,4},{6,7},{7,6},{8,9},{9,8},{10,11... | collective-permute-start | bytes 1572872 | tf_op jit(solution)/shard_map/ppermute | solution.py:155
  86.1 25.8 %copy-start.3 = (f32[32,512]{1,0:T(8,128)S(1)}, f32[32,512]{1,0:T(8,128)}, u32[]{:S(2)}) copy-start(f32[32,512]{1,0:T(8,128)} %param.8) | copy-start | bytes 196612
  86.1 25.8 %copy-start.4 = (f32[32,512]{1,0:T(8,128)S(1)}, f32[32,512]{1,0:T(8,128)}, u32[]{:S(2)}) copy-start(f32[32,512]{1,0:T(8,128)} %param.9) | copy-start | bytes 196612
  87.7 24.2 %all-to-all-start.2 = ((bf16[16,32,512]{2,1,0:T(8,128)(2,1)}), bf16[16,32,512]{2,1,0:T(8,128)(2,1)S(1)}, u32[]{:S(2)}, u32[]{:S(2)}) async-start(bf16[16,32,512]{2,1,0:T(8,128)(2,1)} %bitcast.6), calls=%async_computation.2 | async-start | bytes 1048576 | tf_op jit(solution)/shard_map/all_to_all | solution.py:16
  94.6 23.9 %collective-permute-start.5 = (bf16[256,512]{1,0:T(8,128)(2,1)}, bf16[256,512]{1,0:T(8,128)(2,1)S(1)}, u32[]{:S(2)}, u32[]{:S(2)}) collective-permute-start(bf16[256,512]{1,0:T(8,128)(2,1)} %collective-permute-done.refs_1_), channel_id=1, source_target_pairs={{0,128},{128,256},{256,384},{384,0},{1,129},{129,257},{257,385},{3... | collective-permute-start | bytes 786440 | tf_op jit(solution)/shard_map/ppermute | solution.py:35
  97.0 21.5 %collective-permute-start.6 = (bf16[256,512]{1,0:T(8,128)(2,1)S(1)}, bf16[256,512]{1,0:T(8,128)(2,1)S(1)}, u32[]{:S(2)}, u32[]{:S(2)}) collective-permute-start(bf16[256,512]{1,0:T(8,128)(2,1)S(1)} %constant_dynamic-slice_fusion.refs_0_), channel_id=1, source_target_pairs={{0,384},{128,0},{256,128},{384,256},{1,385},{129,1},{257,129},{385... | collective-permute-start | bytes 786440 | tf_op jit(solution)/shard_map/ppermute | solution.py:35
  113.4 11.7 %all-to-all-start.3 = ((bf16[8,32,512]{2,1,0:T(8,128)(2,1)}), bf16[8,32,512]{2,1,0:T(8,128)(2,1)S(1)}, u32[]{:S(2)}, u32[]{:S(2)}) async-start(bf16[8,32,512]{2,1,0:T(8,128)(2,1)} %broadcast_in_dim.5), calls=%async_computation.3 | async-start | bytes 524288 | tf_op jit(solution)/shard_map/all_to_all | solution.py:16

commit v18 on v16

--- a/solution.py
+++ b/solution.py
@@ -145,16 +145,16 @@
     tt = turn(core, tangent)
     half = projector.shape[0] // 2
     share = lax.dynamic_slice_in_dim(projector, lax.axis_index("c") * half, half, 0)
-    one = back(share, "zh", 4, 1)
     part = jnp.dot(tokens, projector, preferred_element_type=F32).astype(BF16)
-    part = scattered_sum(part, "x", 4).astype(BF16)
-    z, one, tt, share, part = lax.optimization_barrier((z, one, tt, share, part))
-    part = scattered_sum(part, "zh", 4).astype(BF16)
+    part = scattered_sum(part, ("x", "zh"), 16).astype(BF16)
+    z, tt, share, part = lax.optimization_barrier((z, tt, share, part))
     part = spread(part, "zh", 4).reshape(-1, r)
     reduced = spread(part, "x", 4).reshape(-1, r)
+    share, reduced = lax.optimization_barrier((share, reduced))
+    one = back(share, "zh", 4, 1)
     others = lax.ppermute(product(tt, 1, reduced, BF16), "c", [(0, 1), (1, 0)])
     grad = (product(tt, 0, reduced, F32) + others.astype(F32)).astype(BF16)
-    one, share, grad = lax.optimization_barrier((one, share, grad))
+    share, grad = lax.optimization_barrier((share, grad))
     two, three = back(one, "zh", 4, 1), back(share, "zh", 4, 3)
     gradient = scattered_sum(grad, ("y", "zl"), 16)
 

time: 136 us -> 155 us (1.14)
  the two profiles are of different devices: /device:TPU:1 before, /device:TPU:16 now
where the time goes in v18:
time: 155 us; the launch traced here: 154 us
  waiting for transfers between devices  53 us (34%)
  blocking collectives  44.3 us (29%)
  starting transfers between devices  41.5 us (27%)
  Pallas kernels  4.8 us (3%)
  local copies, waits for them, and re-layouts  3.67 us (2%)
  other arithmetic  3.09 us (2%)
  matrix products  2.74 us (2%)
    all_to_all x3, blocking collectives, swap(): return lax.all_to_all(parts, axis, 0, 0)  44.3 us
    all_to_all x3, starting transfers between devices, swap(): return lax.all_to_all(parts, axis, 0, 0)  28 us
    all_to_all x3, waiting for transfers between devices, swap(): return lax.all_to_all(parts, axis, 0, 0)  27.9 us
    ppermute x3, waiting for transfers between devices, back(): return lax.ppermute(block, axis, [(i, (i + k) % n) for i in range(n)])  24.2 us
    ppermute x3, starting transfers between devices, back(): return lax.ppermute(block, axis, [(i, (i + k) % n) for i in range(n)])  11.6 us
  transfers between devices with their start and end apart: 7, of which 5 were waited for; matrix products, arithmetic and copies ran while one was open for 1% of the time, Pallas kernels for 2%

profile of v18, /device:TPU:16, one launch (start us, length us, event | category | flops | bytes accessed | tf_op | source)
XLA Modules:
  0.0 153.9 jit_solution(11271637973447178279)
XLA Ops:
  0.6 1.2 copy-done
  1.9 2.7 %convolution_convert_fusion = bf16[1024,512]{1,0:T(8,128)(2,1)} fusion(bf16[1024,512]{1,0:T(8,128)(2,1)S(1)} %copy-done, bf16[512,512]{1,0:T(8,128)(2,1)} %param.7), kind=kOutput, calls=%fused_computation | convolution fusion | flops 537395200 | bytes 2621440 | tf_op jit(solution)/shard_map/dot_general | solution.py:148
  4.6 12.9 %all-to-all-start = ((bf16[16,64,512]{2,1,0:T(8,128)(2,1)}), bf16[16,64,512]{2,1,0:T(8,128)(2,1)}, u32[]{:S(2)}, u32[]{:S(2)}) async-start(bf16[16,64,512]{2,1,0:T(8,128)(2,1)} %bitcast.3), calls=%async_computation | async-start | bytes 2097152 | tf_op jit(solution)/shard_map/all_to_all | solution.py:16
  17.5 1.6 %copy-done.1 = bf16[1024,1024]{1,0:T(8,128)(2,1)S(1)} copy-done((bf16[1024,1024]{1,0:T(8,128)(2,1)S(1)}, bf16[1024,1024]{1,0:T(8,128)(2,1)}, u32[]{:S(2)}) %copy-start.1) | copy-done | bytes 2097176
  19.1 1.8 %shard_map.76 = bf16[2,16,32,1024]{3,2,1,0:T(8,128)(2,1)S(1)} custom-call(s32[1]{0:T(128)} %bitcast.1.core_ref, bf16[1024,1024]{1,0:T(8,128)(2,1)S(1)} %copy-done.1), custom_call_target="tpu_custom_call" | custom-call | bytes 4194304 | tf_op jit(solution)/shard_map/pallas_call | solution.py:51
  21.0 20.9 %all-to-all-done = bf16[16,64,512]{2,1,0:T(8,128)(2,1)} async-done(((bf16[16,64,512]{2,1,0:T(8,128)(2,1)}), bf16[16,64,512]{2,1,0:T(8,128)(2,1)}, u32[]{:S(2)}, u32[]{:S(2)}) %all-to-all-start) | async-done | bytes 1048608 | tf_op jit(solution)/shard_map/all_to_all | solution.py:16
  41.8 1.4 fusion
  43.2 16.7 %all_to_all.30 = bf16[4,64,512]{2,1,0:T(8,128)(2,1)S(1)} all-to-all(bf16[4,64,512]{2,1,0:T(8,128)(2,1)S(1)} %broadcast_in_dim.8), channel_id=1, replica_groups=mesh['zh'=4,'x'=4,'y'=8,'zl'=2,'c'=2] {'zh'}, dimensions={0} | all-to-all | bytes 524288 | tf_op jit(solution)/shard_map/all_to_all | solution.py:16
  60.0 14.8 %all_to_all.31 = bf16[4,256,512]{2,1,0:T(8,128)(2,1)S(1)} all-to-all(bf16[4,256,512]{2,1,0:T(8,128)(2,1)S(1)} %broadcast_in_dim.10), channel_id=1, replica_groups=mesh['zh'=4,'x'=4,'y'=8,'zl'=2,'c'=2] {'x'}, dimensions={0} | all-to-all | bytes 2097152 | tf_op jit(solution)/shard_map/all_to_all | solution.py:16
  74.8 0.9 shard_map.78
  75.7 1.9 %collective-permute-start.2 = (bf16[512,512]{1,0:T(8,128)(2,1)S(1)}, bf16[512,512]{1,0:T(8,128)(2,1)S(1)}, u32[]{:S(2)}, u32[]{:S(2)}) collective-permute-start(bf16[512,512]{1,0:T(8,128)(2,1)S(1)} %shard_map.78), channel_id=1, source_target_pairs={{0,1},{1,0},{2,3},{3,2},{4,5},{5,4},{6,7},{7,6},{8,9},{9,8},{10,11... | collective-permute-start | bytes 1572872 | tf_op jit(solution)/shard_map/ppermute | solution.py:155
  77.6 0.9 shard_map.77
  78.5 1.0 collective-permute-done.2
  79.5 1.0 add_convert_fusion
  80.4 11.6 %all-to-all-start.3 = ((bf16[16,32,512]{2,1,0:T(8,128)(2,1)}), bf16[16,32,512]{2,1,0:T(8,128)(2,1)S(1)}, u32[]{:S(2)}, u32[]{:S(2)}) async-start(bf16[16,32,512]{2,1,0:T(8,128)(2,1)} %bitcast.8), calls=%async_computation.3 | async-start | bytes 1048576 | tf_op jit(solution)/shard_map/all_to_all | solution.py:16
  92.0 3.7 %collective-permute-start = (bf16[256,512]{1,0:T(8,128)(2,1)S(1)}, bf16[256,512]{1,0:T(8,128)(2,1)S(1)}, u32[]{:S(2)}, u32[]{:S(2)}) collective-permute-start(bf16[256,512]{1,0:T(8,128)(2,1)S(1)} %constant_dynamic-slice_fusion.refs_0_), channel_id=1, source_target_pairs={{0,128},{128,256},{256,384},{384,0},{1,129},{129,257},{257,385},{3... | collective-permute-start | bytes 786440 | tf_op jit(solution)/shard_map/ppermute | solution.py:35
  95.7 23.7 %collective-permute-done.refs_1_ = bf16[256,512]{1,0:T(8,128)(2,1)S(1)} collective-permute-done((bf16[256,512]{1,0:T(8,128)(2,1)S(1)}, bf16[256,512]{1,0:T(8,128)(2,1)S(1)}, u32[]{:S(2)}, u32[]{:S(2)}) %collective-permute-start) | collective-permute-done | bytes 262176 | tf_op jit(solution)/shard_map/ppermute | solution.py:35
  119.5 1.9 %collective-permute-start.1 = (bf16[256,512]{1,0:T(8,128)(2,1)S(1)}, bf16[256,512]{1,0:T(8,128)(2,1)S(1)}, u32[]{:S(2)}, u32[]{:S(2)}) collective-permute-start(bf16[256,512]{1,0:T(8,128)(2,1)S(1)} %collective-permute-done.refs_1_), channel_id=1, source_target_pairs={{0,128},{128,256},{256,384},{384,0},{1,129},{129,257},{257,385},{3... | collective-permute-start | bytes 786440 | tf_op jit(solution)/shard_map/ppermute | solution.py:35
  121.4 6.0 %collective-permute-start.3 = (bf16[256,512]{1,0:T(8,128)(2,1)S(1)}, bf16[256,512]{1,0:T(8,128)(2,1)S(1)}, u32[]{:S(2)}, u32[]{:S(2)}) collective-permute-start(bf16[256,512]{1,0:T(8,128)(2,1)S(1)} %constant_dynamic-slice_fusion.refs_0_), channel_id=1, source_target_pairs={{0,384},{128,0},{256,128},{384,256},{1,385},{129,1},{257,129},{385... | collective-permute-start | bytes 786440 | tf_op jit(solution)/shard_map/ppermute | solution.py:35
  127.5 0.8 divide_convert_fusion
  128.9 3.4 %all-to-all-start.4 = ((bf16[8,32,512]{2,1,0:T(8,128)(2,1)}), bf16[8,32,512]{2,1,0:T(8,128)(2,1)S(1)}, u32[]{:S(2)}, u32[]{:S(2)}) async-start(bf16[8,32,512]{2,1,0:T(8,128)(2,1)} %broadcast_in_dim.22), calls=%async_computation.4 | async-start | bytes 524288 | tf_op jit(solution)/shard_map/all_to_all | solution.py:16
  132.8 7.0 %all-to-all-done.4 = bf16[8,32,512]{2,1,0:T(8,128)(2,1)S(1)} async-done(((bf16[8,32,512]{2,1,0:T(8,128)(2,1)}), bf16[8,32,512]{2,1,0:T(8,128)(2,1)S(1)}, u32[]{:S(2)}, u32[]{:S(2)}) %all-to-all-start.4) | async-done | bytes 262176 | tf_op jit(solution)/shard_map/all_to_all | solution.py:16
  140.3 12.8 %all_to_all.32.in_ref = bf16[8,32,1024]{2,1,0:T(8,128)(2,1)S(1)} all-to-all(bf16[8,32,1024]{2,1,0:T(8,128)(2,1)S(1)} %bitcast.29), channel_id=1, replica_groups=mesh['zh'=4,'x'=4,'y'=8,'zl'=2,'c'=2] {'x','c'}, dimensions={0} | all-to-all | bytes 1048576 | tf_op jit(solution)/shard_map/all_to_all | solution.py:16
  153.1 0.8 shard_map.80
  (16 shorter events, 1.8 us)
Async XLA Ops:
  0.6 1.2 copy-start
  4.6 37.2 %all-to-all-start = ((bf16[16,64,512]{2,1,0:T(8,128)(2,1)}), bf16[16,64,512]{2,1,0:T(8,128)(2,1)}, u32[]{:S(2)}, u32[]{:S(2)}) async-start(bf16[16,64,512]{2,1,0:T(8,128)(2,1)} %bitcast.3), calls=%async_computation | async-start | bytes 2097152 | tf_op jit(solution)/shard_map/all_to_all | solution.py:16
  17.5 1.6 %copy-start.1 = (bf16[1024,1024]{1,0:T(8,128)(2,1)S(1)}, bf16[1024,1024]{1,0:T(8,128)(2,1)}, u32[]{:S(2)}) copy-start(bf16[1024,1024]{1,0:T(8,128)(2,1)} %in_ref.1) | copy-start | bytes 6291460
  19.1 1.8 %copy-start.2 = (bf16[512,512]{1,0:T(8,128)(2,1)S(1)}, bf16[512,512]{1,0:T(8,128)(2,1)}, u32[]{:S(2)}) copy-start(bf16[512,512]{1,0:T(8,128)(2,1)} %param.7) | copy-start | bytes 1572868
  75.7 3.8 %collective-permute-start.2 = (bf16[512,512]{1,0:T(8,128)(2,1)S(1)}, bf16[512,512]{1,0:T(8,128)(2,1)S(1)}, u32[]{:S(2)}, u32[]{:S(2)}) collective-permute-start(bf16[512,512]{1,0:T(8,128)(2,1)S(1)} %shard_map.78), channel_id=1, source_target_pairs={{0,1},{1,0},{2,3},{3,2},{4,5},{5,4},{6,7},{7,6},{8,9},{9,8},{10,11... | collective-permute-start | bytes 1572872 | tf_op jit(solution)/shard_map/ppermute | solution.py:155
  78.5 49.0 %copy-start.3 = (f32[32,512]{1,0:T(8,128)S(1)}, f32[32,512]{1,0:T(8,128)}, u32[]{:S(2)}) copy-start(f32[32,512]{1,0:T(8,128)} %param.8) | copy-start | bytes 196612
  78.5 49.0 %copy-start.4 = (f32[32,512]{1,0:T(8,128)S(1)}, f32[32,512]{1,0:T(8,128)}, u32[]{:S(2)}) copy-start(f32[32,512]{1,0:T(8,128)} %param.9) | copy-start | bytes 196612
  80.4 47.0 %all-to-all-start.3 = ((bf16[16,32,512]{2,1,0:T(8,128)(2,1)}), bf16[16,32,512]{2,1,0:T(8,128)(2,1)S(1)}, u32[]{:S(2)}, u32[]{:S(2)}) async-start(bf16[16,32,512]{2,1,0:T(8,128)(2,1)} %bitcast.8), calls=%async_computation.3 | async-start | bytes 1048576 | tf_op jit(solution)/shard_map/all_to_all | solution.py:16
  92.0 27.4 %collective-permute-start = (bf16[256,512]{1,0:T(8,128)(2,1)S(1)}, bf16[256,512]{1,0:T(8,128)(2,1)S(1)}, u32[]{:S(2)}, u32[]{:S(2)}) collective-permute-start(bf16[256,512]{1,0:T(8,128)(2,1)S(1)} %constant_dynamic-slice_fusion.refs_0_), channel_id=1, source_target_pairs={{0,128},{128,256},{256,384},{384,0},{1,129},{129,257},{257,385},{3... | collective-permute-start | bytes 786440 | tf_op jit(solution)/shard_map/ppermute | solution.py:35
  119.5 12.9 %collective-permute-start.1 = (bf16[256,512]{1,0:T(8,128)(2,1)S(1)}, bf16[256,512]{1,0:T(8,128)(2,1)S(1)}, u32[]{:S(2)}, u32[]{:S(2)}) collective-permute-start(bf16[256,512]{1,0:T(8,128)(2,1)S(1)} %collective-permute-done.refs_1_), channel_id=1, source_target_pairs={{0,128},{128,256},{256,384},{384,0},{1,129},{129,257},{257,385},{3... | collective-permute-start | bytes 786440 | tf_op jit(solution)/shard_map/ppermute | solution.py:35
  121.4 11.4 %collective-permute-start.3 = (bf16[256,512]{1,0:T(8,128)(2,1)S(1)}, bf16[256,512]{1,0:T(8,128)(2,1)S(1)}, u32[]{:S(2)}, u32[]{:S(2)}) collective-permute-start(bf16[256,512]{1,0:T(8,128)(2,1)S(1)} %constant_dynamic-slice_fusion.refs_0_), channel_id=1, source_target_pairs={{0,384},{128,0},{256,128},{384,256},{1,385},{129,1},{257,129},{385... | collective-permute-start | bytes 786440 | tf_op jit(solution)/shard_map/ppermute | solution.py:35
  128.9 10.9 %all-to-all-start.4 = ((bf16[8,32,512]{2,1,0:T(8,128)(2,1)}), bf16[8,32,512]{2,1,0:T(8,128)(2,1)S(1)}, u32[]{:S(2)}, u32[]{:S(2)}) async-start(bf16[8,32,512]{2,1,0:T(8,128)(2,1)} %broadcast_in_dim.22), calls=%async_computation.4 | async-start | bytes 524288 | tf_op jit(solution)/shard_map/all_to_all | solution.py:16

commit v19 on v16

--- a/solution.py
+++ b/solution.py
@@ -157,6 +157,7 @@
     one, share, grad = lax.optimization_barrier((one, share, grad))
     two, three = back(one, "zh", 4, 1), back(share, "zh", 4, 3)
     gradient = scattered_sum(grad, ("y", "zl"), 16)
+    two, three, gradient = lax.optimization_barrier((two, three, gradient))
 
     new_first = 0.9 * first_moment + 0.1 * gradient
     new_second = 0.999 * second_moment + 0.001 * gradient * gradient
@@ -165,7 +166,6 @@
     direction = (new_first / first_fix / (jnp.sqrt(new_second / second_fix) + 1e-08)).astype(BF16)
     rows = direction.shape[0]
     directions = spread(direction, ("x", "c"), 8).reshape(-1, r)
-    two, three, directions = lax.optimization_barrier((two, three, directions))
     out = update_rows(z, directions, (share, one, two, three))
     out = lay(swap(out.reshape(8, rows, -1), ("x", "c")))
     return (out, new_first, new_second)

time: 136 us -> 139 us (1.022)
  blocking collectives: 61 us -> 71.3 us
  starting transfers between devices: 35.9 us -> 31.1 us
  waiting for transfers between devices: 22.7 us -> 20.7 us
    all_to_all x4 -> x5, blocking collectives: 61 us -> 71.3 us  [swap(): return lax.all_to_all(parts, axis, 0, 0)]
    all_to_all x3 -> x2, waiting for transfers between devices: 16.6 us -> 10 us  [swap(): return lax.all_to_all(parts, axis, 0, 0)]
    all_to_all x3 -> x2, starting transfers between devices: 16.5 us -> 11.7 us  [swap(): return lax.all_to_all(parts, axis, 0, 0)]
    ppermute x3, waiting for transfers between devices: 5.5 us -> 10.1 us  [back(): return lax.ppermute(block, axis, [(i, (i + k) % n) for i in range(n)])]
  transfers between devices with their start and end apart: 7 -> 6, of which waited for: 5 -> 5; matrix products, arithmetic and copies ran while one was open for 2% -> 1% of each run, Pallas kernels for 2% -> 2%
where the time goes in v19:
time: 139 us; the launch traced here: 138 us
  blocking collectives  71.3 us (51%)
  starting transfers between devices  31.1 us (22%)
  waiting for transfers between devices  20.7 us (15%)
  Pallas kernels  5.76 us (4%)
  other arithmetic  3.07 us (2%)
  local copies, waits for them, and re-layouts  2.95 us (2%)
  matrix products  2.75 us (2%)
    all_to_all x5, blocking collectives, swap(): return lax.all_to_all(parts, axis, 0, 0)  71.3 us
    ppermute x3, starting transfers between devices, back(): return lax.ppermute(block, axis, [(i, (i + k) % n) for i in range(n)])  13.5 us
    all_to_all x2, starting transfers between devices, swap(): return lax.all_to_all(parts, axis, 0, 0)  11.7 us
    ppermute x3, waiting for transfers between devices, back(): return lax.ppermute(block, axis, [(i, (i + k) % n) for i in range(n)])  10.1 us
    all_to_all x2, waiting for transfers between devices, swap(): return lax.all_to_all(parts, axis, 0, 0)  10 us
    ppermute x1, starting transfers between devices, local(): others = lax.ppermute(product(tt, 1, reduced, BF16), 'c', [(0, 1), (1, 0)])  5.96 us
    unnamed x10, local copies, waits for them, and re-layouts  2.82 us
  transfers between devices with their start and end apart: 6, of which 5 were waited for; matrix products, arithmetic and copies ran while one was open for 1% of the time, Pallas kernels for 2%

profile of v19, /device:TPU:1, one launch (start us, length us, event | category | flops | bytes accessed | tf_op | source)
XLA Modules:
  0.0 138.5 jit_solution(1808864652216757632)
XLA Ops:
  0.7 1.2 copy-done
  1.9 2.7 %convolution_convert_fusion = bf16[1024,512]{1,0:T(8,128)(2,1)} fusion(bf16[1024,512]{1,0:T(8,128)(2,1)S(1)} %copy-done, bf16[512,512]{1,0:T(8,128)(2,1)} %param.7), kind=kOutput, calls=%fused_computation | convolution fusion | flops 537395200 | bytes 2621440 | tf_op jit(solution)/shard_map/dot_general | solution.py:149
  4.6 4.8 %all-to-all-start = ((bf16[4,256,512]{2,1,0:T(8,128)(2,1)}), bf16[4,256,512]{2,1,0:T(8,128)(2,1)}, u32[]{:S(2)}, u32[]{:S(2)}) async-start(bf16[4,256,512]{2,1,0:T(8,128)(2,1)} %bitcast.3), calls=%async_computation | async-start | bytes 2097152 | tf_op jit(solution)/shard_map/all_to_all | solution.py:16
  9.5 6.1 %collective-permute-start = (bf16[256,512]{1,0:T(8,128)(2,1)S(1)}, bf16[256,512]{1,0:T(8,128)(2,1)}, u32[]{:S(2)}, u32[]{:S(2)}) collective-permute-start(bf16[256,512]{1,0:T(8,128)(2,1)S(1)} %constant_dynamic-slice_fusion.refs_0_), channel_id=1, source_target_pairs={{0,128},{128,256},{256,384},{384,0},{1,129},{129,257},{257,385},{3... | collective-permute-start | bytes 786440 | tf_op jit(solution)/shard_map/ppermute | solution.py:35
  15.6 1.6 %copy-done.1 = bf16[1024,1024]{1,0:T(8,128)(2,1)S(1)} copy-done((bf16[1024,1024]{1,0:T(8,128)(2,1)S(1)}, bf16[1024,1024]{1,0:T(8,128)(2,1)}, u32[]{:S(2)}) %copy-start.1) | copy-done | bytes 2097176
  17.1 1.8 %shard_map.76 = bf16[2,16,32,1024]{3,2,1,0:T(8,128)(2,1)S(1)} custom-call(s32[1]{0:T(128)} %bitcast.1.core_ref, bf16[1024,1024]{1,0:T(8,128)(2,1)S(1)} %copy-done.1), custom_call_target="tpu_custom_call" | custom-call | bytes 4194304 | tf_op jit(solution)/shard_map/pallas_call | solution.py:51
  19.3 1.3 fusion
  20.6 5.5 %collective-permute-done.refs_1_ = bf16[256,512]{1,0:T(8,128)(2,1)} collective-permute-done((bf16[256,512]{1,0:T(8,128)(2,1)S(1)}, bf16[256,512]{1,0:T(8,128)(2,1)}, u32[]{:S(2)}, u32[]{:S(2)}) %collective-permute-start) | collective-permute-done | bytes 262176 | tf_op jit(solution)/shard_map/ppermute | solution.py:35
  26.1 19.1 %all_to_all.35 = bf16[4,64,512]{2,1,0:T(8,128)(2,1)S(1)} all-to-all(bf16[4,64,512]{2,1,0:T(8,128)(2,1)S(1)} %bitcast.29), channel_id=1, replica_groups=mesh['zh'=4,'x'=4,'y'=8,'zl'=2,'c'=2] {'zh'}, dimensions={0} | all-to-all | bytes 524288 | tf_op jit(solution)/shard_map/all_to_all | solution.py:16
  45.3 11.8 %all_to_all.36 = bf16[4,64,512]{2,1,0:T(8,128)(2,1)S(1)} all-to-all(bf16[4,64,512]{2,1,0:T(8,128)(2,1)S(1)} %broadcast_in_dim.22), channel_id=1, replica_groups=mesh['zh'=4,'x'=4,'y'=8,'zl'=2,'c'=2] {'zh'}, dimensions={0} | all-to-all | bytes 524288 | tf_op jit(solution)/shard_map/all_to_all | solution.py:16
  57.2 17.3 %all_to_all.37 = bf16[4,256,512]{2,1,0:T(8,128)(2,1)S(1)} all-to-all(bf16[4,256,512]{2,1,0:T(8,128)(2,1)S(1)} %broadcast_in_dim.24), channel_id=1, replica_groups=mesh['zh'=4,'x'=4,'y'=8,'zl'=2,'c'=2] {'x'}, dimensions={0} | all-to-all | bytes 2097152 | tf_op jit(solution)/shard_map/all_to_all | solution.py:16
  74.5 0.9 shard_map.78
  75.3 6.0 %collective-permute-start.1 = (bf16[512,512]{1,0:T(8,128)(2,1)S(1)}, bf16[512,512]{1,0:T(8,128)(2,1)S(1)}, u32[]{:S(2)}, u32[]{:S(2)}) collective-permute-start(bf16[512,512]{1,0:T(8,128)(2,1)S(1)} %shard_map.78), channel_id=1, source_target_pairs={{0,1},{1,0},{2,3},{3,2},{4,5},{5,4},{6,7},{7,6},{8,9},{9,8},{10,11... | collective-permute-start | bytes 1572872 | tf_op jit(solution)/shard_map/ppermute | solution.py:155
  81.3 0.9 shard_map.77
  82.8 1.0 add_convert_fusion
  83.8 6.8 %all-to-all-start.4 = ((bf16[16,32,512]{2,1,0:T(8,128)(2,1)}), bf16[16,32,512]{2,1,0:T(8,128)(2,1)S(1)}, u32[]{:S(2)}, u32[]{:S(2)}) async-start(bf16[16,32,512]{2,1,0:T(8,128)(2,1)} %bitcast.9), calls=%async_computation.4 | async-start | bytes 1048576 | tf_op jit(solution)/shard_map/all_to_all | solution.py:16
  90.6 1.9 %collective-permute-start.2 = (bf16[256,512]{1,0:T(8,128)(2,1)}, bf16[256,512]{1,0:T(8,128)(2,1)S(1)}, u32[]{:S(2)}, u32[]{:S(2)}) collective-permute-start(bf16[256,512]{1,0:T(8,128)(2,1)} %collective-permute-done.refs_1_), channel_id=1, source_target_pairs={{0,128},{128,256},{256,384},{384,0},{1,129},{129,257},{257,385},{3... | collective-permute-start | bytes 786440 | tf_op jit(solution)/shard_map/ppermute | solution.py:35
  92.6 5.5 %collective-permute-start.3 = (bf16[256,512]{1,0:T(8,128)(2,1)S(1)}, bf16[256,512]{1,0:T(8,128)(2,1)S(1)}, u32[]{:S(2)}, u32[]{:S(2)}) collective-permute-start(bf16[256,512]{1,0:T(8,128)(2,1)S(1)} %constant_dynamic-slice_fusion.refs_0_), channel_id=1, source_target_pairs={{0,384},{128,0},{256,128},{384,256},{1,385},{129,1},{257,129},{385... | collective-permute-start | bytes 786440 | tf_op jit(solution)/shard_map/ppermute | solution.py:35
  98.0 9.7 %all-to-all-done.4 = bf16[16,32,512]{2,1,0:T(8,128)(2,1)S(1)} async-done(((bf16[16,32,512]{2,1,0:T(8,128)(2,1)}), bf16[16,32,512]{2,1,0:T(8,128)(2,1)S(1)}, u32[]{:S(2)}, u32[]{:S(2)}) %all-to-all-start.4) | async-done | bytes 524320 | tf_op jit(solution)/shard_map/all_to_all | solution.py:16
  107.8 4.6 %collective-permute-done.2.refs_2_ = bf16[256,512]{1,0:T(8,128)(2,1)S(1)} collective-permute-done((bf16[256,512]{1,0:T(8,128)(2,1)}, bf16[256,512]{1,0:T(8,128)(2,1)S(1)}, u32[]{:S(2)}, u32[]{:S(2)}) %collective-permute-start.2) | collective-permute-done | bytes 262176 | tf_op jit(solution)/shard_map/ppermute | solution.py:35
  113.1 10.3 %all_to_all.38 = bf16[8,32,512]{2,1,0:T(8,128)(2,1)S(1)} all-to-all(bf16[8,32,512]{2,1,0:T(8,128)(2,1)S(1)} %broadcast_in_dim.25), channel_id=1, replica_groups=mesh['zh'=4,'x'=4,'y'=8,'zl'=2,'c'=2] {'x','c'}, dimensions={0} | all-to-all | bytes 524288 | tf_op jit(solution)/shard_map/all_to_all | solution.py:16
  123.4 1.4 %shard_map.79 = bf16[256,1024]{1,0:T(8,128)(2,1)S(1)} custom-call(s32[1]{0:T(128)} %bitcast.z_ref, bf16[256,512]{1,0:T(8,128)(2,1)S(1)} %bitcast.28, bf16[256,512]{1,0:T(8,128)(2,1)S(1)} %constant_dynamic-slice_fusion.refs_0_, bf16[256,512]{1,0:T(8,128)(2,1)} %collective-permute-done.refs_1_, bf16[256,512]{1,0:T(8,128)(2,1)S(1)} %collective-permute-done.2.refs_2_, ...), custom_call_target="tpu_custom_call" | custom-call | flops 268435456 | bytes 1835008 | tf_op jit(solution)/shard_map/pallas_call | solution.py:109
  124.9 12.8 %all_to_all.39.in_ref = bf16[8,32,1024]{2,1,0:T(8,128)(2,1)S(1)} all-to-all(bf16[8,32,1024]{2,1,0:T(8,128)(2,1)S(1)} %bitcast.27), channel_id=1, replica_groups=mesh['zh'=4,'x'=4,'y'=8,'zl'=2,'c'=2] {'x','c'}, dimensions={0} | all-to-all | bytes 1048576 | tf_op jit(solution)/shard_map/all_to_all | solution.py:16
  137.7 0.8 shard_map.80
  (18 shorter events, 1.9 us)
Async XLA Ops:
  0.6 1.2 copy-start
  0.6 8.8 %copy-start.2 = (bf16[512,512]{1,0:T(8,128)(2,1)S(1)}, bf16[512,512]{1,0:T(8,128)(2,1)}, u32[]{:S(2)}) copy-start(bf16[512,512]{1,0:T(8,128)(2,1)} %param.7) | copy-start | bytes 1572868
  4.6 14.7 %all-to-all-start = ((bf16[4,256,512]{2,1,0:T(8,128)(2,1)}), bf16[4,256,512]{2,1,0:T(8,128)(2,1)}, u32[]{:S(2)}, u32[]{:S(2)}) async-start(bf16[4,256,512]{2,1,0:T(8,128)(2,1)} %bitcast.3), calls=%async_computation | async-start | bytes 2097152 | tf_op jit(solution)/shard_map/all_to_all | solution.py:16
  9.5 16.6 %collective-permute-start = (bf16[256,512]{1,0:T(8,128)(2,1)S(1)}, bf16[256,512]{1,0:T(8,128)(2,1)}, u32[]{:S(2)}, u32[]{:S(2)}) collective-permute-start(bf16[256,512]{1,0:T(8,128)(2,1)S(1)} %constant_dynamic-slice_fusion.refs_0_), channel_id=1, source_target_pairs={{0,128},{128,256},{256,384},{384,0},{1,129},{129,257},{257,385},{3... | collective-permute-start | bytes 786440 | tf_op jit(solution)/shard_map/ppermute | solution.py:35
  15.6 1.6 %copy-start.1 = (bf16[1024,1024]{1,0:T(8,128)(2,1)S(1)}, bf16[1024,1024]{1,0:T(8,128)(2,1)}, u32[]{:S(2)}) copy-start(bf16[1024,1024]{1,0:T(8,128)(2,1)} %in_ref.1) | copy-start | bytes 6291460
  75.3 7.5 %collective-permute-start.1 = (bf16[512,512]{1,0:T(8,128)(2,1)S(1)}, bf16[512,512]{1,0:T(8,128)(2,1)S(1)}, u32[]{:S(2)}, u32[]{:S(2)}) collective-permute-start(bf16[512,512]{1,0:T(8,128)(2,1)S(1)} %shard_map.78), channel_id=1, source_target_pairs={{0,1},{1,0},{2,3},{3,2},{4,5},{5,4},{6,7},{7,6},{8,9},{9,8},{10,11... | collective-permute-start | bytes 1572872 | tf_op jit(solution)/shard_map/ppermute | solution.py:155
  82.2 30.2 %copy-start.3 = (f32[32,512]{1,0:T(8,128)S(1)}, f32[32,512]{1,0:T(8,128)}, u32[]{:S(2)}) copy-start(f32[32,512]{1,0:T(8,128)} %param.8) | copy-start | bytes 196612
  82.2 30.2 %copy-start.4 = (f32[32,512]{1,0:T(8,128)S(1)}, f32[32,512]{1,0:T(8,128)}, u32[]{:S(2)}) copy-start(f32[32,512]{1,0:T(8,128)} %param.9) | copy-start | bytes 196612
  83.8 23.9 %all-to-all-start.4 = ((bf16[16,32,512]{2,1,0:T(8,128)(2,1)}), bf16[16,32,512]{2,1,0:T(8,128)(2,1)S(1)}, u32[]{:S(2)}, u32[]{:S(2)}) async-start(bf16[16,32,512]{2,1,0:T(8,128)(2,1)} %bitcast.9), calls=%async_computation.4 | async-start | bytes 1048576 | tf_op jit(solution)/shard_map/all_to_all | solution.py:16
  90.6 21.7 %collective-permute-start.2 = (bf16[256,512]{1,0:T(8,128)(2,1)}, bf16[256,512]{1,0:T(8,128)(2,1)S(1)}, u32[]{:S(2)}, u32[]{:S(2)}) collective-permute-start(bf16[256,512]{1,0:T(8,128)(2,1)} %collective-permute-done.refs_1_), channel_id=1, source_target_pairs={{0,128},{128,256},{256,384},{384,0},{1,129},{129,257},{257,385},{3... | collective-permute-start | bytes 786440 | tf_op jit(solution)/shard_map/ppermute | solution.py:35
  92.6 19.8 %collective-permute-start.3 = (bf16[256,512]{1,0:T(8,128)(2,1)S(1)}, bf16[256,512]{1,0:T(8,128)(2,1)S(1)}, u32[]{:S(2)}, u32[]{:S(2)}) collective-permute-start(bf16[256,512]{1,0:T(8,128)(2,1)S(1)} %constant_dynamic-slice_fusion.refs_0_), channel_id=1, source_target_pairs={{0,384},{128,0},{256,128},{384,256},{1,385},{129,1},{257,129},{385... | collective-permute-start | bytes 786440 | tf_op jit(solution)/shard_map/ppermute | solution.py:35
